TPU v7x, 512 devices: a whole 4x4x16 slice. The times are simulated.
512 devices in a mesh: sx: 32 (over z, core), sy: 16 (over y, x).
Axes of the slice: x: 4, y: 4, z: 16, core: 2. Of those that a mesh axis runs over, the one named last changes fastest.
Arguments:
- local_source: float32 [32, 16, 768, 256], P('sx', 'sy'), may hold values from -6 to 6
- schur: bfloat16 [32, 16, 768, 768], P('sx', 'sy')
- local_inverse: bfloat16 [32, 16, 768, 768], P('sx', 'sy')
- primal_basis: bfloat16 [32, 16, 768, 32], P('sx', 'sy'), may hold values from -0.21875 to 0.21875
- coarse_inverse: float32 [32, 16, 32, 32], P('sx', 'sy')
- primal_map: int32 [32, 16, 32], P('sx', 'sy'), may hold values from 0 to 1023, as said below
- shared_count: int32 [32, 16, 8], P('sx', 'sy'), may hold values from 0 to 64, as said below
- row_order: int32 [32, 16, 768], P('sx', 'sy'), may hold values from 0 to 767, each once within a row
Outputs:
- solution: float32 [32, 16, 768, 256], P('sx', 'sy')
- residual: float32 [32, 16, 768, 256], P('sx', 'sy')
Inputs may be any that keep to these rules, and one draw needn't show every extreme that they name: shared_count[i, j, d] equals shared_count[i + a, j + b, 7 - d] for offset d = (a, b), and is 0 where (i + a, j + b) lies outside the 32 x 16 grid. A neighbour at offset (0, 1), (0, -1), (1, 0) or (-1, 0) inside the grid shares a quarter of 64 rows or more; a diagonal neighbour shares none or a quarter of 64 or more. Some pair shares exactly 64. primal_map[i, j, m] lies in block (i - 1) mod 32, i or (i + 1) mod 32, block b holding the coarse unknowns b * 32 to (b + 1) * 32 - 1. Each subdomain's row_order holds every row once.
All inputs are finite; a program needn't handle non-finite values.
Results may differ from a plain program's by a relative error of at most 0.0072.
Values sent between devices are 32-bit elements; how exact they have to be, the bound alone decides.
No kernel may reach another device: no remote copies, remote signals or barrier semaphores. Data moves between devices by JAX's collectives and lax.ppermute only.
A program may use at most 64 MiB of HBM per device.

v0:
```python
import jax
import jax.numpy as jnp
from jax import lax
from jax.sharding import PartitionSpec as P

MROW = 64
ITERS = 3


directions = ((-1, -1), (-1, 0), (-1, 1), (0, -1), (0, 1), (1, -1), (1, 0), (1, 1))
centre = 1.6
spread = 1.4


def shifted(shard, axis, by):
    peers = lax.axis_size(axis)
    pairs = [(i, i + by) for i in range(peers) if 0 <= i + by < peers]
    return lax.ppermute(shard, axis, pairs)


def from_behind(block, axis, distance):
    devices = range(lax.axis_size(axis))
    route = [((i - distance) % len(devices), i) for i in devices]
    return lax.ppermute(block, axis, route)


def group_rows(counts, order, rows):
    offsets = jnp.cumsum(counts) - counts
    column = jnp.arange(rows, dtype=jnp.int32)
    places = jnp.minimum(offsets[:, None] + column[None, :], order.shape[0] - 1)
    row_map = order[places]
    valid = (column[None, :] < counts[:, None]).astype(jnp.float32)
    return (row_map, valid)


def assemble(vector, row_map, valid):
    outgoing = vector[row_map] * valid[:, :, None]
    arriving = [None] * 8
    relayed = {}
    for sign in (1, -1):
        chosen = [p for p in range(8) if directions[p][0] == sign]
        bundle = jnp.stack([outgoing[p] for p in chosen])
        received = shifted(bundle, "sx", sign)
        for place, p in enumerate(chosen):
            if directions[p][1] == 0:
                arriving[7 - p] = received[place]
            else:
                relayed[p] = received[place]
    for sign in (1, -1):
        chosen = [p for p in range(8) if directions[p][1] == sign]
        bundle = jnp.stack([outgoing[p] if directions[p][0] == 0 else relayed[p] for p in chosen])
        received = shifted(bundle, "sy", sign)
        for place, p in enumerate(chosen):
            arriving[7 - p] = received[place]
    incoming = jnp.stack(arriving) * valid[:, :, None]
    return vector.at[row_map.reshape(-1)].add(incoming.reshape(-1, vector.shape[-1]))


def coarse_solve(primal, primal_ids, inverse_block):
    block_rows = inverse_block.shape[0]
    highest = lax.Precision.HIGHEST
    count_sx = lax.axis_size("sx")
    mine = lax.axis_index("sx")
    block = primal_ids // block_rows
    within = primal_ids % block_rows
    relative = (block - mine + count_sx) % count_sx
    slots = jnp.arange(block_rows, dtype=jnp.int32)

    def chooser(offset):
        return (
            (relative == offset % count_sx)[:, None] & (within[:, None] == slots[None, :])
        ).astype(jnp.float32)

    own = chooser(0)
    upper = chooser(1)
    lower = chooser(-1)
    block_sum = lax.dot_general(own, primal, (((0,), (0,)), ((), ())), precision=highest)
    for sign, select in ((1, upper), (-1, lower)):
        portion = lax.dot_general(select, primal, (((0,), (0,)), ((), ())), precision=highest)
        block_sum = block_sum + from_behind(portion, "sx", sign)
    solved = jnp.dot(inverse_block, block_sum, precision=highest)
    picked = jnp.dot(own, solved, precision=highest)
    for sign, select in ((-1, upper), (1, lower)):
        picked = picked + jnp.dot(select, from_behind(solved, "sx", sign), precision=highest)
    return picked


def body(
    local_source,
    schur,
    local_inverse,
    primal_basis,
    coarse_inverse,
    primal_map,
    shared_count,
    row_order,
):
    source = local_source[0, 0]
    schur_block = schur[0, 0]
    inverse_local = local_inverse[0, 0]
    basis = primal_basis[0, 0]
    inverse_block = coarse_inverse[0, 0]
    primal_ids = primal_map[0, 0]
    row_map, valid = group_rows(shared_count[0, 0], row_order[0, 0], MROW)
    marks = (
        jnp.zeros((source.shape[0],), jnp.float32).at[row_map.reshape(-1)].add(valid.reshape(-1))
    )
    weight = (1.0 - 0.5 * marks)[:, None]
    right = assemble(source, row_map, valid)
    solution = jnp.zeros_like(right)
    residual = right
    sigma = centre / spread
    rho = 1.0 / sigma
    direction = jnp.zeros_like(right)
    for step in range(ITERS):
        scaled = (weight * residual).astype(jnp.bfloat16)
        local = jnp.dot(inverse_local, scaled, preferred_element_type=jnp.float32)
        primal = lax.dot_general(
            basis, scaled, (((0,), (0,)), ((), ())), preferred_element_type=jnp.float32
        )
        picked = coarse_solve(primal, primal_ids, inverse_block).astype(jnp.bfloat16)
        local = local + jnp.dot(basis, picked, preferred_element_type=jnp.float32)
        update = assemble(weight * local, row_map, valid)
        if step == 0:
            direction = update / centre
            rho = 1.0 / sigma
        else:
            rho_new = 1.0 / (2.0 * sigma - rho)
            direction = rho_new * rho * direction + 2.0 * rho_new / spread * update
            rho = rho_new
        solution = solution + direction
        product = jnp.dot(
            schur_block, direction.astype(jnp.bfloat16), preferred_element_type=jnp.float32
        )
        residual = residual - assemble(product, row_map, valid)
    return (solution[None, None], residual[None, None])


def solution(mesh):
    placed = (
        P("sx", "sy", None, None),
        P("sx", "sy", None, None),
        P("sx", "sy", None, None),
        P("sx", "sy", None, None),
        P("sx", "sy", None, None),
        P("sx", "sy", None),
        P("sx", "sy", None),
        P("sx", "sy", None),
    )
    return jax.shard_map(
        body,
        mesh=mesh,
        in_specs=placed,
        out_specs=(P("sx", "sy", None, None), P("sx", "sy", None, None)),
        check_vma=False,
    )
```

profile of v0, /device:TPU:134, one launch (start us, length us, event | category | flops | bytes accessed | tf_op | source)
XLA Modules:
  0.0 317.7 jit_solution(5136331042449865740)
XLA Ops:
  11.6 4.1 %scatter_custom_fusion = f32[768]{0:T(1024)S(1)} fusion(s32[512]{0:T(512)S(1)} %bitcast.137, f32[512]{0:T(512)S(1)} %reshape.346, f32[]{:T(128)} %constant.70.clone.1), kind=kCustom, calls=%fused_computation.222 | custom fusion | flops 512 | bytes 3076 | tf_op jit(solution)/shard_map/scatter-add | solution.py:106
  16.7 3.4 %collective-permute-start.2 = (f32[3,64,256]{2,1,0:T(8,128)S(1)}, f32[3,64,256]{2,1,0:T(8,128)S(1)}, u32[]{:S(2)}, u32[]{:S(2)}) collective-permute-start(f32[3,64,256]{2,1,0:T(8,128)S(1)} %pad_maximum_fusion), channel_id=1, source_target_pairs={{0,1},{1,2},{2,3},{3,4},{4,5},{5,6},{6,7},{7,8},{8,9},{9,10},{10,1... | collective-permute-start | bytes 589832 | tf_op jit(solution)/shard_map/ppermute | solution.py:18
  20.2 6.1 %collective-permute-done.2 = f32[3,64,256]{2,1,0:T(8,128)S(1)} collective-permute-done((f32[3,64,256]{2,1,0:T(8,128)S(1)}, f32[3,64,256]{2,1,0:T(8,128)S(1)}, u32[]{:S(2)}, u32[]{:S(2)}) %collective-permute-start.2) | collective-permute-done | bytes 196640 | tf_op jit(solution)/shard_map/ppermute | solution.py:18
  26.3 2.7 collective-permute-start.3
  29.7 7.5 %collective-permute-done.3 = f32[3,64,256]{2,1,0:T(8,128)S(1)} collective-permute-done((f32[3,64,256]{2,1,0:T(8,128)S(1)}, f32[3,64,256]{2,1,0:T(8,128)S(1)}, u32[]{:S(2)}, u32[]{:S(2)}) %collective-permute-start.3) | collective-permute-done | bytes 196640 | tf_op jit(solution)/shard_map/ppermute | solution.py:18
  37.4 3.6 %scatter_fusion = f32[768,256]{1,0:T(8,128)S(1)} fusion(f32[768,256]{1,0:T(8,128)S(1)} %bitcast.129, s32[512]{0:T(512)S(1)} %bitcast.140, f32[512,256]{1,0:T(8,128)S(1)} %bitcast_multiply_fusion.6), kind=kCustom, calls=%fused_computation.9 | custom fusion | flops 131072 | bytes 1574912 | tf_op jit(solution)/shard_map/scatter-add | solution.py:56
  42.0 2.9 collective-permute-start.5
  47.0 3.0 collective-permute-start.6
  51.8 3.0 collective-permute-done.7
  62.4 5.0 %collective-permute-done.9 = f32[3,64,256]{2,1,0:T(8,128)S(1)} collective-permute-done((f32[3,64,256]{2,1,0:T(8,128)S(1)}, f32[3,64,256]{2,1,0:T(8,128)S(1)}, u32[]{:S(2)}, u32[]{:S(2)}) %collective-permute-start.9) | collective-permute-done | bytes 196640 | tf_op jit(solution)/shard_map/ppermute | solution.py:18
  67.4 3.4 %collective-permute-start.10 = (f32[3,64,256]{2,1,0:T(8,128)S(1)}, f32[3,64,256]{2,1,0:T(8,128)S(1)}, u32[]{:S(2)}, u32[]{:S(2)}) collective-permute-start(f32[3,64,256]{2,1,0:T(8,128)S(1)} %pad_maximum_fusion.2), channel_id=1, source_target_pairs={{0,1},{1,2},{2,3},{3,4},{4,5},{5,6},{6,7},{7,8},{8,9},{9,10},{10,1... | collective-permute-start | bytes 589832 | tf_op jit(solution)/shard_map/ppermute | solution.py:18
  70.9 4.2 %collective-permute-done.10 = f32[3,64,256]{2,1,0:T(8,128)S(1)} collective-permute-done((f32[3,64,256]{2,1,0:T(8,128)S(1)}, f32[3,64,256]{2,1,0:T(8,128)S(1)}, u32[]{:S(2)}, u32[]{:S(2)}) %collective-permute-start.10) | collective-permute-done | bytes 196640 | tf_op jit(solution)/shard_map/ppermute | solution.py:18
  77.0 7.7 %collective-permute-done.11 = f32[3,64,256]{2,1,0:T(8,128)S(1)} collective-permute-done((f32[3,64,256]{2,1,0:T(8,128)S(1)}, f32[3,64,256]{2,1,0:T(8,128)S(1)}, u32[]{:S(2)}, u32[]{:S(2)}) %collective-permute-start.11) | collective-permute-done | bytes 196640 | tf_op jit(solution)/shard_map/ppermute | solution.py:18
  85.0 3.6 %scatter_fusion.1 = f32[768,256]{1,0:T(8,128)S(1)} fusion(f32[768,256]{1,0:T(8,128)S(1)} %copy.23, s32[512]{0:T(512)S(1)} %bitcast.141, f32[512,256]{1,0:T(8,128)S(1)} %bitcast_multiply_fusion.5), kind=kCustom, calls=%fused_computation.10 | custom fusion | flops 131072 | bytes 1574912 | tf_op jit(solution)/shard_map/scatter-add | solution.py:56
  101.2 5.2 %collective-permute-done.13 = f32[3,64,256]{2,1,0:T(8,128)S(1)} collective-permute-done((f32[3,64,256]{2,1,0:T(8,128)S(1)}, f32[3,64,256]{2,1,0:T(8,128)S(1)}, u32[]{:S(2)}, u32[]{:S(2)}) %collective-permute-start.13) | collective-permute-done | bytes 196640 | tf_op jit(solution)/shard_map/ppermute | solution.py:18
  106.5 3.4 %collective-permute-start.14 = (f32[3,64,256]{2,1,0:T(8,128)S(1)}, f32[3,64,256]{2,1,0:T(8,128)S(1)}, u32[]{:S(2)}, u32[]{:S(2)}) collective-permute-start(f32[3,64,256]{2,1,0:T(8,128)S(1)} %pad_maximum_fusion.4), channel_id=1, source_target_pairs={{0,1},{1,2},{2,3},{3,4},{4,5},{5,6},{6,7},{7,8},{8,9},{9,10},{10,1... | collective-permute-start | bytes 589832 | tf_op jit(solution)/shard_map/ppermute | solution.py:18
  109.9 4.2 %collective-permute-done.14 = f32[3,64,256]{2,1,0:T(8,128)S(1)} collective-permute-done((f32[3,64,256]{2,1,0:T(8,128)S(1)}, f32[3,64,256]{2,1,0:T(8,128)S(1)}, u32[]{:S(2)}, u32[]{:S(2)}) %collective-permute-start.14) | collective-permute-done | bytes 196640 | tf_op jit(solution)/shard_map/ppermute | solution.py:18
  116.0 7.7 %collective-permute-done.15 = f32[3,64,256]{2,1,0:T(8,128)S(1)} collective-permute-done((f32[3,64,256]{2,1,0:T(8,128)S(1)}, f32[3,64,256]{2,1,0:T(8,128)S(1)}, u32[]{:S(2)}, u32[]{:S(2)}) %collective-permute-start.15) | collective-permute-done | bytes 196640 | tf_op jit(solution)/shard_map/ppermute | solution.py:18
  124.7 4.1 %scatter_fusion.2 = f32[768,256]{1,0:T(8,128)S(1)} fusion(f32[768,256]{1,0:T(8,128)S(1)} %copy.25, s32[512]{0:T(512)} %bitcast.138, f32[512,256]{1,0:T(8,128)} %bitcast_multiply_fusion.4), kind=kCustom, calls=%fused_computation.11 | custom fusion | flops 131072 | bytes 1574912 | tf_op jit(solution)/shard_map/scatter-add | solution.py:56
  130.6 2.9 collective-permute-start.17
  135.6 3.0 collective-permute-start.18
  140.4 3.0 collective-permute-done.19
  151.0 5.0 %collective-permute-done.21 = f32[3,64,256]{2,1,0:T(8,128)S(1)} collective-permute-done((f32[3,64,256]{2,1,0:T(8,128)S(1)}, f32[3,64,256]{2,1,0:T(8,128)S(1)}, u32[]{:S(2)}, u32[]{:S(2)}) %collective-permute-start.21) | collective-permute-done | bytes 196640 | tf_op jit(solution)/shard_map/ppermute | solution.py:18
  156.0 3.4 %collective-permute-start.22 = (f32[3,64,256]{2,1,0:T(8,128)S(1)}, f32[3,64,256]{2,1,0:T(8,128)S(1)}, u32[]{:S(2)}, u32[]{:S(2)}) collective-permute-start(f32[3,64,256]{2,1,0:T(8,128)S(1)} %pad_maximum_fusion.6), channel_id=1, source_target_pairs={{0,1},{1,2},{2,3},{3,4},{4,5},{5,6},{6,7},{7,8},{8,9},{9,10},{10,1... | collective-permute-start | bytes 589832 | tf_op jit(solution)/shard_map/ppermute | solution.py:18
  159.4 4.2 %collective-permute-done.22 = f32[3,64,256]{2,1,0:T(8,128)S(1)} collective-permute-done((f32[3,64,256]{2,1,0:T(8,128)S(1)}, f32[3,64,256]{2,1,0:T(8,128)S(1)}, u32[]{:S(2)}, u32[]{:S(2)}) %collective-permute-start.22) | collective-permute-done | bytes 196640 | tf_op jit(solution)/shard_map/ppermute | solution.py:18
  165.5 7.7 %collective-permute-done.23 = f32[3,64,256]{2,1,0:T(8,128)S(1)} collective-permute-done((f32[3,64,256]{2,1,0:T(8,128)S(1)}, f32[3,64,256]{2,1,0:T(8,128)S(1)}, u32[]{:S(2)}, u32[]{:S(2)}) %collective-permute-start.23) | collective-permute-done | bytes 196640 | tf_op jit(solution)/shard_map/ppermute | solution.py:18
  173.5 3.6 %scatter_fusion.3 = f32[768,256]{1,0:T(8,128)S(1)} fusion(f32[768,256]{1,0:T(8,128)S(1)} %copy.27, s32[512]{0:T(512)S(1)} %bitcast.142, f32[512,256]{1,0:T(8,128)S(1)} %bitcast_multiply_fusion.3), kind=kCustom, calls=%fused_computation.12 | custom fusion | flops 131072 | bytes 1574912 | tf_op jit(solution)/shard_map/scatter-add | solution.py:56
  189.8 5.0 %collective-permute-done.25 = f32[3,64,256]{2,1,0:T(8,128)S(1)} collective-permute-done((f32[3,64,256]{2,1,0:T(8,128)S(1)}, f32[3,64,256]{2,1,0:T(8,128)S(1)}, u32[]{:S(2)}, u32[]{:S(2)}) %collective-permute-start.25) | collective-permute-done | bytes 196640 | tf_op jit(solution)/shard_map/ppermute | solution.py:18
  194.9 3.4 %collective-permute-start.26 = (f32[3,64,256]{2,1,0:T(8,128)S(1)}, f32[3,64,256]{2,1,0:T(8,128)S(1)}, u32[]{:S(2)}, u32[]{:S(2)}) collective-permute-start(f32[3,64,256]{2,1,0:T(8,128)S(1)} %pad_maximum_fusion.8), channel_id=1, source_target_pairs={{0,1},{1,2},{2,3},{3,4},{4,5},{5,6},{6,7},{7,8},{8,9},{9,10},{10,1... | collective-permute-start | bytes 589832 | tf_op jit(solution)/shard_map/ppermute | solution.py:18
  198.3 4.2 %collective-permute-done.26 = f32[3,64,256]{2,1,0:T(8,128)S(1)} collective-permute-done((f32[3,64,256]{2,1,0:T(8,128)S(1)}, f32[3,64,256]{2,1,0:T(8,128)S(1)}, u32[]{:S(2)}, u32[]{:S(2)}) %collective-permute-start.26) | collective-permute-done | bytes 196640 | tf_op jit(solution)/shard_map/ppermute | solution.py:18
  204.4 7.7 %collective-permute-done.27 = f32[3,64,256]{2,1,0:T(8,128)S(1)} collective-permute-done((f32[3,64,256]{2,1,0:T(8,128)S(1)}, f32[3,64,256]{2,1,0:T(8,128)S(1)}, u32[]{:S(2)}, u32[]{:S(2)}) %collective-permute-start.27) | collective-permute-done | bytes 196640 | tf_op jit(solution)/shard_map/ppermute | solution.py:18
  213.1 4.3 %scatter_fusion.4 = f32[768,256]{1,0:T(8,128)S(1)} fusion(f32[768,256]{1,0:T(8,128)S(1)} %copy.29, s32[512]{0:T(512)} %bitcast.139, f32[512,256]{1,0:T(8,128)} %bitcast_multiply_fusion.2), kind=kCustom, calls=%fused_computation.13 | custom fusion | flops 131072 | bytes 1574912 | tf_op jit(solution)/shard_map/scatter-add | solution.py:56
  219.7 2.9 collective-permute-start.29
  224.7 3.0 collective-permute-start.30
  229.5 3.0 collective-permute-done.31
  243.8 5.0 %collective-permute-done.33 = f32[3,64,256]{2,1,0:T(8,128)S(1)} collective-permute-done((f32[3,64,256]{2,1,0:T(8,128)S(1)}, f32[3,64,256]{2,1,0:T(8,128)S(1)}, u32[]{:S(2)}, u32[]{:S(2)}) %collective-permute-start.33) | collective-permute-done | bytes 196640 | tf_op jit(solution)/shard_map/ppermute | solution.py:18
  248.8 3.4 %collective-permute-start.34 = (f32[3,64,256]{2,1,0:T(8,128)S(1)}, f32[3,64,256]{2,1,0:T(8,128)S(1)}, u32[]{:S(2)}, u32[]{:S(2)}) collective-permute-start(f32[3,64,256]{2,1,0:T(8,128)S(1)} %pad_maximum_fusion.10), channel_id=1, source_target_pairs={{0,1},{1,2},{2,3},{3,4},{4,5},{5,6},{6,7},{7,8},{8,9},{9,10},{10,1... | collective-permute-start | bytes 589832 | tf_op jit(solution)/shard_map/ppermute | solution.py:18
  252.2 4.2 %collective-permute-done.34 = f32[3,64,256]{2,1,0:T(8,128)S(1)} collective-permute-done((f32[3,64,256]{2,1,0:T(8,128)S(1)}, f32[3,64,256]{2,1,0:T(8,128)S(1)}, u32[]{:S(2)}, u32[]{:S(2)}) %collective-permute-start.34) | collective-permute-done | bytes 196640 | tf_op jit(solution)/shard_map/ppermute | solution.py:18
  258.4 7.7 %collective-permute-done.35 = f32[3,64,256]{2,1,0:T(8,128)S(1)} collective-permute-done((f32[3,64,256]{2,1,0:T(8,128)S(1)}, f32[3,64,256]{2,1,0:T(8,128)S(1)}, u32[]{:S(2)}, u32[]{:S(2)}) %collective-permute-start.35) | collective-permute-done | bytes 196640 | tf_op jit(solution)/shard_map/ppermute | solution.py:18
  267.1 4.1 %scatter_fusion.5 = f32[768,256]{1,0:T(8,128)S(1)} fusion(f32[768,256]{1,0:T(8,128)S(1)} %copy.31, s32[512]{0:T(512)S(1)} %bitcast.143, f32[512,256]{1,0:T(8,128)} %bitcast_multiply_fusion.1), kind=kCustom, calls=%fused_computation.14 | custom fusion | flops 131072 | bytes 1574912 | tf_op jit(solution)/shard_map/scatter-add | solution.py:56
  271.2 2.8 convolution_bitcast_fusion
  276.3 3.4 %gather_fusion.7 = f32[512,256]{1,0:T(8,128)} fusion(f32[768,256]{1,0:T(8,128)} %copy.33, s32[1024]{0:T(1024)S(1)} %pad_clamp_fusion), kind=kCustom, calls=%fused_computation.7 | custom fusion | bytes 1050624 | tf_op jit(solution)/shard_map/gather | solution.py:37
  286.0 5.0 %collective-permute-done.37 = f32[3,64,256]{2,1,0:T(8,128)S(1)} collective-permute-done((f32[3,64,256]{2,1,0:T(8,128)S(1)}, f32[3,64,256]{2,1,0:T(8,128)S(1)}, u32[]{:S(2)}, u32[]{:S(2)}) %collective-permute-start.37) | collective-permute-done | bytes 196640 | tf_op jit(solution)/shard_map/ppermute | solution.py:18
  291.1 3.4 %collective-permute-start.38 = (f32[3,64,256]{2,1,0:T(8,128)S(1)}, f32[3,64,256]{2,1,0:T(8,128)S(1)}, u32[]{:S(2)}, u32[]{:S(2)}) collective-permute-start(f32[3,64,256]{2,1,0:T(8,128)S(1)} %pad_maximum_fusion.12), channel_id=1, source_target_pairs={{0,1},{1,2},{2,3},{3,4},{4,5},{5,6},{6,7},{7,8},{8,9},{9,10},{10,1... | collective-permute-start | bytes 589832 | tf_op jit(solution)/shard_map/ppermute | solution.py:18
  294.5 4.2 %collective-permute-done.38 = f32[3,64,256]{2,1,0:T(8,128)S(1)} collective-permute-done((f32[3,64,256]{2,1,0:T(8,128)S(1)}, f32[3,64,256]{2,1,0:T(8,128)S(1)}, u32[]{:S(2)}, u32[]{:S(2)}) %collective-permute-start.38) | collective-permute-done | bytes 196640 | tf_op jit(solution)/shard_map/ppermute | solution.py:18
  300.6 7.7 %collective-permute-done.39 = f32[3,64,256]{2,1,0:T(8,128)S(1)} collective-permute-done((f32[3,64,256]{2,1,0:T(8,128)S(1)}, f32[3,64,256]{2,1,0:T(8,128)S(1)}, u32[]{:S(2)}, u32[]{:S(2)}) %collective-permute-start.39) | collective-permute-done | bytes 196640 | tf_op jit(solution)/shard_map/ppermute | solution.py:18
  309.4 5.5 %scatter_fusion.6 = f32[768,256]{1,0:T(8,128)} fusion(f32[768,256]{1,0:T(8,128)} %copy.33, s32[512]{0:T(512)S(1)} %bitcast.144, f32[512,256]{1,0:T(8,128)} %bitcast_multiply_fusion), kind=kCustom, calls=%fused_computation.15 | custom fusion | flops 131072 | bytes 1574912 | tf_op jit(solution)/shard_map/scatter-add | solution.py:56
  314.9 2.8 subtract_bitcast_fusion
  (280 shorter events, 105.0 us)
Async XLA Ops:
  0.6 44.3 %copy-start = (bf16[1,1,768,768]{3,2,1,0:T(8,128)(2,1)S(1)}, bf16[1,1,768,768]{3,2,1,0:T(8,128)(2,1)}, u32[]{:S(2)}) copy-start(bf16[1,1,768,768]{3,2,1,0:T(8,128)(2,1)} %param.10) | copy-start | bytes 3538948
  6.6 9.7 %collective-permute-start = (f32[3,64,256]{2,1,0:T(8,128)S(1)}, f32[3,64,256]{2,1,0:T(8,128)S(1)}, u32[]{:S(2)}, u32[]{:S(2)}) collective-permute-start(f32[3,64,256]{2,1,0:T(8,128)S(1)} %get-tuple-element.30), channel_id=1, source_target_pairs={{16,0},{32,16},{48,32},{64,48},{80,64},{96,80},{112,96},{128,112},... | collective-permute-start | bytes 589832 | tf_op jit(solution)/shard_map/ppermute | solution.py:18
  8.5 8.2 %collective-permute-start.1 = (f32[3,64,256]{2,1,0:T(8,128)S(1)}, f32[3,64,256]{2,1,0:T(8,128)S(1)}, u32[]{:S(2)}, u32[]{:S(2)}) collective-permute-start(f32[3,64,256]{2,1,0:T(8,128)S(1)} %get-tuple-element.31), channel_id=1, source_target_pairs={{0,16},{16,32},{32,48},{48,64},{64,80},{80,96},{96,112},{112,128},... | collective-permute-start | bytes 589832 | tf_op jit(solution)/shard_map/ppermute | solution.py:18
  16.7 9.5 %collective-permute-start.2 = (f32[3,64,256]{2,1,0:T(8,128)S(1)}, f32[3,64,256]{2,1,0:T(8,128)S(1)}, u32[]{:S(2)}, u32[]{:S(2)}) collective-permute-start(f32[3,64,256]{2,1,0:T(8,128)S(1)} %pad_maximum_fusion), channel_id=1, source_target_pairs={{0,1},{1,2},{2,3},{3,4},{4,5},{5,6},{6,7},{7,8},{8,9},{9,10},{10,1... | collective-permute-start | bytes 589832 | tf_op jit(solution)/shard_map/ppermute | solution.py:18
  20.1 31.4 %copy-start.27 = (pred[32]{0:T(512)(128)(4,1)}, pred[32]{0:T(512)(128)(4,1)S(1)}, u32[]{:S(2)}) copy-start(pred[32]{0:T(512)(128)(4,1)S(1)} %get-tuple-element.60) | copy-start | bytes 100
  20.1 34.6 %copy-start.24 = (pred[32]{0:T(512)(128)(4,1)}, pred[32]{0:T(512)(128)(4,1)S(1)}, u32[]{:S(2)}) copy-start(pred[32]{0:T(512)(128)(4,1)S(1)} %get-tuple-element.61) | copy-start | bytes 100
  26.2 11.2 %copy-start.11 = (s32[512,1]{0,1:T(1,128)S(1)}, s32[512,1]{0,1:T(1,128)}, u32[]{:S(2)}) copy-start(s32[512,1]{0,1:T(1,128)} %copy-done.10) | copy-start | bytes 6148
  26.3 10.9 %collective-permute-start.3 = (f32[3,64,256]{2,1,0:T(8,128)S(1)}, f32[3,64,256]{2,1,0:T(8,128)S(1)}, u32[]{:S(2)}, u32[]{:S(2)}) collective-permute-start(f32[3,64,256]{2,1,0:T(8,128)S(1)} %pad_maximum_fusion.1), channel_id=1, source_target_pairs={{1,0},{2,1},{3,2},{4,3},{5,4},{6,5},{7,6},{8,7},{9,8},{10,9},{11,1... | collective-permute-start | bytes 589832 | tf_op jit(solution)/shard_map/ppermute | solution.py:18
  29.7 25.1 %copy-start.18 = (s32[32]{0:T(128)}, s32[32]{0:T(128)S(1)}, u32[]{:S(2)}) copy-start(s32[32]{0:T(128)S(1)} %and_select_fusion) | copy-start | bytes 388
  42.0 13.0 %copy-start.4 = (bf16[1,1,768,32]{2,3,1,0:T(8,128)(2,1)S(1)}, bf16[1,1,768,32]{2,3,1,0:T(8,128)(2,1)}, u32[]{:S(2)}) copy-start(bf16[1,1,768,32]{2,3,1,0:T(8,128)(2,1)} %param.11) | copy-start | bytes 147460
  42.0 4.6 %collective-permute-start.4 = (f32[32,256]{1,0:T(8,128)S(1)}, f32[32,256]{1,0:T(8,128)S(1)}, u32[]{:S(2)}, u32[]{:S(2)}) collective-permute-start(f32[32,256]{1,0:T(8,128)S(1)} %fusion.59), channel_id=1, source_target_pairs={{496,0},{0,16},{16,32},{32,48},{48,64},{64,80},{80,96},{96,112},{1... | collective-permute-start | bytes 98312 | tf_op jit(solution)/shard_map/ppermute | solution.py:24
  42.0 4.5 %collective-permute-start.5 = (f32[32,256]{1,0:T(8,128)S(1)}, f32[32,256]{1,0:T(8,128)S(1)}, u32[]{:S(2)}, u32[]{:S(2)}) collective-permute-start(f32[32,256]{1,0:T(8,128)S(1)} %fusion.68), channel_id=1, source_target_pairs={{16,0},{32,16},{48,32},{64,48},{80,64},{96,80},{112,96},{128,112},... | collective-permute-start | bytes 98312 | tf_op jit(solution)/shard_map/ppermute | solution.py:24
  47.0 4.6 %collective-permute-start.6 = (f32[32,256]{1,0:T(8,128)S(1)}, f32[32,256]{1,0:T(8,128)S(1)}, u32[]{:S(2)}, u32[]{:S(2)}) collective-permute-start(f32[32,256]{1,0:T(8,128)S(1)} %bitcast.147), channel_id=1, source_target_pairs={{16,0},{32,16},{48,32},{64,48},{80,64},{96,80},{112,96},{128,112},... | collective-permute-start | bytes 98312 | tf_op jit(solution)/shard_map/ppermute | solution.py:24
  50.2 4.6 %collective-permute-start.7 = (f32[32,256]{1,0:T(8,128)S(1)}, f32[32,256]{1,0:T(8,128)S(1)}, u32[]{:S(2)}, u32[]{:S(2)}) collective-permute-start(f32[32,256]{1,0:T(8,128)S(1)} %bitcast.148), channel_id=1, source_target_pairs={{496,0},{0,16},{16,32},{32,48},{48,64},{64,80},{80,96},{96,112},{1... | collective-permute-start | bytes 98312 | tf_op jit(solution)/shard_map/ppermute | solution.py:24
  57.3 5.1 %collective-permute-start.8 = (f32[3,64,256]{2,1,0:T(8,128)S(1)}, f32[3,64,256]{2,1,0:T(8,128)S(1)}, u32[]{:S(2)}, u32[]{:S(2)}) collective-permute-start(f32[3,64,256]{2,1,0:T(8,128)S(1)} %get-tuple-element.26), channel_id=1, source_target_pairs={{16,0},{32,16},{48,32},{64,48},{80,64},{96,80},{112,96},{128,112},... | collective-permute-start | bytes 589832 | tf_op jit(solution)/shard_map/ppermute | solution.py:18
  59.2 8.2 %collective-permute-start.9 = (f32[3,64,256]{2,1,0:T(8,128)S(1)}, f32[3,64,256]{2,1,0:T(8,128)S(1)}, u32[]{:S(2)}, u32[]{:S(2)}) collective-permute-start(f32[3,64,256]{2,1,0:T(8,128)S(1)} %get-tuple-element.27), channel_id=1, source_target_pairs={{0,16},{16,32},{32,48},{48,64},{64,80},{80,96},{96,112},{112,128},... | collective-permute-start | bytes 589832 | tf_op jit(solution)/shard_map/ppermute | solution.py:18
  67.4 7.6 %collective-permute-start.10 = (f32[3,64,256]{2,1,0:T(8,128)S(1)}, f32[3,64,256]{2,1,0:T(8,128)S(1)}, u32[]{:S(2)}, u32[]{:S(2)}) collective-permute-start(f32[3,64,256]{2,1,0:T(8,128)S(1)} %pad_maximum_fusion.2), channel_id=1, source_target_pairs={{0,1},{1,2},{2,3},{3,4},{4,5},{5,6},{6,7},{7,8},{8,9},{9,10},{10,1... | collective-permute-start | bytes 589832 | tf_op jit(solution)/shard_map/ppermute | solution.py:18
  75.1 9.7 %collective-permute-start.11 = (f32[3,64,256]{2,1,0:T(8,128)S(1)}, f32[3,64,256]{2,1,0:T(8,128)S(1)}, u32[]{:S(2)}, u32[]{:S(2)}) collective-permute-start(f32[3,64,256]{2,1,0:T(8,128)S(1)} %pad_maximum_fusion.3), channel_id=1, source_target_pairs={{1,0},{2,1},{3,2},{4,3},{5,4},{6,5},{7,6},{8,7},{9,8},{10,9},{11,1... | collective-permute-start | bytes 589832 | tf_op jit(solution)/shard_map/ppermute | solution.py:18
  96.1 5.1 %collective-permute-start.12 = (f32[3,64,256]{2,1,0:T(8,128)S(1)}, f32[3,64,256]{2,1,0:T(8,128)S(1)}, u32[]{:S(2)}, u32[]{:S(2)}) collective-permute-start(f32[3,64,256]{2,1,0:T(8,128)S(1)} %get-tuple-element.22), channel_id=1, source_target_pairs={{16,0},{32,16},{48,32},{64,48},{80,64},{96,80},{112,96},{128,112},... | collective-permute-start | bytes 589832 | tf_op jit(solution)/shard_map/ppermute | solution.py:18
  98.2 8.2 %collective-permute-start.13 = (f32[3,64,256]{2,1,0:T(8,128)S(1)}, f32[3,64,256]{2,1,0:T(8,128)S(1)}, u32[]{:S(2)}, u32[]{:S(2)}) collective-permute-start(f32[3,64,256]{2,1,0:T(8,128)S(1)} %get-tuple-element.23), channel_id=1, source_target_pairs={{0,16},{16,32},{32,48},{48,64},{64,80},{80,96},{96,112},{112,128},... | collective-permute-start | bytes 589832 | tf_op jit(solution)/shard_map/ppermute | solution.py:18
  106.5 7.6 %collective-permute-start.14 = (f32[3,64,256]{2,1,0:T(8,128)S(1)}, f32[3,64,256]{2,1,0:T(8,128)S(1)}, u32[]{:S(2)}, u32[]{:S(2)}) collective-permute-start(f32[3,64,256]{2,1,0:T(8,128)S(1)} %pad_maximum_fusion.4), channel_id=1, source_target_pairs={{0,1},{1,2},{2,3},{3,4},{4,5},{5,6},{6,7},{7,8},{8,9},{9,10},{10,1... | collective-permute-start | bytes 589832 | tf_op jit(solution)/shard_map/ppermute | solution.py:18
  114.1 9.7 %collective-permute-start.15 = (f32[3,64,256]{2,1,0:T(8,128)S(1)}, f32[3,64,256]{2,1,0:T(8,128)S(1)}, u32[]{:S(2)}, u32[]{:S(2)}) collective-permute-start(f32[3,64,256]{2,1,0:T(8,128)S(1)} %pad_maximum_fusion.5), channel_id=1, source_target_pairs={{1,0},{2,1},{3,2},{4,3},{5,4},{6,5},{7,6},{8,7},{9,8},{10,9},{11,1... | collective-permute-start | bytes 589832 | tf_op jit(solution)/shard_map/ppermute | solution.py:18
  130.6 4.6 %collective-permute-start.16 = (f32[32,256]{1,0:T(8,128)S(1)}, f32[32,256]{1,0:T(8,128)S(1)}, u32[]{:S(2)}, u32[]{:S(2)}) collective-permute-start(f32[32,256]{1,0:T(8,128)S(1)} %fusion.56), channel_id=1, source_target_pairs={{496,0},{0,16},{16,32},{32,48},{48,64},{64,80},{80,96},{96,112},{1... | collective-permute-start | bytes 98312 | tf_op jit(solution)/shard_map/ppermute | solution.py:24
  130.6 4.5 %collective-permute-start.17 = (f32[32,256]{1,0:T(8,128)S(1)}, f32[32,256]{1,0:T(8,128)S(1)}, u32[]{:S(2)}, u32[]{:S(2)}) collective-permute-start(f32[32,256]{1,0:T(8,128)S(1)} %fusion.65), channel_id=1, source_target_pairs={{16,0},{32,16},{48,32},{64,48},{80,64},{96,80},{112,96},{128,112},... | collective-permute-start | bytes 98312 | tf_op jit(solution)/shard_map/ppermute | solution.py:24
  135.6 4.6 %collective-permute-start.18 = (f32[32,256]{1,0:T(8,128)S(1)}, f32[32,256]{1,0:T(8,128)S(1)}, u32[]{:S(2)}, u32[]{:S(2)}) collective-permute-start(f32[32,256]{1,0:T(8,128)S(1)} %bitcast.149), channel_id=1, source_target_pairs={{16,0},{32,16},{48,32},{64,48},{80,64},{96,80},{112,96},{128,112},... | collective-permute-start | bytes 98312 | tf_op jit(solution)/shard_map/ppermute | solution.py:24
  138.8 4.6 %collective-permute-start.19 = (f32[32,256]{1,0:T(8,128)S(1)}, f32[32,256]{1,0:T(8,128)S(1)}, u32[]{:S(2)}, u32[]{:S(2)}) collective-permute-start(f32[32,256]{1,0:T(8,128)S(1)} %bitcast.150), channel_id=1, source_target_pairs={{496,0},{0,16},{16,32},{32,48},{48,64},{64,80},{80,96},{96,112},{1... | collective-permute-start | bytes 98312 | tf_op jit(solution)/shard_map/ppermute | solution.py:24
  145.8 5.1 %collective-permute-start.20 = (f32[3,64,256]{2,1,0:T(8,128)S(1)}, f32[3,64,256]{2,1,0:T(8,128)S(1)}, u32[]{:S(2)}, u32[]{:S(2)}) collective-permute-start(f32[3,64,256]{2,1,0:T(8,128)S(1)} %get-tuple-element.18), channel_id=1, source_target_pairs={{16,0},{32,16},{48,32},{64,48},{80,64},{96,80},{112,96},{128,112},... | collective-permute-start | bytes 589832 | tf_op jit(solution)/shard_map/ppermute | solution.py:18
  147.8 8.2 %collective-permute-start.21 = (f32[3,64,256]{2,1,0:T(8,128)S(1)}, f32[3,64,256]{2,1,0:T(8,128)S(1)}, u32[]{:S(2)}, u32[]{:S(2)}) collective-permute-start(f32[3,64,256]{2,1,0:T(8,128)S(1)} %get-tuple-element.19), channel_id=1, source_target_pairs={{0,16},{16,32},{32,48},{48,64},{64,80},{80,96},{96,112},{112,128},... | collective-permute-start | bytes 589832 | tf_op jit(solution)/shard_map/ppermute | solution.py:18
  156.0 7.6 %collective-permute-start.22 = (f32[3,64,256]{2,1,0:T(8,128)S(1)}, f32[3,64,256]{2,1,0:T(8,128)S(1)}, u32[]{:S(2)}, u32[]{:S(2)}) collective-permute-start(f32[3,64,256]{2,1,0:T(8,128)S(1)} %pad_maximum_fusion.6), channel_id=1, source_target_pairs={{0,1},{1,2},{2,3},{3,4},{4,5},{5,6},{6,7},{7,8},{8,9},{9,10},{10,1... | collective-permute-start | bytes 589832 | tf_op jit(solution)/shard_map/ppermute | solution.py:18
  163.6 9.9 %copy-start.13 = (s32[512,1]{0,1:T(1,128)S(1)}, s32[512,1]{0,1:T(1,128)}, u32[]{:S(2)}) copy-start(s32[512,1]{0,1:T(1,128)} %copy-done.10) | copy-start | bytes 6148
  163.6 9.7 %collective-permute-start.23 = (f32[3,64,256]{2,1,0:T(8,128)S(1)}, f32[3,64,256]{2,1,0:T(8,128)S(1)}, u32[]{:S(2)}, u32[]{:S(2)}) collective-permute-start(f32[3,64,256]{2,1,0:T(8,128)S(1)} %pad_maximum_fusion.7), channel_id=1, source_target_pairs={{1,0},{2,1},{3,2},{4,3},{5,4},{6,5},{7,6},{8,7},{9,8},{10,9},{11,1... | collective-permute-start | bytes 589832 | tf_op jit(solution)/shard_map/ppermute | solution.py:18
  184.7 5.1 %collective-permute-start.24 = (f32[3,64,256]{2,1,0:T(8,128)S(1)}, f32[3,64,256]{2,1,0:T(8,128)S(1)}, u32[]{:S(2)}, u32[]{:S(2)}) collective-permute-start(f32[3,64,256]{2,1,0:T(8,128)S(1)} %get-tuple-element.14), channel_id=1, source_target_pairs={{16,0},{32,16},{48,32},{64,48},{80,64},{96,80},{112,96},{128,112},... | collective-permute-start | bytes 589832 | tf_op jit(solution)/shard_map/ppermute | solution.py:18
  186.6 8.2 %collective-permute-start.25 = (f32[3,64,256]{2,1,0:T(8,128)S(1)}, f32[3,64,256]{2,1,0:T(8,128)S(1)}, u32[]{:S(2)}, u32[]{:S(2)}) collective-permute-start(f32[3,64,256]{2,1,0:T(8,128)S(1)} %get-tuple-element.15), channel_id=1, source_target_pairs={{0,16},{16,32},{32,48},{48,64},{64,80},{80,96},{96,112},{112,128},... | collective-permute-start | bytes 589832 | tf_op jit(solution)/shard_map/ppermute | solution.py:18
  194.9 7.6 %collective-permute-start.26 = (f32[3,64,256]{2,1,0:T(8,128)S(1)}, f32[3,64,256]{2,1,0:T(8,128)S(1)}, u32[]{:S(2)}, u32[]{:S(2)}) collective-permute-start(f32[3,64,256]{2,1,0:T(8,128)S(1)} %pad_maximum_fusion.8), channel_id=1, source_target_pairs={{0,1},{1,2},{2,3},{3,4},{4,5},{5,6},{6,7},{7,8},{8,9},{9,10},{10,1... | collective-permute-start | bytes 589832 | tf_op jit(solution)/shard_map/ppermute | solution.py:18
  202.5 9.7 %collective-permute-start.27 = (f32[3,64,256]{2,1,0:T(8,128)S(1)}, f32[3,64,256]{2,1,0:T(8,128)S(1)}, u32[]{:S(2)}, u32[]{:S(2)}) collective-permute-start(f32[3,64,256]{2,1,0:T(8,128)S(1)} %pad_maximum_fusion.9), channel_id=1, source_target_pairs={{1,0},{2,1},{3,2},{4,3},{5,4},{6,5},{7,6},{8,7},{9,8},{10,9},{11,1... | collective-permute-start | bytes 589832 | tf_op jit(solution)/shard_map/ppermute | solution.py:18
  219.7 4.6 %collective-permute-start.28 = (f32[32,256]{1,0:T(8,128)S(1)}, f32[32,256]{1,0:T(8,128)S(1)}, u32[]{:S(2)}, u32[]{:S(2)}) collective-permute-start(f32[32,256]{1,0:T(8,128)S(1)} %fusion.53), channel_id=1, source_target_pairs={{496,0},{0,16},{16,32},{32,48},{48,64},{64,80},{80,96},{96,112},{1... | collective-permute-start | bytes 98312 | tf_op jit(solution)/shard_map/ppermute | solution.py:24
  219.7 4.5 %collective-permute-start.29 = (f32[32,256]{1,0:T(8,128)S(1)}, f32[32,256]{1,0:T(8,128)S(1)}, u32[]{:S(2)}, u32[]{:S(2)}) collective-permute-start(f32[32,256]{1,0:T(8,128)S(1)} %fusion.62), channel_id=1, source_target_pairs={{16,0},{32,16},{48,32},{64,48},{80,64},{96,80},{112,96},{128,112},... | collective-permute-start | bytes 98312 | tf_op jit(solution)/shard_map/ppermute | solution.py:24
  224.7 4.6 %collective-permute-start.30 = (f32[32,256]{1,0:T(8,128)S(1)}, f32[32,256]{1,0:T(8,128)S(1)}, u32[]{:S(2)}, u32[]{:S(2)}) collective-permute-start(f32[32,256]{1,0:T(8,128)S(1)} %bitcast.145), channel_id=1, source_target_pairs={{16,0},{32,16},{48,32},{64,48},{80,64},{96,80},{112,96},{128,112},... | collective-permute-start | bytes 98312 | tf_op jit(solution)/shard_map/ppermute | solution.py:24
  227.9 4.6 %collective-permute-start.31 = (f32[32,256]{1,0:T(8,128)S(1)}, f32[32,256]{1,0:T(8,128)S(1)}, u32[]{:S(2)}, u32[]{:S(2)}) collective-permute-start(f32[32,256]{1,0:T(8,128)S(1)} %bitcast.146), channel_id=1, source_target_pairs={{496,0},{0,16},{16,32},{32,48},{48,64},{64,80},{80,96},{96,112},{1... | collective-permute-start | bytes 98312 | tf_op jit(solution)/shard_map/ppermute | solution.py:24
  238.7 5.1 %collective-permute-start.32 = (f32[3,64,256]{2,1,0:T(8,128)S(1)}, f32[3,64,256]{2,1,0:T(8,128)S(1)}, u32[]{:S(2)}, u32[]{:S(2)}) collective-permute-start(f32[3,64,256]{2,1,0:T(8,128)S(1)} %get-tuple-element.10), channel_id=1, source_target_pairs={{16,0},{32,16},{48,32},{64,48},{80,64},{96,80},{112,96},{128,112},... | collective-permute-start | bytes 589832 | tf_op jit(solution)/shard_map/ppermute | solution.py:18
  240.6 8.2 %collective-permute-start.33 = (f32[3,64,256]{2,1,0:T(8,128)S(1)}, f32[3,64,256]{2,1,0:T(8,128)S(1)}, u32[]{:S(2)}, u32[]{:S(2)}) collective-permute-start(f32[3,64,256]{2,1,0:T(8,128)S(1)} %get-tuple-element.11), channel_id=1, source_target_pairs={{0,16},{16,32},{32,48},{48,64},{64,80},{80,96},{96,112},{112,128},... | collective-permute-start | bytes 589832 | tf_op jit(solution)/shard_map/ppermute | solution.py:18
  248.8 7.6 %collective-permute-start.34 = (f32[3,64,256]{2,1,0:T(8,128)S(1)}, f32[3,64,256]{2,1,0:T(8,128)S(1)}, u32[]{:S(2)}, u32[]{:S(2)}) collective-permute-start(f32[3,64,256]{2,1,0:T(8,128)S(1)} %pad_maximum_fusion.10), channel_id=1, source_target_pairs={{0,1},{1,2},{2,3},{3,4},{4,5},{5,6},{6,7},{7,8},{8,9},{9,10},{10,1... | collective-permute-start | bytes 589832 | tf_op jit(solution)/shard_map/ppermute | solution.py:18
  256.4 10.7 %copy-start.14 = (s32[512,1]{0,1:T(1,128)S(1)}, s32[512,1]{0,1:T(1,128)}, u32[]{:S(2)}) copy-start(s32[512,1]{0,1:T(1,128)} %copy-done.10) | copy-start | bytes 6148
  256.4 9.7 %collective-permute-start.35 = (f32[3,64,256]{2,1,0:T(8,128)S(1)}, f32[3,64,256]{2,1,0:T(8,128)S(1)}, u32[]{:S(2)}, u32[]{:S(2)}) collective-permute-start(f32[3,64,256]{2,1,0:T(8,128)S(1)} %pad_maximum_fusion.11), channel_id=1, source_target_pairs={{1,0},{2,1},{3,2},{4,3},{5,4},{6,5},{7,6},{8,7},{9,8},{10,9},{11,1... | collective-permute-start | bytes 589832 | tf_op jit(solution)/shard_map/ppermute | solution.py:18
  280.9 5.1 %collective-permute-start.36 = (f32[3,64,256]{2,1,0:T(8,128)S(1)}, f32[3,64,256]{2,1,0:T(8,128)S(1)}, u32[]{:S(2)}, u32[]{:S(2)}) collective-permute-start(f32[3,64,256]{2,1,0:T(8,128)S(1)} %get-tuple-element.6), channel_id=1, source_target_pairs={{16,0},{32,16},{48,32},{64,48},{80,64},{96,80},{112,96},{128,112},... | collective-permute-start | bytes 589832 | tf_op jit(solution)/shard_map/ppermute | solution.py:18
  282.8 8.2 %collective-permute-start.37 = (f32[3,64,256]{2,1,0:T(8,128)S(1)}, f32[3,64,256]{2,1,0:T(8,128)S(1)}, u32[]{:S(2)}, u32[]{:S(2)}) collective-permute-start(f32[3,64,256]{2,1,0:T(8,128)S(1)} %get-tuple-element.7), channel_id=1, source_target_pairs={{0,16},{16,32},{32,48},{48,64},{64,80},{80,96},{96,112},{112,128},... | collective-permute-start | bytes 589832 | tf_op jit(solution)/shard_map/ppermute | solution.py:18
  291.1 7.6 %collective-permute-start.38 = (f32[3,64,256]{2,1,0:T(8,128)S(1)}, f32[3,64,256]{2,1,0:T(8,128)S(1)}, u32[]{:S(2)}, u32[]{:S(2)}) collective-permute-start(f32[3,64,256]{2,1,0:T(8,128)S(1)} %pad_maximum_fusion.12), channel_id=1, source_target_pairs={{0,1},{1,2},{2,3},{3,4},{4,5},{5,6},{6,7},{7,8},{8,9},{9,10},{10,1... | collective-permute-start | bytes 589832 | tf_op jit(solution)/shard_map/ppermute | solution.py:18
  298.7 9.7 %collective-permute-start.39 = (f32[3,64,256]{2,1,0:T(8,128)S(1)}, f32[3,64,256]{2,1,0:T(8,128)S(1)}, u32[]{:S(2)}, u32[]{:S(2)}) collective-permute-start(f32[3,64,256]{2,1,0:T(8,128)S(1)} %pad_maximum_fusion.13), channel_id=1, source_target_pairs={{1,0},{2,1},{3,2},{4,3},{5,4},{6,5},{7,6},{8,7},{9,8},{10,9},{11,1... | collective-permute-start | bytes 589832 | tf_op jit(solution)/shard_map/ppermute | solution.py:18
  (22 other events, 74.4 us)
where the time goes:
time: 319 us; the launch traced here: 318 us
  waiting for transfers between devices  136 us (43%)
  starting transfers between devices  86.4 us (27%)
  other arithmetic  48.2 us (15%)
  local copies, waits for them, and re-layouts  27.7 us (9%)
  matrix products  17.5 us (5%)
    ppermute x28, waiting for transfers between devices, shifted(): return lax.ppermute(shard, axis, pairs)  120 us
    ppermute x28, starting transfers between devices, shifted(): return lax.ppermute(shard, axis, pairs)  68.5 us
    scatter-add x7, other arithmetic, assemble(): vector.at[row_map.reshape(-1)].add(incoming.reshape(-1, vector.shape[-1]))  29 us
    ppermute x12, starting transfers between devices, from_behind(): return lax.ppermute(block, axis, route)  17.8 us
    ppermute x12, waiting for transfers between devices, from_behind(): return lax.ppermute(block, axis, route)  15.7 us
    gather x7, local copies, waits for them, and re-layouts, assemble(): outgoing = vector[row_map] * valid[:, :, None]  14.8 us
    dot_general x3, matrix products, body(): jnp.dot(schur_block, direction.astype(jnp.bfloat16), preferred_element_ty...  8.16 us
  transfers between devices with their start and end apart: 40, of which 36 were waited for; matrix products, arithmetic and copies ran while one was open for 3% of the time, Pallas kernels for 0%

commit v1 on v0

v1 whole, which is shorter than its diff:
```python
from functools import partial

import jax
import jax.numpy as jnp
from jax import lax
from jax.experimental import pallas as pl
from jax.experimental.pallas import tpu as pltpu
from jax.sharding import PartitionSpec as P

MROW = 64
TILE = 8
ITERS = 3
centre = 1.6
spread = 1.4

SIDES = ((1, 1), (1, 0), (1, -1), (-1, 1), (-1, 0), (-1, -1), (0, 1), (0, -1))

VMEM = pl.BlockSpec(memory_space=pltpu.VMEM)
SMEM = pl.BlockSpec(memory_space=pltpu.SMEM)
F32 = jnp.float32
BF16 = jnp.bfloat16
HIGH = lax.Precision.HIGHEST


def swap(x, axis, side, wrap=False):
    n = lax.axis_size(axis)
    if side == 0:
        pairs = [(i, i ^ 1) for i in range(n)]
    else:
        pairs = [(i, ((i + 1) ^ 1) - 1) for i in range(n)]
        if wrap:
            pairs = [(i, p % n) for i, p in pairs]
        else:
            pairs = [(i, p) for i, p in pairs if 0 <= p < n]
    return lax.ppermute(x, axis, pairs)


def groups_of(ids, counts):
    alpha = 1 - 2 * lax.rem(ids[0], 2)
    gamma = 1 - 2 * lax.rem(ids[1], 2)
    size = [counts[d] for d in range(8)]
    out = []
    for s, t in SIDES:
        raw = 3 * (s * alpha + 1) + (t * gamma + 1)
        d = jnp.where(raw > 4, raw - 1, raw)
        start = jnp.int32(0)
        for e in range(8):
            start = start + jnp.where(e < d, size[e], 0)
        out.append((start, counts[d]))
    total = size[0]
    for e in range(1, 8):
        total = total + size[e]
    return out, total


def to_sorted(order):
    n = order.shape[1]
    column = jnp.transpose(jnp.broadcast_to(order, (128, n)))[:, :1]
    return (lax.broadcasted_iota(jnp.int32, (n, n), 1) == column).astype(F32).astype(BF16)


def from_sorted(order):
    n = order.shape[1]
    return (lax.broadcasted_iota(jnp.int32, (n, n), 0) == order).astype(F32).astype(BF16)


def moved(onehot, x):
    high = x.astype(BF16)
    rest = x - high.astype(F32)
    mid = rest.astype(BF16)
    low = (rest - mid.astype(F32)).astype(BF16)
    dot = partial(jnp.dot, onehot, preferred_element_type=F32)
    return dot(high) + dot(mid) + dot(low)


def window(start):
    skip = lax.rem(start, TILE)
    return pl.ds(pl.multiple_of(start - skip, TILE), MROW + TILE), skip


def emit(buf, groups, a_ref, b_ref, c_ref, d_ref):
    for k, (start, _) in enumerate(groups):
        place, skip = window(start)
        rows = pltpu.roll(buf[place, :], lax.rem(MROW + TILE - skip, MROW + TILE), 0)[0:MROW, :]
        if k < 3:
            a_ref[k * MROW:(k + 1) * MROW, :] = rows
        elif k < 6:
            b_ref[(k - 3) * MROW:(k - 2) * MROW, :] = rows
        elif k == 6:
            c_ref[...] = rows
        else:
            d_ref[...] = rows


def absorb(buf, groups, ra, rb, rc, rd):
    pieces = (rc[0:64, :], ra[64:128, :], rd[0:64, :], rc[128:192, :], rb[64:128, :], rd[128:192, :],
              rc[64:128, :], rd[64:128, :])
    at = lax.broadcasted_iota(jnp.int32, (MROW, 1), 0)
    tail = jnp.zeros((TILE, buf.shape[1]), F32)
    for (start, count), piece in zip(groups, pieces):
        place, skip = window(start)
        piece = jnp.concatenate([jnp.where(at < count, piece, 0.0), tail], axis=0)
        buf[place, :] = buf[place, :] + pltpu.roll(piece, skip, 0)


def fill(buf, x):
    n = x.shape[0]
    buf[0:n, :] = x
    buf[n:n + MROW + TILE, :] = jnp.zeros((MROW + TILE, x.shape[1]), F32)


def weights(n, total):
    return jnp.where(lax.broadcasted_iota(jnp.int32, (n, 1), 0) < total, 0.5, 1.0).astype(F32)


def chooser(ids, blocks, peers, size):
    alpha = 1 - 2 * lax.rem(ids[0], 2)
    n = blocks.shape[1]
    rows = lax.broadcasted_iota(jnp.int32, (size, n), 0)
    parts = []
    for shift in (0, 1, -1):
        want = lax.rem(ids[0] + shift * alpha + peers, peers) * size
        parts.append((blocks - want == rows).astype(F32))
    return jnp.concatenate(parts, axis=0)


def k_first(ids, counts, order, source, inverse, sorted_ref, a_ref, b_ref, c_ref, d_ref, buf):
    groups, _ = groups_of(ids, counts)
    x = moved(to_sorted(order[...]), source[...])
    sorted_ref[...] = x
    fill(buf, x)
    emit(buf, groups, a_ref, b_ref, c_ref, d_ref)
    n = inverse.shape[0]
    b_ref[3 * MROW:3 * MROW + n, :] = jnp.zeros((n, b_ref.shape[1]), F32)
    b_ref[3 * MROW:3 * MROW + n, 0:n] = inverse[...]


def k_sort(order, local, schur, basis, local_ref, schur_ref, basis_ref, onehot):
    onehot[...] = to_sorted(order[...])
    n = local.shape[0]
    step = 256
    dot = partial(lax.dot_general, preferred_element_type=F32)
    basis_ref[...] = dot(onehot[...], basis[...], (((1,), (0,)), ((), ()))).astype(BF16)
    for at in range(0, n, step):
        rows = onehot[at:at + step, :]
        for src, dst in ((local, local_ref), (schur, schur_ref)):
            half = dot(rows, src[...], (((1,), (0,)), ((), ()))).astype(BF16)
            dst[at:at + step, :] = dot(half, onehot[...], (((1,), (1,)), ((), ()))).astype(BF16)


def k_residual(first, peers, size, ids, counts, blocks, basis, old, product, ra, rb, rc, rd,
               res_ref, scaled_ref, give_ref, keep_ref, buf):
    groups, total = groups_of(ids, counts)
    if first:
        fill(buf, old[...])
    else:
        fill(buf, product[...])
    absorb(buf, groups, ra, rb, rc, rd)
    n = old.shape[0]
    res = buf[0:n, :] if first else old[...] - buf[0:n, :]
    res_ref[...] = res
    scaled = (weights(n, total) * res).astype(BF16)
    scaled_ref[...] = scaled
    primal = lax.dot_general(basis[...], scaled, (((0,), (0,)), ((), ())), preferred_element_type=F32)
    select = chooser(ids, blocks[...], peers, size)
    spread_out = jnp.dot(select, primal, precision=HIGH, preferred_element_type=F32)
    give_ref[...] = spread_out[size:2 * size, :]
    keep_ref[0:size, :] = spread_out[0:size, :]
    keep_ref[size:2 * size, :] = spread_out[2 * size:3 * size, :]


def k_local(local, scaled, out):
    out[...] = jnp.dot(local[...], scaled[...], preferred_element_type=F32)


def k_coarse(size, inv, inv_b, mine, theirs, own_ref, b_ref):
    dot = partial(jnp.dot, precision=HIGH, preferred_element_type=F32)
    own_ref[...] = dot(inv[...], mine[0:size, :] + theirs[size:2 * size, :])
    b_ref[...] = dot(inv_b[:, 0:size], theirs[0:size, :] + mine[size:2 * size, :])


def k_update(peers, size, ids, counts, blocks, basis, local, sol, sol_a, sol_b,
             up_ref, a_ref, b_ref, c_ref, d_ref, buf):
    groups, total = groups_of(ids, counts)
    select = chooser(ids, blocks[...], peers, size)
    stack = jnp.concatenate([sol[...], sol_a[...], sol_b[...]], axis=0)
    picked = lax.dot_general(select, stack, (((0,), (0,)), ((), ())), precision=HIGH, preferred_element_type=F32)
    n = local.shape[0]
    up = local[...] + jnp.dot(basis[...], picked.astype(BF16), preferred_element_type=F32)
    up = weights(n, total) * up
    up_ref[...] = up
    fill(buf, up)
    emit(buf, groups, a_ref, b_ref, c_ref, d_ref)


def k_apply(keep, gain, ids, counts, schur, up, old, ra, rb, rc, rd, dir_ref, v_ref, a_ref, b_ref, c_ref, d_ref, buf):
    groups, _ = groups_of(ids, counts)
    fill(buf, up[...])
    absorb(buf, groups, ra, rb, rc, rd)
    n = up.shape[0]
    direction = gain * buf[0:n, :]
    if keep is not None:
        direction = keep * old[...] + direction
    dir_ref[...] = direction
    v = jnp.dot(schur[...], direction.astype(BF16), preferred_element_type=F32)
    v_ref[...] = v
    buf[0:n, :] = v
    emit(buf, groups, a_ref, b_ref, c_ref, d_ref)


def k_solution(order, one, two, three, out):
    out[...] = moved(from_sorted(order[...]), one[...] + two[...] + three[...])


def k_final(ids, counts, order, old, product, ra, rb, rc, rd, out, buf):
    groups, _ = groups_of(ids, counts)
    fill(buf, product[...])
    absorb(buf, groups, ra, rb, rc, rd)
    n = old.shape[0]
    out[...] = moved(from_sorted(order[...]), old[...] - buf[0:n, :])


def call(kernel, ins, outs, flops, scratch=(), scalars=0):
    moved_bytes = sum(x.size * x.dtype.itemsize for x in ins)
    moved_bytes += sum(x.size * x.dtype.itemsize for x in outs)
    return pl.pallas_call(
        kernel,
        out_shape=tuple(outs),
        in_specs=[SMEM] * scalars + [VMEM] * (len(ins) - scalars),
        out_specs=tuple([VMEM] * len(outs)),
        scratch_shapes=list(scratch),
        compiler_params=pltpu.CompilerParams(vmem_limit_bytes=28 * 1024 * 1024),
        cost_estimate=pl.CostEstimate(flops=flops, bytes_accessed=moved_bytes, transcendentals=0),
    )(*ins)


def exchange(a, b, c, d, wrap=False):
    rb = swap(b, "sx", 1, wrap)
    ra = swap(a, "sx", 0)
    to_d = jnp.concatenate([ra[128:192], d, rb[128:192]], axis=0)
    to_c = jnp.concatenate([ra[0:64], c, rb[0:64]], axis=0)
    rd = swap(to_d, "sy", 1)
    rc = swap(to_c, "sy", 0)
    return ra, rb, rc, rd


def body(local_source, schur, local_inverse, primal_basis, coarse_inverse, primal_map, shared_count, row_order):
    source = local_source[0, 0]
    n, cols = source.shape
    inv = coarse_inverse[0, 0]
    size = inv.shape[0]
    modes = primal_basis.shape[3]
    peers = lax.axis_size("sx")
    ids = jnp.stack([lax.axis_index("sx"), lax.axis_index("sy")]).astype(jnp.int32)
    counts = shared_count[0, 0]
    order = row_order[0]
    blocks = primal_map[0]

    f32 = lambda *shape: jax.ShapeDtypeStruct(shape, F32)
    b16 = lambda *shape: jax.ShapeDtypeStruct(shape, BF16)
    full = f32(n, cols)
    sent = [f32(3 * MROW, cols), f32(3 * MROW, cols), f32(MROW, cols), f32(MROW, cols)]
    buf = [pltpu.VMEM((n + MROW + TILE, cols), F32)]
    big = 2 * n * n * cols

    src, *out = call(
        k_first,
        (ids, counts, order, source, inv),
        [full, sent[0], f32(3 * MROW + size, cols), sent[2], sent[3]],
        3 * big, buf, 2,
    )
    a_s, s_s, basis = call(
        k_sort,
        (order, local_inverse[0, 0], schur[0, 0], primal_basis[0, 0]),
        [b16(n, n), b16(n, n), b16(n, modes)],
        8 * n * n * n, [pltpu.VMEM((n, n), BF16)],
    )
    got = exchange(*out, wrap=True)
    inv_b = got[1][3 * MROW:3 * MROW + size]

    res, product, direction = src, src, src
    directions = []
    sigma = centre / spread
    rho = 1.0 / sigma
    for step in range(ITERS):
        res, scaled, give, kept = call(
            partial(k_residual, step == 0, peers, size),
            (ids, counts, blocks, basis, res, product, *got),
            [full, b16(n, cols), f32(size, cols), f32(2 * size, cols)],
            2 * n * modes * cols, buf, 2,
        )
        from_a = swap(give, "sx", 0)
        mine = jnp.concatenate([kept[0:size] + from_a, kept[size:2 * size]], axis=0)
        theirs = swap(mine, "sx", 1, True)
        local, = call(k_local, (a_s, scaled), [full], big)
        sol, sol_b = call(
            partial(k_coarse, size), (inv, inv_b, mine, theirs), [f32(size, cols), f32(size, cols)],
            4 * size * size * cols,
        )
        sol_a = swap(sol, "sx", 0)
        up, *out = call(
            partial(k_update, peers, size),
            (ids, counts, blocks, basis, local, sol, sol_a, sol_b),
            [full] + sent, 2 * n * modes * cols, buf, 2,
        )
        got = exchange(*out)
        if step == 0:
            keep, gain = None, 1.0 / centre
        else:
            rho_new = 1.0 / (2.0 * sigma - rho)
            keep, gain = rho_new * rho, 2.0 * rho_new / spread
            rho = rho_new
        direction, product, *out = call(
            partial(k_apply, keep, gain),
            (ids, counts, s_s, up, direction, *got),
            [full, full] + sent, big, buf, 2,
        )
        directions.append(direction)
        got = exchange(*out)
    total, = call(k_solution, (order, *directions), [full], 3 * big)
    residual, = call(k_final, (ids, counts, order, res, product, *got), [full], 3 * big, buf, 2)
    return total[None, None], residual[None, None]


def solution(mesh):
    four = P("sx", "sy", None, None)
    three = P("sx", "sy", None)
    return jax.shard_map(
        body,
        mesh=mesh,
        in_specs=(four, four, four, four, four, three, three, three),
        out_specs=(four, four),
        check_vma=False,
    )
```

time: 319 us -> 222 us (0.70)
  the two profiles are of different devices: /device:TPU:134 before, /device:TPU:249 now
where the time goes in v1:
time: 222 us; the launch traced here: 221 us
  starting transfers between devices  112 us (50%)
  waiting for transfers between devices  77.1 us (35%)
  Pallas kernels  25.8 us (12%)
  local copies, waits for them, and re-layouts  4.79 us (2%)
    ppermute x37, starting transfers between devices, swap(): return lax.ppermute(x, axis, pairs)  112 us
    ppermute x37, waiting for transfers between devices, swap(): return lax.ppermute(x, axis, pairs)  77.1 us
    pallas_call x19, Pallas kernels, call(): pl.pallas_call(kernel, out_shape=tuple(outs), in_specs=[SMEM] * scalars +...  25.8 us
    unnamed x23, local copies, waits for them, and re-layouts  4.65 us
  transfers between devices with their start and end apart: 37, of which 29 were waited for; matrix products, arithmetic and copies ran while one was open for 0% of the time, Pallas kernels for 4%

profile of v1, /device:TPU:249, one launch (start us, length us, event | category | flops | bytes accessed | tf_op | source)
XLA Modules:
  0.0 221.1 jit_solution(10946948602862917724)
XLA Ops:
  6.0 2.7 %collective-permute-start = (f32[192,256]{1,0:T(8,128)S(1)}, f32[192,256]{1,0:T(8,128)S(1)}, u32[]{:S(2)}, u32[]{:S(2)}) collective-permute-start(f32[192,256]{1,0:T(8,128)S(1)} %get-tuple-element.65), channel_id=1, source_target_pairs={{0,16},{16,0},{32,48},{48,32},{64,80},{80,64},{96,112},{112,96},{1... | collective-permute-start | bytes 589832 | tf_op jit(solution)/shard_map/ppermute | solution.py:35
  8.7 4.7 %collective-permute-start.1 = (f32[224,256]{1,0:T(8,128)S(1)}, f32[224,256]{1,0:T(8,128)S(1)}, u32[]{:S(2)}, u32[]{:S(2)}) collective-permute-start(f32[224,256]{1,0:T(8,128)S(1)} %get-tuple-element.66), channel_id=1, source_target_pairs={{0,496},{16,32},{32,16},{48,64},{64,48},{80,96},{96,80},{112,128},... | collective-permute-start | bytes 688136 | tf_op jit(solution)/shard_map/ppermute | solution.py:35
  13.6 3.7 %collective-permute-done.1.rb = f32[224,256]{1,0:T(8,128)S(1)} collective-permute-done((f32[224,256]{1,0:T(8,128)S(1)}, f32[224,256]{1,0:T(8,128)S(1)}, u32[]{:S(2)}, u32[]{:S(2)}) %collective-permute-start.1) | collective-permute-done | bytes 229408 | tf_op jit(solution)/shard_map/ppermute | solution.py:35
  17.3 3.1 %collective-permute-start.2 = (f32[192,256]{1,0:T(8,128)S(1)}, f32[192,256]{1,0:T(8,128)S(1)}, u32[]{:S(2)}, u32[]{:S(2)}) collective-permute-start(f32[192,256]{1,0:T(8,128)S(1)} %pad_maximum_fusion), channel_id=1, source_target_pairs={{0,1},{1,0},{2,3},{3,2},{4,5},{5,4},{6,7},{7,6},{8,9},{9,8},{10,11... | collective-permute-start | bytes 589832 | tf_op jit(solution)/shard_map/ppermute | solution.py:35
  20.4 3.9 %collective-permute-start.3 = (f32[192,256]{1,0:T(8,128)S(1)}, f32[192,256]{1,0:T(8,128)S(1)}, u32[]{:S(2)}, u32[]{:S(2)}) collective-permute-start(f32[192,256]{1,0:T(8,128)S(1)} %pad_maximum_fusion.1), channel_id=1, source_target_pairs={{1,2},{2,1},{3,4},{4,3},{5,6},{6,5},{7,8},{8,7},{9,10},{10,9},{11,... | collective-permute-start | bytes 589832 | tf_op jit(solution)/shard_map/ppermute | solution.py:35
  25.7 4.5 %shard_map.95 = (bf16[768,768]{1,0:T(8,128)(2,1)S(1)}, bf16[768,768]{1,0:T(8,128)(2,1)S(1)}, bf16[768,32]{1,0:T(8,128)(2,1)S(1)}) custom-call(s32[1,768]{1,0:T(1,128)S(1)} %bitcast.38, bf16[768,768]{1,0:T(8,128)(2,1)S(1)} %bitcast.34, bf16[768,768]{1,0:T(8,128)(2,1)S(1)} %bitcast.35, bf16[768,32]{1,0:T(8,128)(2,1)S(1)} %bitcast.12), custom_call_target="tpu_custom_call" | custom-call | flops 3623878656 | bytes 4819968 | tf_op jit(solution)/shard_map/pallas_call | solution.py:226
  32.0 2.2 %collective-permute-start.4 = (f32[32,256]{1,0:T(8,128)S(1)}, f32[32,256]{1,0:T(8,128)S(1)}, u32[]{:S(2)}, u32[]{:S(2)}) collective-permute-start(f32[32,256]{1,0:T(8,128)S(1)} %get-tuple-element.71), channel_id=1, source_target_pairs={{0,16},{16,0},{32,48},{48,32},{64,80},{80,64},{96,112},{112,96},{1... | collective-permute-start | bytes 98312 | tf_op jit(solution)/shard_map/ppermute | solution.py:35
  35.1 4.9 %collective-permute-start.5 = (f32[64,256]{1,0:T(8,128)S(1)}, f32[64,256]{1,0:T(8,128)S(1)}, u32[]{:S(2)}, u32[]{:S(2)}) collective-permute-start(f32[64,256]{1,0:T(8,128)S(1)} %pad_maximum_fusion.14.mine), channel_id=1, source_target_pairs={{0,496},{16,32},{32,16},{48,64},{64,48},{80,96},{96,80},{112,128},... | collective-permute-start | bytes 196616 | tf_op jit(solution)/shard_map/ppermute | solution.py:35
  46.5 2.1 collective-permute-start.7
  48.6 4.8 %collective-permute-start.8 = (f32[192,256]{1,0:T(8,128)S(1)}, f32[192,256]{1,0:T(8,128)S(1)}, u32[]{:S(2)}, u32[]{:S(2)}) collective-permute-start(f32[192,256]{1,0:T(8,128)S(1)} %get-tuple-element.76), channel_id=1, source_target_pairs={{16,32},{32,16},{48,64},{64,48},{80,96},{96,80},{112,128},{128,112... | collective-permute-start | bytes 589832 | tf_op jit(solution)/shard_map/ppermute | solution.py:35
  53.5 3.3 %collective-permute-done.8.rb = f32[192,256]{1,0:T(8,128)S(1)} collective-permute-done((f32[192,256]{1,0:T(8,128)S(1)}, f32[192,256]{1,0:T(8,128)S(1)}, u32[]{:S(2)}, u32[]{:S(2)}) %collective-permute-start.8) | collective-permute-done | bytes 196640 | tf_op jit(solution)/shard_map/ppermute | solution.py:35
  58.9 3.8 %collective-permute-start.10 = (f32[192,256]{1,0:T(8,128)S(1)}, f32[192,256]{1,0:T(8,128)S(1)}, u32[]{:S(2)}, u32[]{:S(2)}) collective-permute-start(f32[192,256]{1,0:T(8,128)S(1)} %pad_maximum_fusion.3), channel_id=1, source_target_pairs={{1,2},{2,1},{3,4},{4,3},{5,6},{6,5},{7,8},{8,7},{9,10},{10,9},{11,... | collective-permute-start | bytes 589832 | tf_op jit(solution)/shard_map/ppermute | solution.py:35
  62.7 2.3 %collective-permute-done.9.rc = f32[192,256]{1,0:T(8,128)S(1)} collective-permute-done((f32[192,256]{1,0:T(8,128)S(1)}, f32[192,256]{1,0:T(8,128)S(1)}, u32[]{:S(2)}, u32[]{:S(2)}) %collective-permute-start.9) | collective-permute-done | bytes 196640 | tf_op jit(solution)/shard_map/ppermute | solution.py:35
  64.9 4.6 %collective-permute-done.10.rd = f32[192,256]{1,0:T(8,128)S(1)} collective-permute-done((f32[192,256]{1,0:T(8,128)S(1)}, f32[192,256]{1,0:T(8,128)S(1)}, u32[]{:S(2)}, u32[]{:S(2)}) %collective-permute-start.10) | collective-permute-done | bytes 196640 | tf_op jit(solution)/shard_map/ppermute | solution.py:35
  71.0 2.3 %collective-permute-start.11 = (f32[192,256]{1,0:T(8,128)S(1)}, f32[192,256]{1,0:T(8,128)S(1)}, u32[]{:S(2)}, u32[]{:S(2)}) collective-permute-start(f32[192,256]{1,0:T(8,128)S(1)} %get-tuple-element.82), channel_id=1, source_target_pairs={{0,16},{16,0},{32,48},{48,32},{64,80},{80,64},{96,112},{112,96},{1... | collective-permute-start | bytes 589832 | tf_op jit(solution)/shard_map/ppermute | solution.py:35
  73.3 4.0 %collective-permute-start.12 = (f32[192,256]{1,0:T(8,128)S(1)}, f32[192,256]{1,0:T(8,128)S(1)}, u32[]{:S(2)}, u32[]{:S(2)}) collective-permute-start(f32[192,256]{1,0:T(8,128)S(1)} %get-tuple-element.83), channel_id=1, source_target_pairs={{16,32},{32,16},{48,64},{64,48},{80,96},{96,80},{112,128},{128,112... | collective-permute-start | bytes 589832 | tf_op jit(solution)/shard_map/ppermute | solution.py:35
  77.4 4.1 %collective-permute-done.12.rb = f32[192,256]{1,0:T(8,128)S(1)} collective-permute-done((f32[192,256]{1,0:T(8,128)S(1)}, f32[192,256]{1,0:T(8,128)S(1)}, u32[]{:S(2)}, u32[]{:S(2)}) %collective-permute-start.12) | collective-permute-done | bytes 196640 | tf_op jit(solution)/shard_map/ppermute | solution.py:35
  83.5 3.3 %collective-permute-start.14 = (f32[192,256]{1,0:T(8,128)S(1)}, f32[192,256]{1,0:T(8,128)S(1)}, u32[]{:S(2)}, u32[]{:S(2)}) collective-permute-start(f32[192,256]{1,0:T(8,128)S(1)} %pad_maximum_fusion.5), channel_id=1, source_target_pairs={{1,2},{2,1},{3,4},{4,3},{5,6},{6,5},{7,8},{8,7},{9,10},{10,9},{11,... | collective-permute-start | bytes 589832 | tf_op jit(solution)/shard_map/ppermute | solution.py:35
  86.8 2.9 %collective-permute-done.13.rc = f32[192,256]{1,0:T(8,128)S(1)} collective-permute-done((f32[192,256]{1,0:T(8,128)S(1)}, f32[192,256]{1,0:T(8,128)S(1)}, u32[]{:S(2)}, u32[]{:S(2)}) %collective-permute-start.13) | collective-permute-done | bytes 196640 | tf_op jit(solution)/shard_map/ppermute | solution.py:35
  89.7 3.8 %collective-permute-done.14.rd = f32[192,256]{1,0:T(8,128)S(1)} collective-permute-done((f32[192,256]{1,0:T(8,128)S(1)}, f32[192,256]{1,0:T(8,128)S(1)}, u32[]{:S(2)}, u32[]{:S(2)}) %collective-permute-start.14) | collective-permute-done | bytes 196640 | tf_op jit(solution)/shard_map/ppermute | solution.py:35
  98.0 4.4 %collective-permute-start.16 = (f32[64,256]{1,0:T(8,128)S(1)}, f32[64,256]{1,0:T(8,128)S(1)}, u32[]{:S(2)}, u32[]{:S(2)}) collective-permute-start(f32[64,256]{1,0:T(8,128)S(1)} %pad_maximum_fusion.15.mine), channel_id=1, source_target_pairs={{0,496},{16,32},{32,16},{48,64},{64,48},{80,96},{96,80},{112,128},... | collective-permute-start | bytes 196616 | tf_op jit(solution)/shard_map/ppermute | solution.py:35
  102.4 2.3 %collective-permute-done.16.theirs = f32[64,256]{1,0:T(8,128)S(1)} collective-permute-done((f32[64,256]{1,0:T(8,128)S(1)}, f32[64,256]{1,0:T(8,128)S(1)}, u32[]{:S(2)}, u32[]{:S(2)}) %collective-permute-start.16) | collective-permute-done | bytes 65568 | tf_op jit(solution)/shard_map/ppermute | solution.py:35
  109.4 2.1 collective-permute-start.18
  111.4 4.4 %collective-permute-start.19 = (f32[192,256]{1,0:T(8,128)S(1)}, f32[192,256]{1,0:T(8,128)S(1)}, u32[]{:S(2)}, u32[]{:S(2)}) collective-permute-start(f32[192,256]{1,0:T(8,128)S(1)} %get-tuple-element.93), channel_id=1, source_target_pairs={{16,32},{32,16},{48,64},{64,48},{80,96},{96,80},{112,128},{128,112... | collective-permute-start | bytes 589832 | tf_op jit(solution)/shard_map/ppermute | solution.py:35
  115.9 3.7 %collective-permute-done.19.rb = f32[192,256]{1,0:T(8,128)S(1)} collective-permute-done((f32[192,256]{1,0:T(8,128)S(1)}, f32[192,256]{1,0:T(8,128)S(1)}, u32[]{:S(2)}, u32[]{:S(2)}) %collective-permute-start.19) | collective-permute-done | bytes 196640 | tf_op jit(solution)/shard_map/ppermute | solution.py:35
  121.6 3.6 %collective-permute-start.21 = (f32[192,256]{1,0:T(8,128)S(1)}, f32[192,256]{1,0:T(8,128)S(1)}, u32[]{:S(2)}, u32[]{:S(2)}) collective-permute-start(f32[192,256]{1,0:T(8,128)S(1)} %pad_maximum_fusion.7), channel_id=1, source_target_pairs={{1,2},{2,1},{3,4},{4,3},{5,6},{6,5},{7,8},{8,7},{9,10},{10,9},{11,... | collective-permute-start | bytes 589832 | tf_op jit(solution)/shard_map/ppermute | solution.py:35
  125.2 2.9 %collective-permute-done.20.rc = f32[192,256]{1,0:T(8,128)S(1)} collective-permute-done((f32[192,256]{1,0:T(8,128)S(1)}, f32[192,256]{1,0:T(8,128)S(1)}, u32[]{:S(2)}, u32[]{:S(2)}) %collective-permute-start.20) | collective-permute-done | bytes 196640 | tf_op jit(solution)/shard_map/ppermute | solution.py:35
  128.1 3.8 %collective-permute-done.21.rd = f32[192,256]{1,0:T(8,128)S(1)} collective-permute-done((f32[192,256]{1,0:T(8,128)S(1)}, f32[192,256]{1,0:T(8,128)S(1)}, u32[]{:S(2)}, u32[]{:S(2)}) %collective-permute-start.21) | collective-permute-done | bytes 196640 | tf_op jit(solution)/shard_map/ppermute | solution.py:35
  133.3 2.3 %collective-permute-start.22 = (f32[192,256]{1,0:T(8,128)S(1)}, f32[192,256]{1,0:T(8,128)S(1)}, u32[]{:S(2)}, u32[]{:S(2)}) collective-permute-start(f32[192,256]{1,0:T(8,128)S(1)} %get-tuple-element.99), channel_id=1, source_target_pairs={{0,16},{16,0},{32,48},{48,32},{64,80},{80,64},{96,112},{112,96},{1... | collective-permute-start | bytes 589832 | tf_op jit(solution)/shard_map/ppermute | solution.py:35
  135.6 4.1 %collective-permute-start.23 = (f32[192,256]{1,0:T(8,128)S(1)}, f32[192,256]{1,0:T(8,128)S(1)}, u32[]{:S(2)}, u32[]{:S(2)}) collective-permute-start(f32[192,256]{1,0:T(8,128)S(1)} %get-tuple-element.100), channel_id=1, source_target_pairs={{16,32},{32,16},{48,64},{64,48},{80,96},{96,80},{112,128},{128,112... | collective-permute-start | bytes 589832 | tf_op jit(solution)/shard_map/ppermute | solution.py:35
  139.8 4.0 %collective-permute-done.23.rb = f32[192,256]{1,0:T(8,128)S(1)} collective-permute-done((f32[192,256]{1,0:T(8,128)S(1)}, f32[192,256]{1,0:T(8,128)S(1)}, u32[]{:S(2)}, u32[]{:S(2)}) %collective-permute-start.23) | collective-permute-done | bytes 196640 | tf_op jit(solution)/shard_map/ppermute | solution.py:35
  145.8 3.4 %collective-permute-start.25 = (f32[192,256]{1,0:T(8,128)S(1)}, f32[192,256]{1,0:T(8,128)S(1)}, u32[]{:S(2)}, u32[]{:S(2)}) collective-permute-start(f32[192,256]{1,0:T(8,128)S(1)} %pad_maximum_fusion.9), channel_id=1, source_target_pairs={{1,2},{2,1},{3,4},{4,3},{5,6},{6,5},{7,8},{8,7},{9,10},{10,9},{11,... | collective-permute-start | bytes 589832 | tf_op jit(solution)/shard_map/ppermute | solution.py:35
  149.2 2.8 %collective-permute-done.24.rc = f32[192,256]{1,0:T(8,128)S(1)} collective-permute-done((f32[192,256]{1,0:T(8,128)S(1)}, f32[192,256]{1,0:T(8,128)S(1)}, u32[]{:S(2)}, u32[]{:S(2)}) %collective-permute-start.24) | collective-permute-done | bytes 196640 | tf_op jit(solution)/shard_map/ppermute | solution.py:35
  152.1 3.8 %collective-permute-done.25.rd = f32[192,256]{1,0:T(8,128)S(1)} collective-permute-done((f32[192,256]{1,0:T(8,128)S(1)}, f32[192,256]{1,0:T(8,128)S(1)}, u32[]{:S(2)}, u32[]{:S(2)}) %collective-permute-start.25) | collective-permute-done | bytes 196640 | tf_op jit(solution)/shard_map/ppermute | solution.py:35
  157.2 2.1 collective-permute-start.26
  160.4 4.4 %collective-permute-start.27 = (f32[64,256]{1,0:T(8,128)S(1)}, f32[64,256]{1,0:T(8,128)S(1)}, u32[]{:S(2)}, u32[]{:S(2)}) collective-permute-start(f32[64,256]{1,0:T(8,128)S(1)} %pad_maximum_fusion.16.mine), channel_id=1, source_target_pairs={{0,496},{16,32},{32,16},{48,64},{64,48},{80,96},{96,80},{112,128},... | collective-permute-start | bytes 196616 | tf_op jit(solution)/shard_map/ppermute | solution.py:35
  164.8 2.4 %collective-permute-done.27.theirs = f32[64,256]{1,0:T(8,128)S(1)} collective-permute-done((f32[64,256]{1,0:T(8,128)S(1)}, f32[64,256]{1,0:T(8,128)S(1)}, u32[]{:S(2)}, u32[]{:S(2)}) %collective-permute-start.27) | collective-permute-done | bytes 65568 | tf_op jit(solution)/shard_map/ppermute | solution.py:35
  173.8 4.4 %collective-permute-start.30 = (f32[192,256]{1,0:T(8,128)S(1)}, f32[192,256]{1,0:T(8,128)S(1)}, u32[]{:S(2)}, u32[]{:S(2)}) collective-permute-start(f32[192,256]{1,0:T(8,128)S(1)} %get-tuple-element.110), channel_id=1, source_target_pairs={{16,32},{32,16},{48,64},{64,48},{80,96},{96,80},{112,128},{128,112... | collective-permute-start | bytes 589832 | tf_op jit(solution)/shard_map/ppermute | solution.py:35
  178.3 3.7 %collective-permute-done.30.rb = f32[192,256]{1,0:T(8,128)S(1)} collective-permute-done((f32[192,256]{1,0:T(8,128)S(1)}, f32[192,256]{1,0:T(8,128)S(1)}, u32[]{:S(2)}, u32[]{:S(2)}) %collective-permute-start.30) | collective-permute-done | bytes 196640 | tf_op jit(solution)/shard_map/ppermute | solution.py:35
  184.0 3.4 %collective-permute-start.32 = (f32[192,256]{1,0:T(8,128)S(1)}, f32[192,256]{1,0:T(8,128)S(1)}, u32[]{:S(2)}, u32[]{:S(2)}) collective-permute-start(f32[192,256]{1,0:T(8,128)S(1)} %pad_maximum_fusion.11), channel_id=1, source_target_pairs={{1,2},{2,1},{3,4},{4,3},{5,6},{6,5},{7,8},{8,7},{9,10},{10,9},{11,... | collective-permute-start | bytes 589832 | tf_op jit(solution)/shard_map/ppermute | solution.py:35
  187.4 3.0 %collective-permute-done.31.rc = f32[192,256]{1,0:T(8,128)S(1)} collective-permute-done((f32[192,256]{1,0:T(8,128)S(1)}, f32[192,256]{1,0:T(8,128)S(1)}, u32[]{:S(2)}, u32[]{:S(2)}) %collective-permute-start.31) | collective-permute-done | bytes 196640 | tf_op jit(solution)/shard_map/ppermute | solution.py:35
  190.5 3.8 %collective-permute-done.32.rd = f32[192,256]{1,0:T(8,128)S(1)} collective-permute-done((f32[192,256]{1,0:T(8,128)S(1)}, f32[192,256]{1,0:T(8,128)S(1)}, u32[]{:S(2)}, u32[]{:S(2)}) %collective-permute-start.32) | collective-permute-done | bytes 196640 | tf_op jit(solution)/shard_map/ppermute | solution.py:35
  195.7 2.3 %collective-permute-start.33 = (f32[192,256]{1,0:T(8,128)S(1)}, f32[192,256]{1,0:T(8,128)S(1)}, u32[]{:S(2)}, u32[]{:S(2)}) collective-permute-start(f32[192,256]{1,0:T(8,128)S(1)} %get-tuple-element.116), channel_id=1, source_target_pairs={{0,16},{16,0},{32,48},{48,32},{64,80},{80,64},{96,112},{112,96},{1... | collective-permute-start | bytes 589832 | tf_op jit(solution)/shard_map/ppermute | solution.py:35
  198.0 4.1 %collective-permute-start.34 = (f32[192,256]{1,0:T(8,128)S(1)}, f32[192,256]{1,0:T(8,128)S(1)}, u32[]{:S(2)}, u32[]{:S(2)}) collective-permute-start(f32[192,256]{1,0:T(8,128)S(1)} %get-tuple-element.117), channel_id=1, source_target_pairs={{16,32},{32,16},{48,64},{64,48},{80,96},{96,80},{112,128},{128,112... | collective-permute-start | bytes 589832 | tf_op jit(solution)/shard_map/ppermute | solution.py:35
  202.1 4.1 %collective-permute-done.34.rb = f32[192,256]{1,0:T(8,128)S(1)} collective-permute-done((f32[192,256]{1,0:T(8,128)S(1)}, f32[192,256]{1,0:T(8,128)S(1)}, u32[]{:S(2)}, u32[]{:S(2)}) %collective-permute-start.34) | collective-permute-done | bytes 196640 | tf_op jit(solution)/shard_map/ppermute | solution.py:35
  208.2 3.4 %collective-permute-start.36 = (f32[192,256]{1,0:T(8,128)S(1)}, f32[192,256]{1,0:T(8,128)S(1)}, u32[]{:S(2)}, u32[]{:S(2)}) collective-permute-start(f32[192,256]{1,0:T(8,128)S(1)} %pad_maximum_fusion.13), channel_id=1, source_target_pairs={{1,2},{2,1},{3,4},{4,3},{5,6},{6,5},{7,8},{8,7},{9,10},{10,9},{11,... | collective-permute-start | bytes 589832 | tf_op jit(solution)/shard_map/ppermute | solution.py:35
  214.5 3.8 %collective-permute-done.36.rd = f32[192,256]{1,0:T(8,128)S(1)} collective-permute-done((f32[192,256]{1,0:T(8,128)S(1)}, f32[192,256]{1,0:T(8,128)S(1)}, u32[]{:S(2)}, u32[]{:S(2)}) %collective-permute-start.36) | collective-permute-done | bytes 196640 | tf_op jit(solution)/shard_map/ppermute | solution.py:35
  218.3 2.8 %shard_map.113 = f32[768,256]{1,0:T(8,128)} custom-call(s32[2]{0:T(128)S(1)} %pad_add_fusion.ids, s32[8]{0:T(128)S(1)} %bitcast.27, s32[1,768]{1,0:T(1,128)S(1)} %bitcast.40, f32[768,256]{1,0:T(8,128)S(1)} %get-tuple-element.114.old, f32[768,256]{1,0:T(8,128)S(1)} %get-tuple-element.115.product, f32[192,256]{1,0:T(8,128)S(1)} %collective-permute-done.33.ra, ...), custom_call_target="tpu_custom_call" | custom-call | flops 905969664 | bytes 3148840 | tf_op jit(solution)/shard_map/pallas_call | solution.py:226
  (104 shorter events, 53.1 us)
Async XLA Ops:
  0.7 0.7 copy-start
  1.4 0.7 copy-start.2
  2.1 1.1 copy-start.7
  3.2 0.7 copy-start.8
  3.9 9.5 %copy-start.10 = (bf16[1,1,768,32]{2,3,1,0:T(8,128)(2,1)S(1)}, bf16[1,1,768,32]{2,3,1,0:T(8,128)(2,1)}, u32[]{:S(2)}) copy-start(bf16[1,1,768,32]{2,3,1,0:T(8,128)(2,1)} %param.11) | copy-start | bytes 147460
  6.0 18.4 %copy-start.5 = (bf16[1,1,768,768]{3,2,1,0:T(8,128)(2,1)S(1)}, bf16[1,1,768,768]{3,2,1,0:T(8,128)(2,1)}, u32[]{:S(2)}) copy-start(bf16[1,1,768,768]{3,2,1,0:T(8,128)(2,1)} %param.10) | copy-start | bytes 3538948
  6.0 18.4 %copy-start.9 = (s32[1,1,768]{2,1,0:T(1,128)S(1)}, s32[1,1,768]{2,1,0:T(1,128)}, u32[]{:S(2)}) copy-start(s32[1,1,768]{2,1,0:T(1,128)} %param.15) | copy-start | bytes 9220
  6.0 7.6 %collective-permute-start = (f32[192,256]{1,0:T(8,128)S(1)}, f32[192,256]{1,0:T(8,128)S(1)}, u32[]{:S(2)}, u32[]{:S(2)}) collective-permute-start(f32[192,256]{1,0:T(8,128)S(1)} %get-tuple-element.65), channel_id=1, source_target_pairs={{0,16},{16,0},{32,48},{48,32},{64,80},{80,64},{96,112},{112,96},{1... | collective-permute-start | bytes 589832 | tf_op jit(solution)/shard_map/ppermute | solution.py:35
  8.7 8.6 %collective-permute-start.1 = (f32[224,256]{1,0:T(8,128)S(1)}, f32[224,256]{1,0:T(8,128)S(1)}, u32[]{:S(2)}, u32[]{:S(2)}) collective-permute-start(f32[224,256]{1,0:T(8,128)S(1)} %get-tuple-element.66), channel_id=1, source_target_pairs={{0,496},{16,32},{32,16},{48,64},{64,48},{80,96},{96,80},{112,128},... | collective-permute-start | bytes 688136 | tf_op jit(solution)/shard_map/ppermute | solution.py:35
  17.3 12.9 %collective-permute-start.2 = (f32[192,256]{1,0:T(8,128)S(1)}, f32[192,256]{1,0:T(8,128)S(1)}, u32[]{:S(2)}, u32[]{:S(2)}) collective-permute-start(f32[192,256]{1,0:T(8,128)S(1)} %pad_maximum_fusion), channel_id=1, source_target_pairs={{0,1},{1,0},{2,3},{3,2},{4,5},{5,4},{6,7},{7,6},{8,9},{9,8},{10,11... | collective-permute-start | bytes 589832 | tf_op jit(solution)/shard_map/ppermute | solution.py:35
  20.4 10.2 %collective-permute-start.3 = (f32[192,256]{1,0:T(8,128)S(1)}, f32[192,256]{1,0:T(8,128)S(1)}, u32[]{:S(2)}, u32[]{:S(2)}) collective-permute-start(f32[192,256]{1,0:T(8,128)S(1)} %pad_maximum_fusion.1), channel_id=1, source_target_pairs={{1,2},{2,1},{3,4},{4,3},{5,6},{6,5},{7,8},{8,7},{9,10},{10,9},{11,... | collective-permute-start | bytes 589832 | tf_op jit(solution)/shard_map/ppermute | solution.py:35
  24.4 1.3 copy-start.6
  25.6 5.0 %copy-start.3 = (s32[1,1,8]{2,1,0:T(1,128)S(1)}, s32[1,1,8]{2,1,0:T(1,128)}, u32[]{:S(2)}) copy-start(s32[1,1,8]{2,1,0:T(1,128)} %param.14) | copy-start | bytes 100
  25.7 5.0 %copy-start.4 = (s32[1,1,32]{2,1,0:T(1,128)S(1)}, s32[1,1,32]{2,1,0:T(1,128)}, u32[]{:S(2)}) copy-start(s32[1,1,32]{2,1,0:T(1,128)} %param.13) | copy-start | bytes 388
  30.6 11.3 %copy-start.1 = (f32[1,1,32,32]{3,2,1,0:T(8,128)S(1)}, f32[1,1,32,32]{3,2,1,0:T(8,128)}, u32[]{:S(2)}) copy-start(f32[1,1,32,32]{3,2,1,0:T(8,128)} %param.12) | copy-start | bytes 12292
  32.0 3.1 %collective-permute-start.4 = (f32[32,256]{1,0:T(8,128)S(1)}, f32[32,256]{1,0:T(8,128)S(1)}, u32[]{:S(2)}, u32[]{:S(2)}) collective-permute-start(f32[32,256]{1,0:T(8,128)S(1)} %get-tuple-element.71), channel_id=1, source_target_pairs={{0,16},{16,0},{32,48},{48,32},{64,80},{80,64},{96,112},{112,96},{1... | collective-permute-start | bytes 98312 | tf_op jit(solution)/shard_map/ppermute | solution.py:35
  35.1 6.8 %collective-permute-start.5 = (f32[64,256]{1,0:T(8,128)S(1)}, f32[64,256]{1,0:T(8,128)S(1)}, u32[]{:S(2)}, u32[]{:S(2)}) collective-permute-start(f32[64,256]{1,0:T(8,128)S(1)} %pad_maximum_fusion.14.mine), channel_id=1, source_target_pairs={{0,496},{16,32},{32,16},{48,64},{64,48},{80,96},{96,80},{112,128},... | collective-permute-start | bytes 196616 | tf_op jit(solution)/shard_map/ppermute | solution.py:35
  42.1 3.1 %collective-permute-start.6 = (f32[32,256]{1,0:T(8,128)S(1)}, f32[32,256]{1,0:T(8,128)S(1)}, u32[]{:S(2)}, u32[]{:S(2)}) collective-permute-start(f32[32,256]{1,0:T(8,128)S(1)} %get-tuple-element.72.sol), channel_id=1, source_target_pairs={{0,16},{16,0},{32,48},{48,32},{64,80},{80,64},{96,112},{112,96},{1... | collective-permute-start | bytes 98312 | tf_op jit(solution)/shard_map/ppermute | solution.py:35
  46.5 6.9 %collective-permute-start.7 = (f32[192,256]{1,0:T(8,128)S(1)}, f32[192,256]{1,0:T(8,128)S(1)}, u32[]{:S(2)}, u32[]{:S(2)}) collective-permute-start(f32[192,256]{1,0:T(8,128)S(1)} %get-tuple-element.75), channel_id=1, source_target_pairs={{0,16},{16,0},{32,48},{48,32},{64,80},{80,64},{96,112},{112,96},{1... | collective-permute-start | bytes 589832 | tf_op jit(solution)/shard_map/ppermute | solution.py:35
  48.6 8.2 %collective-permute-start.8 = (f32[192,256]{1,0:T(8,128)S(1)}, f32[192,256]{1,0:T(8,128)S(1)}, u32[]{:S(2)}, u32[]{:S(2)}) collective-permute-start(f32[192,256]{1,0:T(8,128)S(1)} %get-tuple-element.76), channel_id=1, source_target_pairs={{16,32},{32,16},{48,64},{64,48},{80,96},{96,80},{112,128},{128,112... | collective-permute-start | bytes 589832 | tf_op jit(solution)/shard_map/ppermute | solution.py:35
  56.8 8.1 %collective-permute-start.9 = (f32[192,256]{1,0:T(8,128)S(1)}, f32[192,256]{1,0:T(8,128)S(1)}, u32[]{:S(2)}, u32[]{:S(2)}) collective-permute-start(f32[192,256]{1,0:T(8,128)S(1)} %pad_maximum_fusion.2), channel_id=1, source_target_pairs={{0,1},{1,0},{2,3},{3,2},{4,5},{5,4},{6,7},{7,6},{8,9},{9,8},{10,11... | collective-permute-start | bytes 589832 | tf_op jit(solution)/shard_map/ppermute | solution.py:35
  58.9 10.7 %collective-permute-start.10 = (f32[192,256]{1,0:T(8,128)S(1)}, f32[192,256]{1,0:T(8,128)S(1)}, u32[]{:S(2)}, u32[]{:S(2)}) collective-permute-start(f32[192,256]{1,0:T(8,128)S(1)} %pad_maximum_fusion.3), channel_id=1, source_target_pairs={{1,2},{2,1},{3,4},{4,3},{5,6},{6,5},{7,8},{8,7},{9,10},{10,9},{11,... | collective-permute-start | bytes 589832 | tf_op jit(solution)/shard_map/ppermute | solution.py:35
  71.0 6.4 %collective-permute-start.11 = (f32[192,256]{1,0:T(8,128)S(1)}, f32[192,256]{1,0:T(8,128)S(1)}, u32[]{:S(2)}, u32[]{:S(2)}) collective-permute-start(f32[192,256]{1,0:T(8,128)S(1)} %get-tuple-element.82), channel_id=1, source_target_pairs={{0,16},{16,0},{32,48},{48,32},{64,80},{80,64},{96,112},{112,96},{1... | collective-permute-start | bytes 589832 | tf_op jit(solution)/shard_map/ppermute | solution.py:35
  73.3 8.2 %collective-permute-start.12 = (f32[192,256]{1,0:T(8,128)S(1)}, f32[192,256]{1,0:T(8,128)S(1)}, u32[]{:S(2)}, u32[]{:S(2)}) collective-permute-start(f32[192,256]{1,0:T(8,128)S(1)} %get-tuple-element.83), channel_id=1, source_target_pairs={{16,32},{32,16},{48,64},{64,48},{80,96},{96,80},{112,128},{128,112... | collective-permute-start | bytes 589832 | tf_op jit(solution)/shard_map/ppermute | solution.py:35
  81.6 8.2 %collective-permute-start.13 = (f32[192,256]{1,0:T(8,128)S(1)}, f32[192,256]{1,0:T(8,128)S(1)}, u32[]{:S(2)}, u32[]{:S(2)}) collective-permute-start(f32[192,256]{1,0:T(8,128)S(1)} %pad_maximum_fusion.4), channel_id=1, source_target_pairs={{0,1},{1,0},{2,3},{3,2},{4,5},{5,4},{6,7},{7,6},{8,9},{9,8},{10,11... | collective-permute-start | bytes 589832 | tf_op jit(solution)/shard_map/ppermute | solution.py:35
  83.5 10.0 %collective-permute-start.14 = (f32[192,256]{1,0:T(8,128)S(1)}, f32[192,256]{1,0:T(8,128)S(1)}, u32[]{:S(2)}, u32[]{:S(2)}) collective-permute-start(f32[192,256]{1,0:T(8,128)S(1)} %pad_maximum_fusion.5), channel_id=1, source_target_pairs={{1,2},{2,1},{3,4},{4,3},{5,6},{6,5},{7,8},{8,7},{9,10},{10,9},{11,... | collective-permute-start | bytes 589832 | tf_op jit(solution)/shard_map/ppermute | solution.py:35
  94.8 3.1 %collective-permute-start.15 = (f32[32,256]{1,0:T(8,128)S(1)}, f32[32,256]{1,0:T(8,128)S(1)}, u32[]{:S(2)}, u32[]{:S(2)}) collective-permute-start(f32[32,256]{1,0:T(8,128)S(1)} %get-tuple-element.88), channel_id=1, source_target_pairs={{0,16},{16,0},{32,48},{48,32},{64,80},{80,64},{96,112},{112,96},{1... | collective-permute-start | bytes 98312 | tf_op jit(solution)/shard_map/ppermute | solution.py:35
  98.0 6.8 %collective-permute-start.16 = (f32[64,256]{1,0:T(8,128)S(1)}, f32[64,256]{1,0:T(8,128)S(1)}, u32[]{:S(2)}, u32[]{:S(2)}) collective-permute-start(f32[64,256]{1,0:T(8,128)S(1)} %pad_maximum_fusion.15.mine), channel_id=1, source_target_pairs={{0,496},{16,32},{32,16},{48,64},{64,48},{80,96},{96,80},{112,128},... | collective-permute-start | bytes 196616 | tf_op jit(solution)/shard_map/ppermute | solution.py:35
  105.0 3.1 %collective-permute-start.17 = (f32[32,256]{1,0:T(8,128)S(1)}, f32[32,256]{1,0:T(8,128)S(1)}, u32[]{:S(2)}, u32[]{:S(2)}) collective-permute-start(f32[32,256]{1,0:T(8,128)S(1)} %get-tuple-element.89.sol), channel_id=1, source_target_pairs={{0,16},{16,0},{32,48},{48,32},{64,80},{80,64},{96,112},{112,96},{1... | collective-permute-start | bytes 98312 | tf_op jit(solution)/shard_map/ppermute | solution.py:35
  109.4 6.5 %collective-permute-start.18 = (f32[192,256]{1,0:T(8,128)S(1)}, f32[192,256]{1,0:T(8,128)S(1)}, u32[]{:S(2)}, u32[]{:S(2)}) collective-permute-start(f32[192,256]{1,0:T(8,128)S(1)} %get-tuple-element.92), channel_id=1, source_target_pairs={{0,16},{16,0},{32,48},{48,32},{64,80},{80,64},{96,112},{112,96},{1... | collective-permute-start | bytes 589832 | tf_op jit(solution)/shard_map/ppermute | solution.py:35
  111.4 8.2 %collective-permute-start.19 = (f32[192,256]{1,0:T(8,128)S(1)}, f32[192,256]{1,0:T(8,128)S(1)}, u32[]{:S(2)}, u32[]{:S(2)}) collective-permute-start(f32[192,256]{1,0:T(8,128)S(1)} %get-tuple-element.93), channel_id=1, source_target_pairs={{16,32},{32,16},{48,64},{64,48},{80,96},{96,80},{112,128},{128,112... | collective-permute-start | bytes 589832 | tf_op jit(solution)/shard_map/ppermute | solution.py:35
  119.7 8.4 %collective-permute-start.20 = (f32[192,256]{1,0:T(8,128)S(1)}, f32[192,256]{1,0:T(8,128)S(1)}, u32[]{:S(2)}, u32[]{:S(2)}) collective-permute-start(f32[192,256]{1,0:T(8,128)S(1)} %pad_maximum_fusion.6), channel_id=1, source_target_pairs={{0,1},{1,0},{2,3},{3,2},{4,5},{5,4},{6,7},{7,6},{8,9},{9,8},{10,11... | collective-permute-start | bytes 589832 | tf_op jit(solution)/shard_map/ppermute | solution.py:35
  121.6 10.2 %collective-permute-start.21 = (f32[192,256]{1,0:T(8,128)S(1)}, f32[192,256]{1,0:T(8,128)S(1)}, u32[]{:S(2)}, u32[]{:S(2)}) collective-permute-start(f32[192,256]{1,0:T(8,128)S(1)} %pad_maximum_fusion.7), channel_id=1, source_target_pairs={{1,2},{2,1},{3,4},{4,3},{5,6},{6,5},{7,8},{8,7},{9,10},{10,9},{11,... | collective-permute-start | bytes 589832 | tf_op jit(solution)/shard_map/ppermute | solution.py:35
  133.3 6.4 %collective-permute-start.22 = (f32[192,256]{1,0:T(8,128)S(1)}, f32[192,256]{1,0:T(8,128)S(1)}, u32[]{:S(2)}, u32[]{:S(2)}) collective-permute-start(f32[192,256]{1,0:T(8,128)S(1)} %get-tuple-element.99), channel_id=1, source_target_pairs={{0,16},{16,0},{32,48},{48,32},{64,80},{80,64},{96,112},{112,96},{1... | collective-permute-start | bytes 589832 | tf_op jit(solution)/shard_map/ppermute | solution.py:35
  135.6 8.2 %collective-permute-start.23 = (f32[192,256]{1,0:T(8,128)S(1)}, f32[192,256]{1,0:T(8,128)S(1)}, u32[]{:S(2)}, u32[]{:S(2)}) collective-permute-start(f32[192,256]{1,0:T(8,128)S(1)} %get-tuple-element.100), channel_id=1, source_target_pairs={{16,32},{32,16},{48,64},{64,48},{80,96},{96,80},{112,128},{128,112... | collective-permute-start | bytes 589832 | tf_op jit(solution)/shard_map/ppermute | solution.py:35
  143.8 8.2 %collective-permute-start.24 = (f32[192,256]{1,0:T(8,128)S(1)}, f32[192,256]{1,0:T(8,128)S(1)}, u32[]{:S(2)}, u32[]{:S(2)}) collective-permute-start(f32[192,256]{1,0:T(8,128)S(1)} %pad_maximum_fusion.8), channel_id=1, source_target_pairs={{0,1},{1,0},{2,3},{3,2},{4,5},{5,4},{6,7},{7,6},{8,9},{9,8},{10,11... | collective-permute-start | bytes 589832 | tf_op jit(solution)/shard_map/ppermute | solution.py:35
  145.8 10.1 %collective-permute-start.25 = (f32[192,256]{1,0:T(8,128)S(1)}, f32[192,256]{1,0:T(8,128)S(1)}, u32[]{:S(2)}, u32[]{:S(2)}) collective-permute-start(f32[192,256]{1,0:T(8,128)S(1)} %pad_maximum_fusion.9), channel_id=1, source_target_pairs={{1,2},{2,1},{3,4},{4,3},{5,6},{6,5},{7,8},{8,7},{9,10},{10,9},{11,... | collective-permute-start | bytes 589832 | tf_op jit(solution)/shard_map/ppermute | solution.py:35
  157.2 3.1 %collective-permute-start.26 = (f32[32,256]{1,0:T(8,128)S(1)}, f32[32,256]{1,0:T(8,128)S(1)}, u32[]{:S(2)}, u32[]{:S(2)}) collective-permute-start(f32[32,256]{1,0:T(8,128)S(1)} %get-tuple-element.105), channel_id=1, source_target_pairs={{0,16},{16,0},{32,48},{48,32},{64,80},{80,64},{96,112},{112,96},{1... | collective-permute-start | bytes 98312 | tf_op jit(solution)/shard_map/ppermute | solution.py:35
  160.4 6.8 %collective-permute-start.27 = (f32[64,256]{1,0:T(8,128)S(1)}, f32[64,256]{1,0:T(8,128)S(1)}, u32[]{:S(2)}, u32[]{:S(2)}) collective-permute-start(f32[64,256]{1,0:T(8,128)S(1)} %pad_maximum_fusion.16.mine), channel_id=1, source_target_pairs={{0,496},{16,32},{32,16},{48,64},{64,48},{80,96},{96,80},{112,128},... | collective-permute-start | bytes 196616 | tf_op jit(solution)/shard_map/ppermute | solution.py:35
  167.3 3.1 %collective-permute-start.28 = (f32[32,256]{1,0:T(8,128)S(1)}, f32[32,256]{1,0:T(8,128)S(1)}, u32[]{:S(2)}, u32[]{:S(2)}) collective-permute-start(f32[32,256]{1,0:T(8,128)S(1)} %get-tuple-element.106.sol), channel_id=1, source_target_pairs={{0,16},{16,0},{32,48},{48,32},{64,80},{80,64},{96,112},{112,96},{1... | collective-permute-start | bytes 98312 | tf_op jit(solution)/shard_map/ppermute | solution.py:35
  171.7 6.5 %collective-permute-start.29 = (f32[192,256]{1,0:T(8,128)S(1)}, f32[192,256]{1,0:T(8,128)S(1)}, u32[]{:S(2)}, u32[]{:S(2)}) collective-permute-start(f32[192,256]{1,0:T(8,128)S(1)} %get-tuple-element.109), channel_id=1, source_target_pairs={{0,16},{16,0},{32,48},{48,32},{64,80},{80,64},{96,112},{112,96},{1... | collective-permute-start | bytes 589832 | tf_op jit(solution)/shard_map/ppermute | solution.py:35
  173.8 8.2 %collective-permute-start.30 = (f32[192,256]{1,0:T(8,128)S(1)}, f32[192,256]{1,0:T(8,128)S(1)}, u32[]{:S(2)}, u32[]{:S(2)}) collective-permute-start(f32[192,256]{1,0:T(8,128)S(1)} %get-tuple-element.110), channel_id=1, source_target_pairs={{16,32},{32,16},{48,64},{64,48},{80,96},{96,80},{112,128},{128,112... | collective-permute-start | bytes 589832 | tf_op jit(solution)/shard_map/ppermute | solution.py:35
  182.1 8.4 %collective-permute-start.31 = (f32[192,256]{1,0:T(8,128)S(1)}, f32[192,256]{1,0:T(8,128)S(1)}, u32[]{:S(2)}, u32[]{:S(2)}) collective-permute-start(f32[192,256]{1,0:T(8,128)S(1)} %pad_maximum_fusion.10), channel_id=1, source_target_pairs={{0,1},{1,0},{2,3},{3,2},{4,5},{5,4},{6,7},{7,6},{8,9},{9,8},{10,11... | collective-permute-start | bytes 589832 | tf_op jit(solution)/shard_map/ppermute | solution.py:35
  184.0 10.2 %collective-permute-start.32 = (f32[192,256]{1,0:T(8,128)S(1)}, f32[192,256]{1,0:T(8,128)S(1)}, u32[]{:S(2)}, u32[]{:S(2)}) collective-permute-start(f32[192,256]{1,0:T(8,128)S(1)} %pad_maximum_fusion.11), channel_id=1, source_target_pairs={{1,2},{2,1},{3,4},{4,3},{5,6},{6,5},{7,8},{8,7},{9,10},{10,9},{11,... | collective-permute-start | bytes 589832 | tf_op jit(solution)/shard_map/ppermute | solution.py:35
  195.7 6.4 %collective-permute-start.33 = (f32[192,256]{1,0:T(8,128)S(1)}, f32[192,256]{1,0:T(8,128)S(1)}, u32[]{:S(2)}, u32[]{:S(2)}) collective-permute-start(f32[192,256]{1,0:T(8,128)S(1)} %get-tuple-element.116), channel_id=1, source_target_pairs={{0,16},{16,0},{32,48},{48,32},{64,80},{80,64},{96,112},{112,96},{1... | collective-permute-start | bytes 589832 | tf_op jit(solution)/shard_map/ppermute | solution.py:35
  198.0 8.2 %collective-permute-start.34 = (f32[192,256]{1,0:T(8,128)S(1)}, f32[192,256]{1,0:T(8,128)S(1)}, u32[]{:S(2)}, u32[]{:S(2)}) collective-permute-start(f32[192,256]{1,0:T(8,128)S(1)} %get-tuple-element.117), channel_id=1, source_target_pairs={{16,32},{32,16},{48,64},{64,48},{80,96},{96,80},{112,128},{128,112... | collective-permute-start | bytes 589832 | tf_op jit(solution)/shard_map/ppermute | solution.py:35
  206.3 8.2 %collective-permute-start.35 = (f32[192,256]{1,0:T(8,128)S(1)}, f32[192,256]{1,0:T(8,128)S(1)}, u32[]{:S(2)}, u32[]{:S(2)}) collective-permute-start(f32[192,256]{1,0:T(8,128)S(1)} %pad_maximum_fusion.12), channel_id=1, source_target_pairs={{0,1},{1,0},{2,3},{3,2},{4,5},{5,4},{6,7},{7,6},{8,9},{9,8},{10,11... | collective-permute-start | bytes 589832 | tf_op jit(solution)/shard_map/ppermute | solution.py:35
  208.2 10.1 %collective-permute-start.36 = (f32[192,256]{1,0:T(8,128)S(1)}, f32[192,256]{1,0:T(8,128)S(1)}, u32[]{:S(2)}, u32[]{:S(2)}) collective-permute-start(f32[192,256]{1,0:T(8,128)S(1)} %pad_maximum_fusion.13), channel_id=1, source_target_pairs={{1,2},{2,1},{3,4},{4,3},{5,6},{6,5},{7,8},{8,7},{9,10},{10,9},{11,... | collective-permute-start | bytes 589832 | tf_op jit(solution)/shard_map/ppermute | solution.py:35

commit v2 on v1

--- a/solution.py
+++ b/solution.py
@@ -35,22 +35,54 @@
     return lax.ppermute(x, axis, pairs)
 
 
-def groups_of(ids, counts):
-    alpha = 1 - 2 * lax.rem(ids[0], 2)
-    gamma = 1 - 2 * lax.rem(ids[1], 2)
+def pair(x, axis, side):
+    n = lax.axis_size(axis)
+    if side == 0:
+        pairs = [[i, i + 1] for i in range(0, n, 2)]
+    else:
+        pairs = [[i, (i + 1) % n] for i in range(1, n, 2)]
+    return lax.all_gather(x, axis, axis_index_groups=pairs, tiled=True)
+
+
+def partner_half(side, axis):
+    odd = lax.rem(lax.axis_index(axis), 2)
+    return 1 - odd if side == 0 else odd
+
+
+def half_of(ref, axis, side, rows, at=0, take=None):
+    take = rows if take is None else take
+    if ref.shape[0] != 2 * rows:
+        return ref[at:at + take, :]
+    return ref[pl.ds(pl.multiple_of(partner_half(side, axis) * rows, TILE) + at, take), :]
+
+
+def here():
+    return lax.axis_index("sx"), lax.axis_index("sy")
+
+
+def table_of(counts):
+    i, j = here()
+    alpha = 1 - 2 * lax.rem(i, 2)
+    gamma = 1 - 2 * lax.rem(j, 2)
     size = [counts[d] for d in range(8)]
-    out = []
+    first = [jnp.int32(0)]
+    for d in range(8):
+        first.append(first[d] + size[d])
+    starts, sizes = [], []
     for s, t in SIDES:
         raw = 3 * (s * alpha + 1) + (t * gamma + 1)
         d = jnp.where(raw > 4, raw - 1, raw)
-        start = jnp.int32(0)
-        for e in range(8):
-            start = start + jnp.where(e < d, size[e], 0)
-        out.append((start, counts[d]))
-    total = size[0]
-    for e in range(1, 8):
-        total = total + size[e]
-    return out, total
+        start, count = first[0], size[0]
+        for e in range(1, 8):
+            start = jnp.where(d == e, first[e], start)
+            count = jnp.where(d == e, size[e], count)
+        starts.append(start)
+        sizes.append(count)
+    return starts, sizes, first[8]
+
+
+def groups_of(table):
+    return [(table[0, k], table[0, 8 + k]) for k in range(8)]
 
 
 def to_sorted(order):
@@ -93,11 +125,12 @@
 
 
 def absorb(buf, groups, ra, rb, rc, rd):
-    pieces = (rc[0:64, :], ra[64:128, :], rd[0:64, :], rc[128:192, :], rb[64:128, :], rd[128:192, :],
-              rc[64:128, :], rd[64:128, :])
+    edge_a = half_of(ra, "sx", 0, 3 * MROW, MROW, MROW)
+    pieces = [half_of(rc, "sy", 0, 3 * MROW, k * MROW, MROW) for k in range(3)]
+    order = (pieces[0], edge_a, rd[0:64, :], pieces[2], rb[64:128, :], rd[128:192, :], pieces[1], rd[64:128, :])
     at = lax.broadcasted_iota(jnp.int32, (MROW, 1), 0)
     tail = jnp.zeros((TILE, buf.shape[1]), F32)
-    for (start, count), piece in zip(groups, pieces):
+    for (start, count), piece in zip(groups, order):
         place, skip = window(start)
         piece = jnp.concatenate([jnp.where(at < count, piece, 0.0), tail], axis=0)
         buf[place, :] = buf[place, :] + pltpu.roll(piece, skip, 0)
@@ -109,30 +142,47 @@
     buf[n:n + MROW + TILE, :] = jnp.zeros((MROW + TILE, x.shape[1]), F32)
 
 
-def weights(n, total):
+def weights(n, table):
+    total = jnp.max(table[1:2, :], axis=1, keepdims=True)
     return jnp.where(lax.broadcasted_iota(jnp.int32, (n, 1), 0) < total, 0.5, 1.0).astype(F32)
 
 
-def chooser(ids, blocks, peers, size):
-    alpha = 1 - 2 * lax.rem(ids[0], 2)
+def chooser(blocks, peers, size):
+    mine = lax.axis_index("sx")
+    alpha = 1 - 2 * lax.rem(mine, 2)
     n = blocks.shape[1]
     rows = lax.broadcasted_iota(jnp.int32, (size, n), 0)
     parts = []
     for shift in (0, 1, -1):
-        want = lax.rem(ids[0] + shift * alpha + peers, peers) * size
+        want = lax.rem(mine + shift * alpha + peers, peers) * size
         parts.append((blocks - want == rows).astype(F32))
     return jnp.concatenate(parts, axis=0)
 
 
-def k_first(ids, counts, order, source, inverse, sorted_ref, a_ref, b_ref, c_ref, d_ref, buf):
-    groups, _ = groups_of(ids, counts)
+def k_first(counts, order, source, inverse, sorted_ref, table_ref, a_ref, b_ref, c_ref, d_ref, buf):
+    starts, sizes, total = table_of(counts)
+    at = lax.broadcasted_iota(jnp.int32, table_ref.shape, 1)
+    row = lax.broadcasted_iota(jnp.int32, table_ref.shape, 0)
+    table = jnp.full(table_ref.shape, total, jnp.int32)
+    for k, value in enumerate(starts + sizes):
+        table = jnp.where((row == 0) & (at == k), value, table)
+    table_ref[...] = table
     x = moved(to_sorted(order[...]), source[...])
     sorted_ref[...] = x
     fill(buf, x)
-    emit(buf, groups, a_ref, b_ref, c_ref, d_ref)
+    emit(buf, list(zip(starts, sizes)), a_ref, b_ref, c_ref, d_ref)
     n = inverse.shape[0]
     b_ref[3 * MROW:3 * MROW + n, :] = jnp.zeros((n, b_ref.shape[1]), F32)
     b_ref[3 * MROW:3 * MROW + n, 0:n] = inverse[...]
+
+
+def k_relay(ra, rb, c, d, to_c, to_d):
+    to_c[0:64, :] = half_of(ra, "sx", 0, 3 * MROW, 0, MROW)
+    to_d[0:64, :] = half_of(ra, "sx", 0, 3 * MROW, 2 * MROW, MROW)
+    to_c[64:128, :] = c[...]
+    to_d[64:128, :] = d[...]
+    to_c[128:192, :] = rb[0:64, :]
+    to_d[128:192, :] = rb[128:192, :]
 
 
 def k_sort(order, local, schur, basis, local_ref, schur_ref, basis_ref, onehot):
@@ -148,9 +198,9 @@
             dst[at:at + step, :] = dot(half, onehot[...], (((1,), (1,)), ((), ()))).astype(BF16)
 
 
-def k_residual(first, peers, size, ids, counts, blocks, basis, old, product, ra, rb, rc, rd,
+def k_residual(first, peers, size, table, blocks, basis, old, product, ra, rb, rc, rd,
                res_ref, scaled_ref, give_ref, keep_ref, buf):
-    groups, total = groups_of(ids, counts)
+    groups = groups_of(table)
     if first:
         fill(buf, old[...])
     else:
@@ -159,42 +209,47 @@
     n = old.shape[0]
     res = buf[0:n, :] if first else old[...] - buf[0:n, :]
     res_ref[...] = res
-    scaled = (weights(n, total) * res).astype(BF16)
+    scaled = (weights(n, table) * res).astype(BF16)
     scaled_ref[...] = scaled
     primal = lax.dot_general(basis[...], scaled, (((0,), (0,)), ((), ())), preferred_element_type=F32)
-    select = chooser(ids, blocks[...], peers, size)
+    select = chooser(blocks[...], peers, size)
     spread_out = jnp.dot(select, primal, precision=HIGH, preferred_element_type=F32)
     give_ref[...] = spread_out[size:2 * size, :]
     keep_ref[0:size, :] = spread_out[0:size, :]
     keep_ref[size:2 * size, :] = spread_out[2 * size:3 * size, :]
 
 
-def k_local(local, scaled, out):
-    out[...] = jnp.dot(local[...], scaled[...], preferred_element_type=F32)
-
-
-def k_coarse(size, inv, inv_b, mine, theirs, own_ref, b_ref):
+def k_middle(size, kept, from_a, mine):
+    mine[0:size, :] = kept[0:size, :] + half_of(from_a, "sx", 0, size)
+    mine[size:2 * size, :] = kept[size:2 * size, :]
+
+
+def k_coarse(size, inv, first_b, mine, theirs, own_ref, b_ref):
     dot = partial(jnp.dot, precision=HIGH, preferred_element_type=F32)
-    own_ref[...] = dot(inv[...], mine[0:size, :] + theirs[size:2 * size, :])
-    b_ref[...] = dot(inv_b[:, 0:size], theirs[0:size, :] + mine[size:2 * size, :])
-
-
-def k_update(peers, size, ids, counts, blocks, basis, local, sol, sol_a, sol_b,
+    their_own = half_of(theirs, "sx", 1, 2 * size, 0, size)
+    their_mine = half_of(theirs, "sx", 1, 2 * size, size, size)
+    inv_b = first_b[3 * MROW:3 * MROW + size, 0:size]
+    own_ref[...] = dot(inv[...], mine[0:size, :] + their_mine)
+    b_ref[...] = dot(inv_b, their_own + mine[size:2 * size, :])
+
+
+def k_update(peers, size, table, blocks, basis, matrix, scaled, sol, sol_a, sol_b,
              up_ref, a_ref, b_ref, c_ref, d_ref, buf):
-    groups, total = groups_of(ids, counts)
-    select = chooser(ids, blocks[...], peers, size)
-    stack = jnp.concatenate([sol[...], sol_a[...], sol_b[...]], axis=0)
+    groups = groups_of(table)
+    select = chooser(blocks[...], peers, size)
+    stack = jnp.concatenate([sol[...], half_of(sol_a, "sx", 0, size), sol_b[...]], axis=0)
     picked = lax.dot_general(select, stack, (((0,), (0,)), ((), ())), precision=HIGH, preferred_element_type=F32)
-    n = local.shape[0]
-    up = local[...] + jnp.dot(basis[...], picked.astype(BF16), preferred_element_type=F32)
-    up = weights(n, total) * up
+    n = scaled.shape[0]
+    up = jnp.dot(matrix[...], scaled[...], preferred_element_type=F32)
+    up = up + jnp.dot(basis[...], picked.astype(BF16), preferred_element_type=F32)
+    up = weights(n, table) * up
     up_ref[...] = up
     fill(buf, up)
     emit(buf, groups, a_ref, b_ref, c_ref, d_ref)
 
 
-def k_apply(keep, gain, ids, counts, schur, up, old, ra, rb, rc, rd, dir_ref, v_ref, a_ref, b_ref, c_ref, d_ref, buf):
-    groups, _ = groups_of(ids, counts)
+def k_apply(keep, gain, table, schur, up, old, ra, rb, rc, rd, dir_ref, v_ref, a_ref, b_ref, c_ref, d_ref, buf):
+    groups = groups_of(table)
     fill(buf, up[...])
     absorb(buf, groups, ra, rb, rc, rd)
     n = up.shape[0]
@@ -212,8 +267,8 @@
     out[...] = moved(from_sorted(order[...]), one[...] + two[...] + three[...])
 
 
-def k_final(ids, counts, order, old, product, ra, rb, rc, rd, out, buf):
-    groups, _ = groups_of(ids, counts)
+def k_final(table, order, old, product, ra, rb, rc, rd, out, buf):
+    groups = groups_of(table)
     fill(buf, product[...])
     absorb(buf, groups, ra, rb, rc, rd)
     n = old.shape[0]
@@ -234,13 +289,14 @@
     )(*ins)
 
 
-def exchange(a, b, c, d, wrap=False):
-    rb = swap(b, "sx", 1, wrap)
-    ra = swap(a, "sx", 0)
-    to_d = jnp.concatenate([ra[128:192], d, rb[128:192]], axis=0)
-    to_c = jnp.concatenate([ra[0:64], c, rb[0:64]], axis=0)
+def exchange(a, b, c, d, hide=False):
+    cols = c.shape[1]
+    rb = swap(b, "sx", 1, b.shape[0] > 3 * MROW)
+    ra = swap(a, "sx", 0) if hide else pair(a, "sx", 0)
+    leg = jax.ShapeDtypeStruct((3 * MROW, cols), F32)
+    to_c, to_d = call(k_relay, (ra, rb, c, d), [leg, leg], 0)
     rd = swap(to_d, "sy", 1)
-    rc = swap(to_c, "sy", 0)
+    rc = swap(to_c, "sy", 0) if hide else pair(to_c, "sy", 0)
     return ra, rb, rc, rd
 
 
@@ -251,7 +307,6 @@
     size = inv.shape[0]
     modes = primal_basis.shape[3]
     peers = lax.axis_size("sx")
-    ids = jnp.stack([lax.axis_index("sx"), lax.axis_index("sy")]).astype(jnp.int32)
     counts = shared_count[0, 0]
     order = row_order[0]
     blocks = primal_map[0]
@@ -263,11 +318,11 @@
     buf = [pltpu.VMEM((n + MROW + TILE, cols), F32)]
     big = 2 * n * n * cols
 
-    src, *out = call(
+    src, table, *out = call(
         k_first,
-        (ids, counts, order, source, inv),
-        [full, sent[0], f32(3 * MROW + size, cols), sent[2], sent[3]],
-        3 * big, buf, 2,
+        (counts, order, source, inv),
+        [full, jax.ShapeDtypeStruct((8, 128), jnp.int32), sent[0], f32(3 * MROW + size, cols), sent[2], sent[3]],
+        3 * big, buf, 1,
     )
     a_s, s_s, basis = call(
         k_sort,
@@ -275,8 +330,8 @@
         [b16(n, n), b16(n, n), b16(n, modes)],
         8 * n * n * n, [pltpu.VMEM((n, n), BF16)],
     )
-    got = exchange(*out, wrap=True)
-    inv_b = got[1][3 * MROW:3 * MROW + size]
+    got = exchange(*out, hide=True)
+    first_b = got[1]
 
     res, product, direction = src, src, src
     directions = []
@@ -285,23 +340,22 @@
     for step in range(ITERS):
         res, scaled, give, kept = call(
             partial(k_residual, step == 0, peers, size),
-            (ids, counts, blocks, basis, res, product, *got),
+            (table, blocks, basis, res, product, *got),
             [full, b16(n, cols), f32(size, cols), f32(2 * size, cols)],
-            2 * n * modes * cols, buf, 2,
+            2 * n * modes * cols, buf,
         )
-        from_a = swap(give, "sx", 0)
-        mine = jnp.concatenate([kept[0:size] + from_a, kept[size:2 * size]], axis=0)
-        theirs = swap(mine, "sx", 1, True)
-        local, = call(k_local, (a_s, scaled), [full], big)
+        from_a = pair(give, "sx", 0)
+        mine, = call(partial(k_middle, size), (kept, from_a), [f32(2 * size, cols)], 0)
+        theirs = pair(mine, "sx", 1)
         sol, sol_b = call(
-            partial(k_coarse, size), (inv, inv_b, mine, theirs), [f32(size, cols), f32(size, cols)],
+            partial(k_coarse, size), (inv, first_b, mine, theirs), [f32(size, cols), f32(size, cols)],
             4 * size * size * cols,
         )
-        sol_a = swap(sol, "sx", 0)
+        sol_a = pair(sol, "sx", 0)
         up, *out = call(
             partial(k_update, peers, size),
-            (ids, counts, blocks, basis, local, sol, sol_a, sol_b),
-            [full] + sent, 2 * n * modes * cols, buf, 2,
+            (table, blocks, basis, a_s, scaled, sol, sol_a, sol_b),
+            [full] + sent, big, buf,
         )
         got = exchange(*out)
         if step == 0:
@@ -312,13 +366,13 @@
             rho = rho_new
         direction, product, *out = call(
             partial(k_apply, keep, gain),
-            (ids, counts, s_s, up, direction, *got),
-            [full, full] + sent, big, buf, 2,
+            (table, s_s, up, direction, *got),
+            [full, full] + sent, big, buf,
         )
         directions.append(direction)
-        got = exchange(*out)
+        got = exchange(*out, hide=step == ITERS - 1)
     total, = call(k_solution, (order, *directions), [full], 3 * big)
-    residual, = call(k_final, (ids, counts, order, res, product, *got), [full], 3 * big, buf, 2)
+    residual, = call(k_final, (table, order, res, product, *got), [full], 3 * big, buf)
     return total[None, None], residual[None, None]
 
 

time: 222 us -> 187 us (0.84)
  blocking collectives: 0 us -> 74.7 us
  starting transfers between devices: 112 us -> 58.3 us
  waiting for transfers between devices: 77.1 us -> 28 us
  Pallas kernels: 25.8 us -> 20 us
    all_gather x0 -> x19, blocking collectives: none -> 74.7 us  [pair(): return lax.all_gather(x, axis, axis_index_groups=pairs, tiled=True)]
    ppermute x37 -> x18, starting transfers between devices: 112 us -> 58.3 us  [swap(): return lax.ppermute(x, axis, pairs)]
    ppermute x37 -> x18, waiting for transfers between devices: 77.1 us -> 28 us  [swap(): return lax.ppermute(x, axis, pairs)]
    pallas_call x19 -> x26, Pallas kernels: 25.8 us -> 20 us  [call(): pl.pallas_call(kernel, out_shape=tuple(outs), in_specs=[SMEM] * scalars +...]
    unnamed x23 -> x21, local copies, waits for them, and re-layouts: 4.65 us -> 4.64 us
  transfers between devices with their start and end apart: 37 -> 18, of which waited for: 29 -> 11; matrix products, arithmetic and copies ran while one was open for 0% -> 0% of each run, Pallas kernels for 4% -> 4%
where the time goes in v2:
time: 187 us
  blocking collectives  74.7 us (40%)
  starting transfers between devices  58.3 us (31%)
  waiting for transfers between devices  28 us (15%)
  Pallas kernels  20 us (11%)
  local copies, waits for them, and re-layouts  4.64 us (2%)
    all_gather x19, blocking collectives, pair(): return lax.all_gather(x, axis, axis_index_groups=pairs, tiled=True)  74.7 us
    ppermute x18, starting transfers between devices, swap(): return lax.ppermute(x, axis, pairs)  58.3 us
    ppermute x18, waiting for transfers between devices, swap(): return lax.ppermute(x, axis, pairs)  28 us
    pallas_call x26, Pallas kernels, call(): pl.pallas_call(kernel, out_shape=tuple(outs), in_specs=[SMEM] * scalars +...  20 us
    unnamed x21, local copies, waits for them, and re-layouts  4.64 us
  transfers between devices with their start and end apart: 18, of which 11 were waited for; matrix products, arithmetic and copies ran while one was open for 0% of the time, Pallas kernels for 4%

profile of v2, /device:TPU:249, one launch (start us, length us, event | category | flops | bytes accessed | tf_op | source)
XLA Modules:
  0.0 186.5 jit_solution(3434573959581185976)
XLA Ops:
  3.8 2.1 %shard_map.95 = (f32[768,256]{1,0:T(8,128)S(1)}, s32[8,128]{1,0:T(8,128)S(1)}, f32[192,256]{1,0:T(8,128)S(1)}, f32[224,256]{1,0:T(8,128)S(1)}, f32[64,256]{1,0:T(8,128)S(1)}, /*index=5*/f32[64,256]{1,0:T(8,128)S(1)}) custom-call(s32[8]{0:T(128)S(1)} %bitcast.28, s32[1,768]{1,0:T(1,128)S(1)} %bitcast.24, f32[768,256]{1,0:T(8,128)S(1)} %bitcast.23, ...), custom_call_target="tpu_custom_call" | custom-call | flops 905969664 | bytes 2141216 | tf_op jit(solution)/shard_map/pallas_call | solution.py:281
  5.9 5.3 %collective-permute-start.1 = (f32[224,256]{1,0:T(8,128)S(1)}, f32[224,256]{1,0:T(8,128)S(1)}, u32[]{:S(2)}, u32[]{:S(2)}) collective-permute-start(f32[224,256]{1,0:T(8,128)S(1)} %get-tuple-element.82), channel_id=1, source_target_pairs={{0,496},{16,32},{32,16},{48,64},{64,48},{80,96},{96,80},{112,128},... | collective-permute-start | bytes 688136 | tf_op jit(solution)/shard_map/ppermute | solution.py:35
  11.2 1.9 %collective-permute-start = (f32[192,256]{1,0:T(8,128)S(1)}, f32[192,256]{1,0:T(8,128)S(1)}, u32[]{:S(2)}, u32[]{:S(2)}) collective-permute-start(f32[192,256]{1,0:T(8,128)S(1)} %get-tuple-element.81), channel_id=1, source_target_pairs={{0,16},{16,0},{32,48},{48,32},{64,80},{80,64},{96,112},{112,96},{1... | collective-permute-start | bytes 589832 | tf_op jit(solution)/shard_map/ppermute | solution.py:35
  14.9 3.1 %collective-permute-start.2 = (f32[192,256]{1,0:T(8,128)S(1)}, f32[192,256]{1,0:T(8,128)S(1)}, u32[]{:S(2)}, u32[]{:S(2)}) collective-permute-start(f32[192,256]{1,0:T(8,128)S(1)} %get-tuple-element.85), channel_id=1, source_target_pairs={{0,1},{1,0},{2,3},{3,2},{4,5},{5,4},{6,7},{7,6},{8,9},{9,8},{10,11... | collective-permute-start | bytes 589832 | tf_op jit(solution)/shard_map/ppermute | solution.py:35
  18.1 3.9 %collective-permute-start.3 = (f32[192,256]{1,0:T(8,128)S(1)}, f32[192,256]{1,0:T(8,128)S(1)}, u32[]{:S(2)}, u32[]{:S(2)}) collective-permute-start(f32[192,256]{1,0:T(8,128)S(1)} %get-tuple-element.86), channel_id=1, source_target_pairs={{1,2},{2,1},{3,4},{4,3},{5,6},{6,5},{7,8},{8,7},{9,10},{10,9},{11,... | collective-permute-start | bytes 589832 | tf_op jit(solution)/shard_map/ppermute | solution.py:35
  23.3 4.5 %shard_map.96 = (bf16[768,768]{1,0:T(8,128)(2,1)S(1)}, bf16[768,768]{1,0:T(8,128)(2,1)S(1)}, bf16[768,32]{1,0:T(8,128)(2,1)S(1)}) custom-call(s32[1,768]{1,0:T(1,128)S(1)} %bitcast.25, bf16[768,768]{1,0:T(8,128)(2,1)S(1)} %bitcast.21, bf16[768,768]{1,0:T(8,128)(2,1)S(1)} %bitcast.22, bf16[768,32]{1,0:T(8,128)(2,1)S(1)} %bitcast.10), custom_call_target="tpu_custom_call" | custom-call | flops 3623878656 | bytes 4819968 | tf_op jit(solution)/shard_map/pallas_call | solution.py:281
  29.3 2.4 %all_gather.57.from_a = f32[64,256]{1,0:T(8,128)S(1)} all-gather(f32[32,256]{1,0:T(8,128)S(1)} %get-tuple-element.89), channel_id=1, replica_groups={{0,16},{32,48},{64,80},{96,112},{128,144},{160,176},{192,208},{224,240}..., dimensions={0}, use_global_device_ids=true | all-gather | bytes 98304 | tf_op jit(solution)/shard_map/all_gather | solution.py:44
  31.7 5.6 %all_gather.58.theirs = f32[128,256]{1,0:T(8,128)S(1)} all-gather(f32[64,256]{1,0:T(8,128)S(1)} %shard_map.99.mine), channel_id=1, replica_groups={{16,32},{48,64},{80,96},{112,128},{144,160},{176,192},{208,224},{240,25..., dimensions={0}, use_global_device_ids=true | all-gather | bytes 196608 | tf_op jit(solution)/shard_map/all_gather | solution.py:44
  37.5 1.8 all_gather.59.sol_a
  40.4 4.3 %collective-permute-start.4 = (f32[192,256]{1,0:T(8,128)S(1)}, f32[192,256]{1,0:T(8,128)S(1)}, u32[]{:S(2)}, u32[]{:S(2)}) collective-permute-start(f32[192,256]{1,0:T(8,128)S(1)} %get-tuple-element.94), channel_id=1, source_target_pairs={{16,32},{32,16},{48,64},{64,48},{80,96},{96,80},{112,128},{128,112... | collective-permute-start | bytes 589832 | tf_op jit(solution)/shard_map/ppermute | solution.py:35
  44.6 2.1 %all_gather.60.ra = f32[384,256]{1,0:T(8,128)S(1)} all-gather(f32[192,256]{1,0:T(8,128)S(1)} %get-tuple-element.93), channel_id=1, replica_groups={{0,16},{32,48},{64,80},{96,112},{128,144},{160,176},{192,208},{224,240}..., dimensions={0}, use_global_device_ids=true | all-gather | bytes 589824 | tf_op jit(solution)/shard_map/all_gather | solution.py:44
  46.7 1.9 collective-permute-done.4.rb
  48.6 3.9 %collective-permute-start.5 = (f32[192,256]{1,0:T(8,128)S(1)}, f32[192,256]{1,0:T(8,128)S(1)}, u32[]{:S(2)}, u32[]{:S(2)}) collective-permute-start(f32[192,256]{1,0:T(8,128)S(1)} %get-tuple-element.98), channel_id=1, source_target_pairs={{1,2},{2,1},{3,4},{4,3},{5,6},{6,5},{7,8},{8,7},{9,10},{10,9},{11,... | collective-permute-start | bytes 589832 | tf_op jit(solution)/shard_map/ppermute | solution.py:35
  52.5 7.0 %all_gather.61.rc = f32[384,256]{1,0:T(8,128)S(1)} all-gather(f32[192,256]{1,0:T(8,128)S(1)} %get-tuple-element.97), channel_id=1, replica_groups={{0,1},{2,3},{4,5},{6,7},{8,9},{10,11},{12,13},{14,15},{16,17},{18,19},{..., dimensions={0}, use_global_device_ids=true | all-gather | bytes 589824 | tf_op jit(solution)/shard_map/all_gather | solution.py:44
  60.4 3.6 %collective-permute-start.6 = (f32[192,256]{1,0:T(8,128)S(1)}, f32[192,256]{1,0:T(8,128)S(1)}, u32[]{:S(2)}, u32[]{:S(2)}) collective-permute-start(f32[192,256]{1,0:T(8,128)S(1)} %get-tuple-element.103), channel_id=1, source_target_pairs={{16,32},{32,16},{48,64},{64,48},{80,96},{96,80},{112,128},{128,112... | collective-permute-start | bytes 589832 | tf_op jit(solution)/shard_map/ppermute | solution.py:35
  64.0 2.1 %all_gather.62.ra = f32[384,256]{1,0:T(8,128)S(1)} all-gather(f32[192,256]{1,0:T(8,128)S(1)} %get-tuple-element.102), channel_id=1, replica_groups={{0,16},{32,48},{64,80},{96,112},{128,144},{160,176},{192,208},{224,240}..., dimensions={0}, use_global_device_ids=true | all-gather | bytes 589824 | tf_op jit(solution)/shard_map/all_gather | solution.py:44
  66.1 2.5 %collective-permute-done.6.rb = f32[192,256]{1,0:T(8,128)S(1)} collective-permute-done((f32[192,256]{1,0:T(8,128)S(1)}, f32[192,256]{1,0:T(8,128)S(1)}, u32[]{:S(2)}, u32[]{:S(2)}) %collective-permute-start.6) | collective-permute-done | bytes 196640 | tf_op jit(solution)/shard_map/ppermute | solution.py:35
  68.6 3.5 %collective-permute-start.7 = (f32[192,256]{1,0:T(8,128)S(1)}, f32[192,256]{1,0:T(8,128)S(1)}, u32[]{:S(2)}, u32[]{:S(2)}) collective-permute-start(f32[192,256]{1,0:T(8,128)S(1)} %get-tuple-element.107), channel_id=1, source_target_pairs={{1,2},{2,1},{3,4},{4,3},{5,6},{6,5},{7,8},{8,7},{9,10},{10,9},{11,... | collective-permute-start | bytes 589832 | tf_op jit(solution)/shard_map/ppermute | solution.py:35
  72.1 7.4 %all_gather.63.rc = f32[384,256]{1,0:T(8,128)S(1)} all-gather(f32[192,256]{1,0:T(8,128)S(1)} %get-tuple-element.106), channel_id=1, replica_groups={{0,1},{2,3},{4,5},{6,7},{8,9},{10,11},{12,13},{14,15},{16,17},{18,19},{..., dimensions={0}, use_global_device_ids=true | all-gather | bytes 589824 | tf_op jit(solution)/shard_map/all_gather | solution.py:44
  80.4 1.9 %all_gather.64.from_a = f32[64,256]{1,0:T(8,128)S(1)} all-gather(f32[32,256]{1,0:T(8,128)S(1)} %get-tuple-element.110), channel_id=1, replica_groups={{0,16},{32,48},{64,80},{96,112},{128,144},{160,176},{192,208},{224,240}..., dimensions={0}, use_global_device_ids=true | all-gather | bytes 98304 | tf_op jit(solution)/shard_map/all_gather | solution.py:44
  82.3 5.6 %all_gather.65.theirs = f32[128,256]{1,0:T(8,128)S(1)} all-gather(f32[64,256]{1,0:T(8,128)S(1)} %shard_map.106.mine), channel_id=1, replica_groups={{16,32},{48,64},{80,96},{112,128},{144,160},{176,192},{208,224},{240,25..., dimensions={0}, use_global_device_ids=true | all-gather | bytes 196608 | tf_op jit(solution)/shard_map/all_gather | solution.py:44
  88.1 1.8 all_gather.66.sol_a
  90.9 3.2 %collective-permute-start.8 = (f32[192,256]{1,0:T(8,128)S(1)}, f32[192,256]{1,0:T(8,128)S(1)}, u32[]{:S(2)}, u32[]{:S(2)}) collective-permute-start(f32[192,256]{1,0:T(8,128)S(1)} %get-tuple-element.115), channel_id=1, source_target_pairs={{16,32},{32,16},{48,64},{64,48},{80,96},{96,80},{112,128},{128,112... | collective-permute-start | bytes 589832 | tf_op jit(solution)/shard_map/ppermute | solution.py:35
  94.1 2.1 %all_gather.67.ra = f32[384,256]{1,0:T(8,128)S(1)} all-gather(f32[192,256]{1,0:T(8,128)S(1)} %get-tuple-element.114), channel_id=1, replica_groups={{0,16},{32,48},{64,80},{96,112},{128,144},{160,176},{192,208},{224,240}..., dimensions={0}, use_global_device_ids=true | all-gather | bytes 589824 | tf_op jit(solution)/shard_map/all_gather | solution.py:44
  96.2 2.9 %collective-permute-done.8.rb = f32[192,256]{1,0:T(8,128)S(1)} collective-permute-done((f32[192,256]{1,0:T(8,128)S(1)}, f32[192,256]{1,0:T(8,128)S(1)}, u32[]{:S(2)}, u32[]{:S(2)}) %collective-permute-start.8) | collective-permute-done | bytes 196640 | tf_op jit(solution)/shard_map/ppermute | solution.py:35
  99.1 3.9 %collective-permute-start.9 = (f32[192,256]{1,0:T(8,128)S(1)}, f32[192,256]{1,0:T(8,128)S(1)}, u32[]{:S(2)}, u32[]{:S(2)}) collective-permute-start(f32[192,256]{1,0:T(8,128)S(1)} %get-tuple-element.119), channel_id=1, source_target_pairs={{1,2},{2,1},{3,4},{4,3},{5,6},{6,5},{7,8},{8,7},{9,10},{10,9},{11,... | collective-permute-start | bytes 589832 | tf_op jit(solution)/shard_map/ppermute | solution.py:35
  103.0 7.0 %all_gather.68.rc = f32[384,256]{1,0:T(8,128)S(1)} all-gather(f32[192,256]{1,0:T(8,128)S(1)} %get-tuple-element.118), channel_id=1, replica_groups={{0,1},{2,3},{4,5},{6,7},{8,9},{10,11},{12,13},{14,15},{16,17},{18,19},{..., dimensions={0}, use_global_device_ids=true | all-gather | bytes 589824 | tf_op jit(solution)/shard_map/all_gather | solution.py:44
  111.0 2.5 %collective-permute-start.10 = (f32[192,256]{1,0:T(8,128)S(1)}, f32[192,256]{1,0:T(8,128)S(1)}, u32[]{:S(2)}, u32[]{:S(2)}) collective-permute-start(f32[192,256]{1,0:T(8,128)S(1)} %get-tuple-element.124), channel_id=1, source_target_pairs={{16,32},{32,16},{48,64},{64,48},{80,96},{96,80},{112,128},{128,112... | collective-permute-start | bytes 589832 | tf_op jit(solution)/shard_map/ppermute | solution.py:35
  113.5 2.1 %all_gather.69.ra = f32[384,256]{1,0:T(8,128)S(1)} all-gather(f32[192,256]{1,0:T(8,128)S(1)} %get-tuple-element.123), channel_id=1, replica_groups={{0,16},{32,48},{64,80},{96,112},{128,144},{160,176},{192,208},{224,240}..., dimensions={0}, use_global_device_ids=true | all-gather | bytes 589824 | tf_op jit(solution)/shard_map/all_gather | solution.py:44
  115.6 3.6 %collective-permute-done.10.rb = f32[192,256]{1,0:T(8,128)S(1)} collective-permute-done((f32[192,256]{1,0:T(8,128)S(1)}, f32[192,256]{1,0:T(8,128)S(1)}, u32[]{:S(2)}, u32[]{:S(2)}) %collective-permute-start.10) | collective-permute-done | bytes 196640 | tf_op jit(solution)/shard_map/ppermute | solution.py:35
  119.2 3.7 %collective-permute-start.11 = (f32[192,256]{1,0:T(8,128)S(1)}, f32[192,256]{1,0:T(8,128)S(1)}, u32[]{:S(2)}, u32[]{:S(2)}) collective-permute-start(f32[192,256]{1,0:T(8,128)S(1)} %get-tuple-element.128), channel_id=1, source_target_pairs={{1,2},{2,1},{3,4},{4,3},{5,6},{6,5},{7,8},{8,7},{9,10},{10,9},{11,... | collective-permute-start | bytes 589832 | tf_op jit(solution)/shard_map/ppermute | solution.py:35
  122.9 7.4 %all_gather.70.rc = f32[384,256]{1,0:T(8,128)S(1)} all-gather(f32[192,256]{1,0:T(8,128)S(1)} %get-tuple-element.127), channel_id=1, replica_groups={{0,1},{2,3},{4,5},{6,7},{8,9},{10,11},{12,13},{14,15},{16,17},{18,19},{..., dimensions={0}, use_global_device_ids=true | all-gather | bytes 589824 | tf_op jit(solution)/shard_map/all_gather | solution.py:44
  131.1 1.9 %all_gather.71.from_a = f32[64,256]{1,0:T(8,128)S(1)} all-gather(f32[32,256]{1,0:T(8,128)S(1)} %get-tuple-element.131), channel_id=1, replica_groups={{0,16},{32,48},{64,80},{96,112},{128,144},{160,176},{192,208},{224,240}..., dimensions={0}, use_global_device_ids=true | all-gather | bytes 98304 | tf_op jit(solution)/shard_map/all_gather | solution.py:44
  133.0 5.6 %all_gather.72.theirs = f32[128,256]{1,0:T(8,128)S(1)} all-gather(f32[64,256]{1,0:T(8,128)S(1)} %shard_map.113.mine), channel_id=1, replica_groups={{16,32},{48,64},{80,96},{112,128},{144,160},{176,192},{208,224},{240,25..., dimensions={0}, use_global_device_ids=true | all-gather | bytes 196608 | tf_op jit(solution)/shard_map/all_gather | solution.py:44
  138.8 1.8 all_gather.73.sol_a
  141.7 2.1 %collective-permute-start.12 = (f32[192,256]{1,0:T(8,128)S(1)}, f32[192,256]{1,0:T(8,128)S(1)}, u32[]{:S(2)}, u32[]{:S(2)}) collective-permute-start(f32[192,256]{1,0:T(8,128)S(1)} %get-tuple-element.136), channel_id=1, source_target_pairs={{16,32},{32,16},{48,64},{64,48},{80,96},{96,80},{112,128},{128,112... | collective-permute-start | bytes 589832 | tf_op jit(solution)/shard_map/ppermute | solution.py:35
  143.8 2.1 %all_gather.74.ra = f32[384,256]{1,0:T(8,128)S(1)} all-gather(f32[192,256]{1,0:T(8,128)S(1)} %get-tuple-element.135), channel_id=1, replica_groups={{0,16},{32,48},{64,80},{96,112},{128,144},{160,176},{192,208},{224,240}..., dimensions={0}, use_global_device_ids=true | all-gather | bytes 589824 | tf_op jit(solution)/shard_map/all_gather | solution.py:44
  145.8 4.0 %collective-permute-done.12.rb = f32[192,256]{1,0:T(8,128)S(1)} collective-permute-done((f32[192,256]{1,0:T(8,128)S(1)}, f32[192,256]{1,0:T(8,128)S(1)}, u32[]{:S(2)}, u32[]{:S(2)}) %collective-permute-start.12) | collective-permute-done | bytes 196640 | tf_op jit(solution)/shard_map/ppermute | solution.py:35
  149.9 3.9 %collective-permute-start.13 = (f32[192,256]{1,0:T(8,128)S(1)}, f32[192,256]{1,0:T(8,128)S(1)}, u32[]{:S(2)}, u32[]{:S(2)}) collective-permute-start(f32[192,256]{1,0:T(8,128)S(1)} %get-tuple-element.140), channel_id=1, source_target_pairs={{1,2},{2,1},{3,4},{4,3},{5,6},{6,5},{7,8},{8,7},{9,10},{10,9},{11,... | collective-permute-start | bytes 589832 | tf_op jit(solution)/shard_map/ppermute | solution.py:35
  153.8 7.0 %all_gather.75.rc = f32[384,256]{1,0:T(8,128)S(1)} all-gather(f32[192,256]{1,0:T(8,128)S(1)} %get-tuple-element.139), channel_id=1, replica_groups={{0,1},{2,3},{4,5},{6,7},{8,9},{10,11},{12,13},{14,15},{16,17},{18,19},{..., dimensions={0}, use_global_device_ids=true | all-gather | bytes 589824 | tf_op jit(solution)/shard_map/all_gather | solution.py:44
  161.8 2.3 %collective-permute-start.14 = (f32[192,256]{1,0:T(8,128)S(1)}, f32[192,256]{1,0:T(8,128)S(1)}, u32[]{:S(2)}, u32[]{:S(2)}) collective-permute-start(f32[192,256]{1,0:T(8,128)S(1)} %get-tuple-element.144), channel_id=1, source_target_pairs={{0,16},{16,0},{32,48},{48,32},{64,80},{80,64},{96,112},{112,96},{1... | collective-permute-start | bytes 589832 | tf_op jit(solution)/shard_map/ppermute | solution.py:35
  164.1 1.9 %collective-permute-start.15 = (f32[192,256]{1,0:T(8,128)S(1)}, f32[192,256]{1,0:T(8,128)S(1)}, u32[]{:S(2)}, u32[]{:S(2)}) collective-permute-start(f32[192,256]{1,0:T(8,128)S(1)} %get-tuple-element.145), channel_id=1, source_target_pairs={{16,32},{32,16},{48,64},{64,48},{80,96},{96,80},{112,128},{128,112... | collective-permute-start | bytes 589832 | tf_op jit(solution)/shard_map/ppermute | solution.py:35
  166.0 6.3 %collective-permute-done.15.rb = f32[192,256]{1,0:T(8,128)S(1)} collective-permute-done((f32[192,256]{1,0:T(8,128)S(1)}, f32[192,256]{1,0:T(8,128)S(1)}, u32[]{:S(2)}, u32[]{:S(2)}) %collective-permute-start.15) | collective-permute-done | bytes 196640 | tf_op jit(solution)/shard_map/ppermute | solution.py:35
  172.3 1.9 %collective-permute-start.16 = (f32[192,256]{1,0:T(8,128)S(1)}, f32[192,256]{1,0:T(8,128)S(1)}, u32[]{:S(2)}, u32[]{:S(2)}) collective-permute-start(f32[192,256]{1,0:T(8,128)S(1)} %get-tuple-element.148), channel_id=1, source_target_pairs={{0,1},{1,0},{2,3},{3,2},{4,5},{5,4},{6,7},{7,6},{8,9},{9,8},{10,11... | collective-permute-start | bytes 589832 | tf_op jit(solution)/shard_map/ppermute | solution.py:35
  174.2 3.5 %collective-permute-start.17 = (f32[192,256]{1,0:T(8,128)S(1)}, f32[192,256]{1,0:T(8,128)S(1)}, u32[]{:S(2)}, u32[]{:S(2)}) collective-permute-start(f32[192,256]{1,0:T(8,128)S(1)} %get-tuple-element.149), channel_id=1, source_target_pairs={{1,2},{2,1},{3,4},{4,3},{5,6},{6,5},{7,8},{8,7},{9,10},{10,9},{11,... | collective-permute-start | bytes 589832 | tf_op jit(solution)/shard_map/ppermute | solution.py:35
  177.7 2.0 %shard_map.118 = f32[768,256]{1,0:T(8,128)} custom-call(s32[1,768]{1,0:T(1,128)S(1)} %bitcast.26, f32[768,256]{1,0:T(8,128)S(1)} %get-tuple-element.99.old.one, f32[768,256]{1,0:T(8,128)S(1)} %get-tuple-element.120.old.two, f32[768,256]{1,0:T(8,128)S(1)} %get-tuple-element.141.three), custom_call_target="tpu_custom_call" | custom-call | flops 905969664 | bytes 3148800 | tf_op jit(solution)/shard_map/pallas_call | solution.py:281
  180.5 3.7 %collective-permute-done.17.rd = f32[192,256]{1,0:T(8,128)S(1)} collective-permute-done((f32[192,256]{1,0:T(8,128)S(1)}, f32[192,256]{1,0:T(8,128)S(1)}, u32[]{:S(2)}, u32[]{:S(2)}) %collective-permute-start.17) | collective-permute-done | bytes 196640 | tf_op jit(solution)/shard_map/ppermute | solution.py:35
  184.2 2.3 %shard_map.120 = f32[768,256]{1,0:T(8,128)} custom-call(s32[8,128]{1,0:T(8,128)S(1)} %get-tuple-element.76.table, s32[1,768]{1,0:T(1,128)S(1)} %bitcast.27, f32[768,256]{1,0:T(8,128)S(1)} %get-tuple-element.142.old, f32[768,256]{1,0:T(8,128)S(1)} %get-tuple-element.143.product, f32[192,256]{1,0:T(8,128)S(1)} %collective-permute-done.14.ra, ...), custom_call_target="tpu_custom_call" | custom-call | flops 905969664 | bytes 3152896 | tf_op jit(solution)/shard_map/pallas_call | solution.py:281
  (54 shorter events, 16.7 us)
Async XLA Ops:
  0.6 0.7 copy-start
  1.4 1.1 copy-start.5
  2.5 0.7 copy-start.6
  3.2 0.7 copy-start.8
  3.8 9.3 %copy-start.9 = (bf16[1,1,768,32]{2,3,1,0:T(8,128)(2,1)S(1)}, bf16[1,1,768,32]{2,3,1,0:T(8,128)(2,1)}, u32[]{:S(2)}) copy-start(bf16[1,1,768,32]{2,3,1,0:T(8,128)(2,1)} %param.11) | copy-start | bytes 147460
  3.8 18.2 %copy-start.3 = (bf16[1,1,768,768]{3,2,1,0:T(8,128)(2,1)S(1)}, bf16[1,1,768,768]{3,2,1,0:T(8,128)(2,1)}, u32[]{:S(2)}) copy-start(bf16[1,1,768,768]{3,2,1,0:T(8,128)(2,1)} %param.10) | copy-start | bytes 3538948
  3.8 18.2 %copy-start.7 = (s32[1,1,768]{2,1,0:T(1,128)S(1)}, s32[1,1,768]{2,1,0:T(1,128)}, u32[]{:S(2)}) copy-start(s32[1,1,768]{2,1,0:T(1,128)} %param.15) | copy-start | bytes 9220
  5.9 9.0 %collective-permute-start.1 = (f32[224,256]{1,0:T(8,128)S(1)}, f32[224,256]{1,0:T(8,128)S(1)}, u32[]{:S(2)}, u32[]{:S(2)}) collective-permute-start(f32[224,256]{1,0:T(8,128)S(1)} %get-tuple-element.82), channel_id=1, source_target_pairs={{0,496},{16,32},{32,16},{48,64},{64,48},{80,96},{96,80},{112,128},... | collective-permute-start | bytes 688136 | tf_op jit(solution)/shard_map/ppermute | solution.py:35
  11.2 3.3 %collective-permute-start = (f32[192,256]{1,0:T(8,128)S(1)}, f32[192,256]{1,0:T(8,128)S(1)}, u32[]{:S(2)}, u32[]{:S(2)}) collective-permute-start(f32[192,256]{1,0:T(8,128)S(1)} %get-tuple-element.81), channel_id=1, source_target_pairs={{0,16},{16,0},{32,48},{48,32},{64,80},{80,64},{96,112},{112,96},{1... | collective-permute-start | bytes 589832 | tf_op jit(solution)/shard_map/ppermute | solution.py:35
  14.9 12.9 %collective-permute-start.2 = (f32[192,256]{1,0:T(8,128)S(1)}, f32[192,256]{1,0:T(8,128)S(1)}, u32[]{:S(2)}, u32[]{:S(2)}) collective-permute-start(f32[192,256]{1,0:T(8,128)S(1)} %get-tuple-element.85), channel_id=1, source_target_pairs={{0,1},{1,0},{2,3},{3,2},{4,5},{5,4},{6,7},{7,6},{8,9},{9,8},{10,11... | collective-permute-start | bytes 589832 | tf_op jit(solution)/shard_map/ppermute | solution.py:35
  18.1 10.5 %collective-permute-start.3 = (f32[192,256]{1,0:T(8,128)S(1)}, f32[192,256]{1,0:T(8,128)S(1)}, u32[]{:S(2)}, u32[]{:S(2)}) collective-permute-start(f32[192,256]{1,0:T(8,128)S(1)} %get-tuple-element.86), channel_id=1, source_target_pairs={{1,2},{2,1},{3,4},{4,3},{5,6},{6,5},{7,8},{8,7},{9,10},{10,9},{11,... | collective-permute-start | bytes 589832 | tf_op jit(solution)/shard_map/ppermute | solution.py:35
  22.0 1.3 copy-start.4
  23.3 5.3 %copy-start.2 = (s32[1,1,32]{2,1,0:T(1,128)S(1)}, s32[1,1,32]{2,1,0:T(1,128)}, u32[]{:S(2)}) copy-start(s32[1,1,32]{2,1,0:T(1,128)} %param.13) | copy-start | bytes 388
  28.5 8.8 %copy-start.1 = (f32[1,1,32,32]{3,2,1,0:T(8,128)S(1)}, f32[1,1,32,32]{3,2,1,0:T(8,128)}, u32[]{:S(2)}) copy-start(f32[1,1,32,32]{3,2,1,0:T(8,128)} %param.12) | copy-start | bytes 12292
  40.4 8.2 %collective-permute-start.4 = (f32[192,256]{1,0:T(8,128)S(1)}, f32[192,256]{1,0:T(8,128)S(1)}, u32[]{:S(2)}, u32[]{:S(2)}) collective-permute-start(f32[192,256]{1,0:T(8,128)S(1)} %get-tuple-element.94), channel_id=1, source_target_pairs={{16,32},{32,16},{48,64},{64,48},{80,96},{96,80},{112,128},{128,112... | collective-permute-start | bytes 589832 | tf_op jit(solution)/shard_map/ppermute | solution.py:35
  48.6 10.9 %collective-permute-start.5 = (f32[192,256]{1,0:T(8,128)S(1)}, f32[192,256]{1,0:T(8,128)S(1)}, u32[]{:S(2)}, u32[]{:S(2)}) collective-permute-start(f32[192,256]{1,0:T(8,128)S(1)} %get-tuple-element.98), channel_id=1, source_target_pairs={{1,2},{2,1},{3,4},{4,3},{5,6},{6,5},{7,8},{8,7},{9,10},{10,9},{11,... | collective-permute-start | bytes 589832 | tf_op jit(solution)/shard_map/ppermute | solution.py:35
  60.4 8.2 %collective-permute-start.6 = (f32[192,256]{1,0:T(8,128)S(1)}, f32[192,256]{1,0:T(8,128)S(1)}, u32[]{:S(2)}, u32[]{:S(2)}) collective-permute-start(f32[192,256]{1,0:T(8,128)S(1)} %get-tuple-element.103), channel_id=1, source_target_pairs={{16,32},{32,16},{48,64},{64,48},{80,96},{96,80},{112,128},{128,112... | collective-permute-start | bytes 589832 | tf_op jit(solution)/shard_map/ppermute | solution.py:35
  68.6 10.9 %collective-permute-start.7 = (f32[192,256]{1,0:T(8,128)S(1)}, f32[192,256]{1,0:T(8,128)S(1)}, u32[]{:S(2)}, u32[]{:S(2)}) collective-permute-start(f32[192,256]{1,0:T(8,128)S(1)} %get-tuple-element.107), channel_id=1, source_target_pairs={{1,2},{2,1},{3,4},{4,3},{5,6},{6,5},{7,8},{8,7},{9,10},{10,9},{11,... | collective-permute-start | bytes 589832 | tf_op jit(solution)/shard_map/ppermute | solution.py:35
  90.9 8.2 %collective-permute-start.8 = (f32[192,256]{1,0:T(8,128)S(1)}, f32[192,256]{1,0:T(8,128)S(1)}, u32[]{:S(2)}, u32[]{:S(2)}) collective-permute-start(f32[192,256]{1,0:T(8,128)S(1)} %get-tuple-element.115), channel_id=1, source_target_pairs={{16,32},{32,16},{48,64},{64,48},{80,96},{96,80},{112,128},{128,112... | collective-permute-start | bytes 589832 | tf_op jit(solution)/shard_map/ppermute | solution.py:35
  99.1 10.9 %collective-permute-start.9 = (f32[192,256]{1,0:T(8,128)S(1)}, f32[192,256]{1,0:T(8,128)S(1)}, u32[]{:S(2)}, u32[]{:S(2)}) collective-permute-start(f32[192,256]{1,0:T(8,128)S(1)} %get-tuple-element.119), channel_id=1, source_target_pairs={{1,2},{2,1},{3,4},{4,3},{5,6},{6,5},{7,8},{8,7},{9,10},{10,9},{11,... | collective-permute-start | bytes 589832 | tf_op jit(solution)/shard_map/ppermute | solution.py:35
  111.0 8.2 %collective-permute-start.10 = (f32[192,256]{1,0:T(8,128)S(1)}, f32[192,256]{1,0:T(8,128)S(1)}, u32[]{:S(2)}, u32[]{:S(2)}) collective-permute-start(f32[192,256]{1,0:T(8,128)S(1)} %get-tuple-element.124), channel_id=1, source_target_pairs={{16,32},{32,16},{48,64},{64,48},{80,96},{96,80},{112,128},{128,112... | collective-permute-start | bytes 589832 | tf_op jit(solution)/shard_map/ppermute | solution.py:35
  119.2 11.1 %collective-permute-start.11 = (f32[192,256]{1,0:T(8,128)S(1)}, f32[192,256]{1,0:T(8,128)S(1)}, u32[]{:S(2)}, u32[]{:S(2)}) collective-permute-start(f32[192,256]{1,0:T(8,128)S(1)} %get-tuple-element.128), channel_id=1, source_target_pairs={{1,2},{2,1},{3,4},{4,3},{5,6},{6,5},{7,8},{8,7},{9,10},{10,9},{11,... | collective-permute-start | bytes 589832 | tf_op jit(solution)/shard_map/ppermute | solution.py:35
  141.7 8.2 %collective-permute-start.12 = (f32[192,256]{1,0:T(8,128)S(1)}, f32[192,256]{1,0:T(8,128)S(1)}, u32[]{:S(2)}, u32[]{:S(2)}) collective-permute-start(f32[192,256]{1,0:T(8,128)S(1)} %get-tuple-element.136), channel_id=1, source_target_pairs={{16,32},{32,16},{48,64},{64,48},{80,96},{96,80},{112,128},{128,112... | collective-permute-start | bytes 589832 | tf_op jit(solution)/shard_map/ppermute | solution.py:35
  149.9 10.9 %collective-permute-start.13 = (f32[192,256]{1,0:T(8,128)S(1)}, f32[192,256]{1,0:T(8,128)S(1)}, u32[]{:S(2)}, u32[]{:S(2)}) collective-permute-start(f32[192,256]{1,0:T(8,128)S(1)} %get-tuple-element.140), channel_id=1, source_target_pairs={{1,2},{2,1},{3,4},{4,3},{5,6},{6,5},{7,8},{8,7},{9,10},{10,9},{11,... | collective-permute-start | bytes 589832 | tf_op jit(solution)/shard_map/ppermute | solution.py:35
  161.8 4.2 %collective-permute-start.14 = (f32[192,256]{1,0:T(8,128)S(1)}, f32[192,256]{1,0:T(8,128)S(1)}, u32[]{:S(2)}, u32[]{:S(2)}) collective-permute-start(f32[192,256]{1,0:T(8,128)S(1)} %get-tuple-element.144), channel_id=1, source_target_pairs={{0,16},{16,0},{32,48},{48,32},{64,80},{80,64},{96,112},{112,96},{1... | collective-permute-start | bytes 589832 | tf_op jit(solution)/shard_map/ppermute | solution.py:35
  164.1 8.2 %collective-permute-start.15 = (f32[192,256]{1,0:T(8,128)S(1)}, f32[192,256]{1,0:T(8,128)S(1)}, u32[]{:S(2)}, u32[]{:S(2)}) collective-permute-start(f32[192,256]{1,0:T(8,128)S(1)} %get-tuple-element.145), channel_id=1, source_target_pairs={{16,32},{32,16},{48,64},{64,48},{80,96},{96,80},{112,128},{128,112... | collective-permute-start | bytes 589832 | tf_op jit(solution)/shard_map/ppermute | solution.py:35
  172.3 8.2 %collective-permute-start.16 = (f32[192,256]{1,0:T(8,128)S(1)}, f32[192,256]{1,0:T(8,128)S(1)}, u32[]{:S(2)}, u32[]{:S(2)}) collective-permute-start(f32[192,256]{1,0:T(8,128)S(1)} %get-tuple-element.148), channel_id=1, source_target_pairs={{0,1},{1,0},{2,3},{3,2},{4,5},{5,4},{6,7},{7,6},{8,9},{9,8},{10,11... | collective-permute-start | bytes 589832 | tf_op jit(solution)/shard_map/ppermute | solution.py:35
  174.2 10.0 %collective-permute-start.17 = (f32[192,256]{1,0:T(8,128)S(1)}, f32[192,256]{1,0:T(8,128)S(1)}, u32[]{:S(2)}, u32[]{:S(2)}) collective-permute-start(f32[192,256]{1,0:T(8,128)S(1)} %get-tuple-element.149), channel_id=1, source_target_pairs={{1,2},{2,1},{3,4},{4,3},{5,6},{6,5},{7,8},{8,7},{9,10},{10,9},{11,... | collective-permute-start | bytes 589832 | tf_op jit(solution)/shard_map/ppermute | solution.py:35

commit v3 on v2

--- a/solution.py
+++ b/solution.py
@@ -16,44 +16,55 @@
 SIDES = ((1, 1), (1, 0), (1, -1), (-1, 1), (-1, 0), (-1, -1), (0, 1), (0, -1))
 
 VMEM = pl.BlockSpec(memory_space=pltpu.VMEM)
-SMEM = pl.BlockSpec(memory_space=pltpu.SMEM)
+FAR = pl.BlockSpec(memory_space=pltpu.HBM)
+LOOSE = pl.BlockSpec(memory_space=pl.ANY)
 F32 = jnp.float32
 BF16 = jnp.bfloat16
 HIGH = lax.Precision.HIGHEST
 
 
-def swap(x, axis, side, wrap=False):
-    n = lax.axis_size(axis)
-    if side == 0:
-        pairs = [(i, i ^ 1) for i in range(n)]
-    else:
-        pairs = [(i, ((i + 1) ^ 1) - 1) for i in range(n)]
-        if wrap:
-            pairs = [(i, p % n) for i, p in pairs]
-        else:
-            pairs = [(i, p) for i, p in pairs if 0 <= p < n]
-    return lax.ppermute(x, axis, pairs)
-
-
-def pair(x, axis, side):
-    n = lax.axis_size(axis)
-    if side == 0:
-        pairs = [[i, i + 1] for i in range(0, n, 2)]
-    else:
-        pairs = [[i, (i + 1) % n] for i in range(1, n, 2)]
-    return lax.all_gather(x, axis, axis_index_groups=pairs, tiled=True)
-
-
-def partner_half(side, axis):
-    odd = lax.rem(lax.axis_index(axis), 2)
-    return 1 - odd if side == 0 else odd
-
-
-def half_of(ref, axis, side, rows, at=0, take=None):
+def other(i, j, side):
+    if side in "AB":
+        return (i ^ 1 if side == "A" else ((i + 1) ^ 1) - 1), j
+    return i, (j ^ 1 if (side == "C") == (i % 2 == 0) else ((j + 1) ^ 1) - 1)
+
+
+def links(side):
+    sizes = lax.axis_size("sx"), lax.axis_size("sy")
+    for i in range(sizes[0]):
+        for j in range(sizes[1]):
+            yield sizes, (i, j), other(i, j, side)
+
+
+def swap(x, side, wrap=False):
+    pairs = []
+    for (n, m), (i, j), (p, q) in links(side):
+        if wrap or (0 <= p < n and 0 <= q < m):
+            pairs.append((i * m + j, p % n * m + q % m))
+    return lax.ppermute(x, ("sx", "sy"), pairs)
+
+
+def leads(i, j, side):
+    if side == "A":
+        return 1 - i % 2
+    if side == "B":
+        return i % 2
+    return (1 + i + j) % 2 if side == "C" else (i + j) % 2
+
+
+def pair(x, side):
+    pairs = []
+    for (n, m), (i, j), (p, q) in links(side):
+        if leads(i, j, side):
+            pairs.append([i * m + j, p % n * m + q % m])
+    return lax.all_gather(x, ("sx", "sy"), axis_index_groups=pairs, tiled=True)
+
+
+def half_of(ref, side, rows, at=0, take=None):
     take = rows if take is None else take
     if ref.shape[0] != 2 * rows:
         return ref[at:at + take, :]
-    return ref[pl.ds(pl.multiple_of(partner_half(side, axis) * rows, TILE) + at, take), :]
+    return ref[pl.ds(pl.multiple_of(lax.rem(leads(*here(), side), 2) * rows, TILE) + at, take), :]
 
 
 def here():
@@ -63,7 +74,7 @@
 def table_of(counts):
     i, j = here()
     alpha = 1 - 2 * lax.rem(i, 2)
-    gamma = 1 - 2 * lax.rem(j, 2)
+    gamma = 1 - 2 * lax.rem(i + j, 2)
     size = [counts[d] for d in range(8)]
     first = [jnp.int32(0)]
     for d in range(8):
@@ -125,8 +136,8 @@
 
 
 def absorb(buf, groups, ra, rb, rc, rd):
-    edge_a = half_of(ra, "sx", 0, 3 * MROW, MROW, MROW)
-    pieces = [half_of(rc, "sy", 0, 3 * MROW, k * MROW, MROW) for k in range(3)]
+    edge_a = half_of(ra, "A", 3 * MROW, MROW, MROW)
+    pieces = [half_of(rc, "C", 3 * MROW, k * MROW, MROW) for k in range(3)]
     order = (pieces[0], edge_a, rd[0:64, :], pieces[2], rb[64:128, :], rd[128:192, :], pieces[1], rd[64:128, :])
     at = lax.broadcasted_iota(jnp.int32, (MROW, 1), 0)
     tail = jnp.zeros((TILE, buf.shape[1]), F32)
@@ -159,7 +170,18 @@
     return jnp.concatenate(parts, axis=0)
 
 
-def k_first(counts, order, source, inverse, sorted_ref, table_ref, a_ref, b_ref, c_ref, d_ref, buf):
+def k_first(counts_in, order_in, source_in, inverse_in, sorted_ref, table_ref, a_ref, b_ref, c_ref, d_ref,
+            buf, counts, order, source, inverse, arrived):
+    copies = [
+        pltpu.make_async_copy(src, dst, arrived.at[k])
+        for k, (src, dst) in enumerate(
+            ((order_in, order), (counts_in, counts), (source_in, source), (inverse_in, inverse)))
+    ]
+    for copy in copies:
+        copy.start()
+    copies[0].wait()
+    onehot = to_sorted(order[...])
+    copies[1].wait()
     starts, sizes, total = table_of(counts)
     at = lax.broadcasted_iota(jnp.int32, table_ref.shape, 1)
     row = lax.broadcasted_iota(jnp.int32, table_ref.shape, 0)
@@ -167,39 +189,46 @@
     for k, value in enumerate(starts + sizes):
         table = jnp.where((row == 0) & (at == k), value, table)
     table_ref[...] = table
-    x = moved(to_sorted(order[...]), source[...])
+    copies[2].wait()
+    x = moved(onehot, source[...])
     sorted_ref[...] = x
     fill(buf, x)
     emit(buf, list(zip(starts, sizes)), a_ref, b_ref, c_ref, d_ref)
     n = inverse.shape[0]
+    copies[3].wait()
     b_ref[3 * MROW:3 * MROW + n, :] = jnp.zeros((n, b_ref.shape[1]), F32)
     b_ref[3 * MROW:3 * MROW + n, 0:n] = inverse[...]
 
 
-def k_relay(ra, rb, c, d, to_c, to_d):
-    to_c[0:64, :] = half_of(ra, "sx", 0, 3 * MROW, 0, MROW)
-    to_d[0:64, :] = half_of(ra, "sx", 0, 3 * MROW, 2 * MROW, MROW)
+def k_relay(ra, rb, c, d, *rest):
+    to_c, to_d = rest[-2:]
+    to_c[0:64, :] = half_of(ra, "A", 3 * MROW, 2 * MROW, MROW)
+    to_d[0:64, :] = half_of(ra, "A", 3 * MROW, 0, MROW)
     to_c[64:128, :] = c[...]
     to_d[64:128, :] = d[...]
-    to_c[128:192, :] = rb[0:64, :]
-    to_d[128:192, :] = rb[128:192, :]
-
-
-def k_sort(order, local, schur, basis, local_ref, schur_ref, basis_ref, onehot):
+    to_c[128:192, :] = rb[128:192, :]
+    to_d[128:192, :] = rb[0:64, :]
+
+
+def k_sort(order, matrix, *rest):
+    onehot = rest[-1]
     onehot[...] = to_sorted(order[...])
-    n = local.shape[0]
+    n = matrix.shape[0]
     step = 256
     dot = partial(lax.dot_general, preferred_element_type=F32)
-    basis_ref[...] = dot(onehot[...], basis[...], (((1,), (0,)), ((), ()))).astype(BF16)
+    if len(rest) == 4:
+        basis, out, basis_ref = rest[:3]
+        basis_ref[...] = dot(onehot[...], basis[...], (((1,), (0,)), ((), ()))).astype(BF16)
+    else:
+        out = rest[0]
     for at in range(0, n, step):
-        rows = onehot[at:at + step, :]
-        for src, dst in ((local, local_ref), (schur, schur_ref)):
-            half = dot(rows, src[...], (((1,), (0,)), ((), ()))).astype(BF16)
-            dst[at:at + step, :] = dot(half, onehot[...], (((1,), (1,)), ((), ()))).astype(BF16)
+        half = dot(onehot[at:at + step, :], matrix[...], (((1,), (0,)), ((), ()))).astype(BF16)
+        out[at:at + step, :] = dot(half, onehot[...], (((1,), (1,)), ((), ()))).astype(BF16)
 
 
 def k_residual(first, peers, size, table, blocks, basis, old, product, ra, rb, rc, rd,
-               res_ref, scaled_ref, give_ref, keep_ref, buf):
+               *rest):
+    res_ref, scaled_ref, give_ref, keep_ref, buf = rest[-5:]
     groups = groups_of(table)
     if first:
         fill(buf, old[...])
@@ -220,14 +249,14 @@
 
 
 def k_middle(size, kept, from_a, mine):
-    mine[0:size, :] = kept[0:size, :] + half_of(from_a, "sx", 0, size)
+    mine[0:size, :] = kept[0:size, :] + half_of(from_a, "A", size)
     mine[size:2 * size, :] = kept[size:2 * size, :]
 
 
 def k_coarse(size, inv, first_b, mine, theirs, own_ref, b_ref):
     dot = partial(jnp.dot, precision=HIGH, preferred_element_type=F32)
-    their_own = half_of(theirs, "sx", 1, 2 * size, 0, size)
-    their_mine = half_of(theirs, "sx", 1, 2 * size, size, size)
+    their_own = half_of(theirs, "B", 2 * size, 0, size)
+    their_mine = half_of(theirs, "B", 2 * size, size, size)
     inv_b = first_b[3 * MROW:3 * MROW + size, 0:size]
     own_ref[...] = dot(inv[...], mine[0:size, :] + their_mine)
     b_ref[...] = dot(inv_b, their_own + mine[size:2 * size, :])
@@ -237,7 +266,7 @@
              up_ref, a_ref, b_ref, c_ref, d_ref, buf):
     groups = groups_of(table)
     select = chooser(blocks[...], peers, size)
-    stack = jnp.concatenate([sol[...], half_of(sol_a, "sx", 0, size), sol_b[...]], axis=0)
+    stack = jnp.concatenate([sol[...], half_of(sol_a, "A", size), sol_b[...]], axis=0)
     picked = lax.dot_general(select, stack, (((0,), (0,)), ((), ())), precision=HIGH, preferred_element_type=F32)
     n = scaled.shape[0]
     up = jnp.dot(matrix[...], scaled[...], preferred_element_type=F32)
@@ -263,7 +292,8 @@
     emit(buf, groups, a_ref, b_ref, c_ref, d_ref)
 
 
-def k_solution(order, one, two, three, out):
+def k_solution(order, one, two, three, out, token):
+    token[...] = jnp.zeros(token.shape, F32)
     out[...] = moved(from_sorted(order[...]), one[...] + two[...] + three[...])
 
 
@@ -275,28 +305,27 @@
     out[...] = moved(from_sorted(order[...]), old[...] - buf[0:n, :])
 
 
-def call(kernel, ins, outs, flops, scratch=(), scalars=0):
+def call(kernel, ins, outs, flops, scratch=(), far=0, after=(), room=28):
     moved_bytes = sum(x.size * x.dtype.itemsize for x in ins)
     moved_bytes += sum(x.size * x.dtype.itemsize for x in outs)
     return pl.pallas_call(
         kernel,
         out_shape=tuple(outs),
-        in_specs=[SMEM] * scalars + [VMEM] * (len(ins) - scalars),
+        in_specs=[FAR] * far + [VMEM] * (len(ins) - far) + [LOOSE] * len(after),
         out_specs=tuple([VMEM] * len(outs)),
         scratch_shapes=list(scratch),
-        compiler_params=pltpu.CompilerParams(vmem_limit_bytes=28 * 1024 * 1024),
+        compiler_params=pltpu.CompilerParams(vmem_limit_bytes=room * 1024 * 1024),
         cost_estimate=pl.CostEstimate(flops=flops, bytes_accessed=moved_bytes, transcendentals=0),
-    )(*ins)
-
-
-def exchange(a, b, c, d, hide=False):
-    cols = c.shape[1]
-    rb = swap(b, "sx", 1, b.shape[0] > 3 * MROW)
-    ra = swap(a, "sx", 0) if hide else pair(a, "sx", 0)
-    leg = jax.ShapeDtypeStruct((3 * MROW, cols), F32)
-    to_c, to_d = call(k_relay, (ra, rb, c, d), [leg, leg], 0)
-    rd = swap(to_d, "sy", 1)
-    rc = swap(to_c, "sy", 0) if hide else pair(to_c, "sy", 0)
+    )(*ins, *after)
+
+
+def exchange(a, b, c, d, first=False, beside=()):
+    leg = jax.ShapeDtypeStruct((3 * MROW, c.shape[1]), F32)
+    rb = swap(b, "B", first)
+    ra = swap(a, "A") if first else pair(a, "A")
+    to_c, to_d = call(k_relay, (ra, rb, c, d), [leg, leg], 0, after=beside)
+    rd = swap(to_d, "D")
+    rc = swap(to_c, "C") if first else pair(to_c, "C")
     return ra, rb, rc, rd
 
 
@@ -322,15 +351,19 @@
         k_first,
         (counts, order, source, inv),
         [full, jax.ShapeDtypeStruct((8, 128), jnp.int32), sent[0], f32(3 * MROW + size, cols), sent[2], sent[3]],
-        3 * big, buf, 1,
+        2 * big,
+        buf + [
+            pltpu.SMEM((8,), jnp.int32), pltpu.VMEM(order.shape, jnp.int32), pltpu.VMEM((n, cols), F32),
+            pltpu.VMEM((size, size), F32), pltpu.SemaphoreType.DMA((4,)),
+        ],
+        4, (), 62,
     )
-    a_s, s_s, basis = call(
-        k_sort,
-        (order, local_inverse[0, 0], schur[0, 0], primal_basis[0, 0]),
-        [b16(n, n), b16(n, n), b16(n, modes)],
-        8 * n * n * n, [pltpu.VMEM((n, n), BF16)],
+    onehot = [pltpu.VMEM((n, n), BF16)]
+    a_s, basis = call(
+        k_sort, (order, local_inverse[0, 0], primal_basis[0, 0]), [b16(n, n), b16(n, modes)], 4 * n * n * n, onehot,
     )
-    got = exchange(*out, hide=True)
+    s_s, = call(k_sort, (order, schur[0, 0]), [b16(n, n)], 4 * n * n * n, onehot)
+    got = exchange(*out, first=True, beside=(a_s,))
     first_b = got[1]
 
     res, product, direction = src, src, src
@@ -342,16 +375,16 @@
             partial(k_residual, step == 0, peers, size),
             (table, blocks, basis, res, product, *got),
             [full, b16(n, cols), f32(size, cols), f32(2 * size, cols)],
-            2 * n * modes * cols, buf,
+            2 * n * modes * cols, buf, after=(s_s,) if step == 0 else (),
         )
-        from_a = pair(give, "sx", 0)
+        from_a = pair(give, "A")
         mine, = call(partial(k_middle, size), (kept, from_a), [f32(2 * size, cols)], 0)
-        theirs = pair(mine, "sx", 1)
+        theirs = pair(mine, "B")
         sol, sol_b = call(
             partial(k_coarse, size), (inv, first_b, mine, theirs), [f32(size, cols), f32(size, cols)],
             4 * size * size * cols,
         )
-        sol_a = pair(sol, "sx", 0)
+        sol_a = pair(sol, "A")
         up, *out = call(
             partial(k_update, peers, size),
             (table, blocks, basis, a_s, scaled, sol, sol_a, sol_b),
@@ -370,9 +403,12 @@
             [full, full] + sent, big, buf,
         )
         directions.append(direction)
-        got = exchange(*out, hide=step == ITERS - 1)
-    total, = call(k_solution, (order, *directions), [full], 3 * big)
-    residual, = call(k_final, (table, order, res, product, *got), [full], 3 * big, buf)
+        beside = ()
+        if step == ITERS - 1:
+            total, token = call(k_solution, (order, *directions), [full, f32(8, 128)], 2 * big)
+            beside = (token,)
+        got = exchange(*out, beside=beside)
+    residual, = call(k_final, (table, order, res, product, *got), [full], 2 * big, buf)
     return total[None, None], residual[None, None]
 
 

time: 187 us -> 181 us (0.968)
  the two profiles are of different devices: /device:TPU:249 before, /device:TPU:105 now
where the time goes in v3:
time: 181 us
  blocking collectives  93 us (51%)
  starting transfers between devices  54.6 us (30%)
  Pallas kernels  22.1 us (12%)
  waiting for transfers between devices  9.73 us (5%)
    all_gather x21, blocking collectives, pair(): return lax.all_gather(x, ('sx', 'sy'), axis_index_groups=pairs, tiled=True)  93 us
    ppermute x16, starting transfers between devices, swap(): return lax.ppermute(x, ('sx', 'sy'), pairs)  54.6 us
    pallas_call x27, Pallas kernels, call(): pl.pallas_call(kernel, out_shape=tuple(outs), in_specs=[FAR] * far + [VME...  22.1 us
    ppermute x16, waiting for transfers between devices, swap(): return lax.ppermute(x, ('sx', 'sy'), pairs)  9.73 us
  transfers between devices with their start and end apart: 16, of which 6 were waited for; matrix products, arithmetic and copies ran while one was open for 0% of the time, Pallas kernels for 4%

profile of v3, /device:TPU:105, one launch (start us, length us, event | category | flops | bytes accessed | tf_op | source)
XLA Modules:
  0.0 180.7 jit_solution(10533096275215162503)
XLA Ops:
  0.7 3.7 %shard_map.95 = (f32[768,256]{1,0:T(8,128)}, s32[8,128]{1,0:T(8,128)}, f32[192,256]{1,0:T(8,128)}, f32[224,256]{1,0:T(8,128)}, f32[64,256]{1,0:T(8,128)}, /*index=5*/f32[64,256]{1,0:T(8,128)}) custom-call(s32[8]{0:T(128)} %bitcast.31, s32[1,768]{1,0:T(1,128)} %bitcast.21, f32[768,256]{1,0:T(8,128)} %bitcast.29, f32[32,32]{1,0:T(8,128)} %bitcast.11), custom_call_target="tpu_custom_call" | custom-call | flops 603979776 | bytes 2141216 | tf_op jit(solution)/shard_map/pallas_call | solution.py:311
  4.3 5.3 %collective-permute-start.1 = (f32[224,256]{1,0:T(8,128)}, f32[224,256]{1,0:T(8,128)S(1)}, u32[]{:S(2)}, u32[]{:S(2)}) collective-permute-start(f32[224,256]{1,0:T(8,128)} %get-tuple-element.82), channel_id=1, source_target_pairs={{0,496},{1,497},{2,498},{3,499},{4,500},{5,501},{6,502},{7,503},{8... | collective-permute-start | bytes 688136 | tf_op jit(solution)/shard_map/ppermute | solution.py:44
  9.7 1.9 %collective-permute-start = (f32[192,256]{1,0:T(8,128)}, f32[192,256]{1,0:T(8,128)S(1)}, u32[]{:S(2)}, u32[]{:S(2)}) collective-permute-start(f32[192,256]{1,0:T(8,128)} %get-tuple-element.81), channel_id=1, source_target_pairs={{0,16},{1,17},{2,18},{3,19},{4,20},{5,21},{6,22},{7,23},{8,24},{9,... | collective-permute-start | bytes 589832 | tf_op jit(solution)/shard_map/ppermute | solution.py:44
  11.8 2.7 %shard_map.97 = (bf16[768,768]{1,0:T(8,128)(2,1)S(1)}, bf16[768,32]{1,0:T(8,128)(2,1)S(1)}) custom-call(s32[1,768]{1,0:T(1,128)S(1)} %bitcast.22, bf16[768,768]{1,0:T(8,128)(2,1)S(1)} %bitcast.26, bf16[768,32]{1,0:T(8,128)(2,1)S(1)} %bitcast.10), custom_call_target="tpu_custom_call" | custom-call | flops 1811939328 | bytes 2460672 | tf_op jit(solution)/shard_map/pallas_call | solution.py:311
  14.6 4.4 %collective-permute-start.2 = (f32[192,256]{1,0:T(8,128)S(1)}, f32[192,256]{1,0:T(8,128)S(1)}, u32[]{:S(2)}, u32[]{:S(2)}) collective-permute-start(f32[192,256]{1,0:T(8,128)S(1)} %get-tuple-element.85), channel_id=1, source_target_pairs={{0,1},{1,0},{2,3},{3,2},{4,5},{5,4},{6,7},{7,6},{8,9},{9,8},{10,11... | collective-permute-start | bytes 589832 | tf_op jit(solution)/shard_map/ppermute | solution.py:44
  19.0 2.0 %collective-permute-start.3 = (f32[192,256]{1,0:T(8,128)S(1)}, f32[192,256]{1,0:T(8,128)S(1)}, u32[]{:S(2)}, u32[]{:S(2)}) collective-permute-start(f32[192,256]{1,0:T(8,128)S(1)} %get-tuple-element.86), channel_id=1, source_target_pairs={{1,2},{2,1},{3,4},{4,3},{5,6},{6,5},{7,8},{8,7},{9,10},{10,9},{11,... | collective-permute-start | bytes 589832 | tf_op jit(solution)/shard_map/ppermute | solution.py:44
  21.0 2.3 %shard_map.96.rest_0_.schur = bf16[768,768]{1,0:T(8,128)(2,1)S(1)} custom-call(s32[1,768]{1,0:T(1,128)S(1)} %bitcast.23, bf16[768,768]{1,0:T(8,128)(2,1)S(1)} %bitcast.27), custom_call_target="tpu_custom_call" | custom-call | flops 1811939328 | bytes 2362368 | tf_op jit(solution)/shard_map/pallas_call | solution.py:311
  23.4 2.1 %collective-permute-done.3.rd = f32[192,256]{1,0:T(8,128)S(1)} collective-permute-done((f32[192,256]{1,0:T(8,128)S(1)}, f32[192,256]{1,0:T(8,128)S(1)}, u32[]{:S(2)}, u32[]{:S(2)}) %collective-permute-start.3) | collective-permute-done | bytes 196640 | tf_op jit(solution)/shard_map/ppermute | solution.py:44
  26.3 4.4 %all_gather.63.from_a = f32[64,256]{1,0:T(8,128)S(1)} all-gather(f32[32,256]{1,0:T(8,128)S(1)} %get-tuple-element.89), channel_id=1, replica_groups={{0,16},{1,17},{2,18},{3,19},{4,20},{5,21},{6,22},{7,23},{8,24},{9,25},{..., dimensions={0}, use_global_device_ids=true | all-gather | bytes 98304 | tf_op jit(solution)/shard_map/all_gather | solution.py:60
  30.7 5.6 %all_gather.64.theirs = f32[128,256]{1,0:T(8,128)S(1)} all-gather(f32[64,256]{1,0:T(8,128)S(1)} %shard_map.100.mine), channel_id=1, replica_groups={{16,32},{17,33},{18,34},{19,35},{20,36},{21,37},{22,38},{23,39},{24,40}..., dimensions={0}, use_global_device_ids=true | all-gather | bytes 196608 | tf_op jit(solution)/shard_map/all_gather | solution.py:60
  36.4 1.8 %all_gather.65.sol_a = f32[64,256]{1,0:T(8,128)S(1)} all-gather(f32[32,256]{1,0:T(8,128)S(1)} %get-tuple-element.90.sol), channel_id=1, replica_groups={{0,16},{1,17},{2,18},{3,19},{4,20},{5,21},{6,22},{7,23},{8,24},{9,25},{..., dimensions={0}, use_global_device_ids=true | all-gather | bytes 98304 | tf_op jit(solution)/shard_map/all_gather | solution.py:60
  39.3 3.8 %collective-permute-start.4 = (f32[192,256]{1,0:T(8,128)S(1)}, f32[192,256]{1,0:T(8,128)S(1)}, u32[]{:S(2)}, u32[]{:S(2)}) collective-permute-start(f32[192,256]{1,0:T(8,128)S(1)} %get-tuple-element.94), channel_id=1, source_target_pairs={{16,32},{17,33},{18,34},{19,35},{20,36},{21,37},{22,38},{23,39},{2... | collective-permute-start | bytes 589832 | tf_op jit(solution)/shard_map/ppermute | solution.py:44
  43.1 2.1 %all_gather.66.ra = f32[384,256]{1,0:T(8,128)S(1)} all-gather(f32[192,256]{1,0:T(8,128)S(1)} %get-tuple-element.93), channel_id=1, replica_groups={{0,16},{1,17},{2,18},{3,19},{4,20},{5,21},{6,22},{7,23},{8,24},{9,25},{..., dimensions={0}, use_global_device_ids=true | all-gather | bytes 589824 | tf_op jit(solution)/shard_map/all_gather | solution.py:60
  45.2 2.3 %collective-permute-done.4.rb = f32[192,256]{1,0:T(8,128)S(1)} collective-permute-done((f32[192,256]{1,0:T(8,128)S(1)}, f32[192,256]{1,0:T(8,128)S(1)}, u32[]{:S(2)}, u32[]{:S(2)}) %collective-permute-start.4) | collective-permute-done | bytes 196640 | tf_op jit(solution)/shard_map/ppermute | solution.py:44
  47.5 1.9 %collective-permute-start.5 = (f32[192,256]{1,0:T(8,128)S(1)}, f32[192,256]{1,0:T(8,128)S(1)}, u32[]{:S(2)}, u32[]{:S(2)}) collective-permute-start(f32[192,256]{1,0:T(8,128)S(1)} %get-tuple-element.98), channel_id=1, source_target_pairs={{1,2},{2,1},{3,4},{4,3},{5,6},{6,5},{7,8},{8,7},{9,10},{10,9},{11,... | collective-permute-start | bytes 589832 | tf_op jit(solution)/shard_map/ppermute | solution.py:44
  49.5 8.1 %all_gather.67.rc = f32[384,256]{1,0:T(8,128)S(1)} all-gather(f32[192,256]{1,0:T(8,128)S(1)} %get-tuple-element.97), channel_id=1, replica_groups={{0,1},{2,3},{4,5},{6,7},{8,9},{10,11},{12,13},{14,15},{17,18},{19,20},{..., dimensions={0}, use_global_device_ids=true | all-gather | bytes 589824 | tf_op jit(solution)/shard_map/all_gather | solution.py:60
  58.5 4.5 %collective-permute-start.6 = (f32[192,256]{1,0:T(8,128)S(1)}, f32[192,256]{1,0:T(8,128)S(1)}, u32[]{:S(2)}, u32[]{:S(2)}) collective-permute-start(f32[192,256]{1,0:T(8,128)S(1)} %get-tuple-element.103), channel_id=1, source_target_pairs={{16,32},{17,33},{18,34},{19,35},{20,36},{21,37},{22,38},{23,39},{2... | collective-permute-start | bytes 589832 | tf_op jit(solution)/shard_map/ppermute | solution.py:44
  63.0 2.1 %all_gather.68.ra = f32[384,256]{1,0:T(8,128)S(1)} all-gather(f32[192,256]{1,0:T(8,128)S(1)} %get-tuple-element.102), channel_id=1, replica_groups={{0,16},{1,17},{2,18},{3,19},{4,20},{5,21},{6,22},{7,23},{8,24},{9,25},{..., dimensions={0}, use_global_device_ids=true | all-gather | bytes 589824 | tf_op jit(solution)/shard_map/all_gather | solution.py:60
  65.1 1.6 collective-permute-done.6.rb
  66.7 1.9 %collective-permute-start.7 = (f32[192,256]{1,0:T(8,128)S(1)}, f32[192,256]{1,0:T(8,128)S(1)}, u32[]{:S(2)}, u32[]{:S(2)}) collective-permute-start(f32[192,256]{1,0:T(8,128)S(1)} %get-tuple-element.107), channel_id=1, source_target_pairs={{1,2},{2,1},{3,4},{4,3},{5,6},{6,5},{7,8},{8,7},{9,10},{10,9},{11,... | collective-permute-start | bytes 589832 | tf_op jit(solution)/shard_map/ppermute | solution.py:44
  68.7 7.7 %all_gather.69.rc = f32[384,256]{1,0:T(8,128)S(1)} all-gather(f32[192,256]{1,0:T(8,128)S(1)} %get-tuple-element.106), channel_id=1, replica_groups={{0,1},{2,3},{4,5},{6,7},{8,9},{10,11},{12,13},{14,15},{17,18},{19,20},{..., dimensions={0}, use_global_device_ids=true | all-gather | bytes 589824 | tf_op jit(solution)/shard_map/all_gather | solution.py:60
  77.2 1.9 %all_gather.70.from_a = f32[64,256]{1,0:T(8,128)S(1)} all-gather(f32[32,256]{1,0:T(8,128)S(1)} %get-tuple-element.110), channel_id=1, replica_groups={{0,16},{1,17},{2,18},{3,19},{4,20},{5,21},{6,22},{7,23},{8,24},{9,25},{..., dimensions={0}, use_global_device_ids=true | all-gather | bytes 98304 | tf_op jit(solution)/shard_map/all_gather | solution.py:60
  79.0 5.8 %all_gather.71.theirs = f32[128,256]{1,0:T(8,128)S(1)} all-gather(f32[64,256]{1,0:T(8,128)S(1)} %shard_map.107.mine), channel_id=1, replica_groups={{16,32},{17,33},{18,34},{19,35},{20,36},{21,37},{22,38},{23,39},{24,40}..., dimensions={0}, use_global_device_ids=true | all-gather | bytes 196608 | tf_op jit(solution)/shard_map/all_gather | solution.py:60
  85.1 1.8 %all_gather.72.sol_a = f32[64,256]{1,0:T(8,128)S(1)} all-gather(f32[32,256]{1,0:T(8,128)S(1)} %get-tuple-element.111.sol), channel_id=1, replica_groups={{0,16},{1,17},{2,18},{3,19},{4,20},{5,21},{6,22},{7,23},{8,24},{9,25},{..., dimensions={0}, use_global_device_ids=true | all-gather | bytes 98304 | tf_op jit(solution)/shard_map/all_gather | solution.py:60
  87.9 4.9 %collective-permute-start.8 = (f32[192,256]{1,0:T(8,128)S(1)}, f32[192,256]{1,0:T(8,128)S(1)}, u32[]{:S(2)}, u32[]{:S(2)}) collective-permute-start(f32[192,256]{1,0:T(8,128)S(1)} %get-tuple-element.115), channel_id=1, source_target_pairs={{16,32},{17,33},{18,34},{19,35},{20,36},{21,37},{22,38},{23,39},{2... | collective-permute-start | bytes 589832 | tf_op jit(solution)/shard_map/ppermute | solution.py:44
  92.8 2.1 %all_gather.73.ra = f32[384,256]{1,0:T(8,128)S(1)} all-gather(f32[192,256]{1,0:T(8,128)S(1)} %get-tuple-element.114), channel_id=1, replica_groups={{0,16},{1,17},{2,18},{3,19},{4,20},{5,21},{6,22},{7,23},{8,24},{9,25},{..., dimensions={0}, use_global_device_ids=true | all-gather | bytes 589824 | tf_op jit(solution)/shard_map/all_gather | solution.py:60
  94.9 1.3 collective-permute-done.8.rb
  96.2 1.9 %collective-permute-start.9 = (f32[192,256]{1,0:T(8,128)S(1)}, f32[192,256]{1,0:T(8,128)S(1)}, u32[]{:S(2)}, u32[]{:S(2)}) collective-permute-start(f32[192,256]{1,0:T(8,128)S(1)} %get-tuple-element.119), channel_id=1, source_target_pairs={{1,2},{2,1},{3,4},{4,3},{5,6},{6,5},{7,8},{8,7},{9,10},{10,9},{11,... | collective-permute-start | bytes 589832 | tf_op jit(solution)/shard_map/ppermute | solution.py:44
  98.1 8.1 %all_gather.74.rc = f32[384,256]{1,0:T(8,128)S(1)} all-gather(f32[192,256]{1,0:T(8,128)S(1)} %get-tuple-element.118), channel_id=1, replica_groups={{0,1},{2,3},{4,5},{6,7},{8,9},{10,11},{12,13},{14,15},{17,18},{19,20},{..., dimensions={0}, use_global_device_ids=true | all-gather | bytes 589824 | tf_op jit(solution)/shard_map/all_gather | solution.py:60
  107.1 5.8 %collective-permute-start.10 = (f32[192,256]{1,0:T(8,128)S(1)}, f32[192,256]{1,0:T(8,128)S(1)}, u32[]{:S(2)}, u32[]{:S(2)}) collective-permute-start(f32[192,256]{1,0:T(8,128)S(1)} %get-tuple-element.124), channel_id=1, source_target_pairs={{16,32},{17,33},{18,34},{19,35},{20,36},{21,37},{22,38},{23,39},{2... | collective-permute-start | bytes 589832 | tf_op jit(solution)/shard_map/ppermute | solution.py:44
  112.9 2.1 %all_gather.75.ra = f32[384,256]{1,0:T(8,128)S(1)} all-gather(f32[192,256]{1,0:T(8,128)S(1)} %get-tuple-element.123), channel_id=1, replica_groups={{0,16},{1,17},{2,18},{3,19},{4,20},{5,21},{6,22},{7,23},{8,24},{9,25},{..., dimensions={0}, use_global_device_ids=true | all-gather | bytes 589824 | tf_op jit(solution)/shard_map/all_gather | solution.py:60
  115.0 1.3 collective-permute-done.10.rb
  116.3 1.9 %collective-permute-start.11 = (f32[192,256]{1,0:T(8,128)S(1)}, f32[192,256]{1,0:T(8,128)S(1)}, u32[]{:S(2)}, u32[]{:S(2)}) collective-permute-start(f32[192,256]{1,0:T(8,128)S(1)} %get-tuple-element.128), channel_id=1, source_target_pairs={{1,2},{2,1},{3,4},{4,3},{5,6},{6,5},{7,8},{8,7},{9,10},{10,9},{11,... | collective-permute-start | bytes 589832 | tf_op jit(solution)/shard_map/ppermute | solution.py:44
  118.2 8.1 %all_gather.76.rc = f32[384,256]{1,0:T(8,128)S(1)} all-gather(f32[192,256]{1,0:T(8,128)S(1)} %get-tuple-element.127), channel_id=1, replica_groups={{0,1},{2,3},{4,5},{6,7},{8,9},{10,11},{12,13},{14,15},{17,18},{19,20},{..., dimensions={0}, use_global_device_ids=true | all-gather | bytes 589824 | tf_op jit(solution)/shard_map/all_gather | solution.py:60
  127.1 1.9 %all_gather.77.from_a = f32[64,256]{1,0:T(8,128)S(1)} all-gather(f32[32,256]{1,0:T(8,128)S(1)} %get-tuple-element.131), channel_id=1, replica_groups={{0,16},{1,17},{2,18},{3,19},{4,20},{5,21},{6,22},{7,23},{8,24},{9,25},{..., dimensions={0}, use_global_device_ids=true | all-gather | bytes 98304 | tf_op jit(solution)/shard_map/all_gather | solution.py:60
  129.0 6.0 %all_gather.78.theirs = f32[128,256]{1,0:T(8,128)S(1)} all-gather(f32[64,256]{1,0:T(8,128)S(1)} %shard_map.114.mine), channel_id=1, replica_groups={{16,32},{17,33},{18,34},{19,35},{20,36},{21,37},{22,38},{23,39},{24,40}..., dimensions={0}, use_global_device_ids=true | all-gather | bytes 196608 | tf_op jit(solution)/shard_map/all_gather | solution.py:60
  135.2 1.8 %all_gather.79.sol_a = f32[64,256]{1,0:T(8,128)S(1)} all-gather(f32[32,256]{1,0:T(8,128)S(1)} %get-tuple-element.132.sol), channel_id=1, replica_groups={{0,16},{1,17},{2,18},{3,19},{4,20},{5,21},{6,22},{7,23},{8,24},{9,25},{..., dimensions={0}, use_global_device_ids=true | all-gather | bytes 98304 | tf_op jit(solution)/shard_map/all_gather | solution.py:60
  138.0 4.9 %collective-permute-start.12 = (f32[192,256]{1,0:T(8,128)S(1)}, f32[192,256]{1,0:T(8,128)S(1)}, u32[]{:S(2)}, u32[]{:S(2)}) collective-permute-start(f32[192,256]{1,0:T(8,128)S(1)} %get-tuple-element.136), channel_id=1, source_target_pairs={{16,32},{17,33},{18,34},{19,35},{20,36},{21,37},{22,38},{23,39},{2... | collective-permute-start | bytes 589832 | tf_op jit(solution)/shard_map/ppermute | solution.py:44
  142.9 2.1 %all_gather.80.ra = f32[384,256]{1,0:T(8,128)S(1)} all-gather(f32[192,256]{1,0:T(8,128)S(1)} %get-tuple-element.135), channel_id=1, replica_groups={{0,16},{1,17},{2,18},{3,19},{4,20},{5,21},{6,22},{7,23},{8,24},{9,25},{..., dimensions={0}, use_global_device_ids=true | all-gather | bytes 589824 | tf_op jit(solution)/shard_map/all_gather | solution.py:60
  145.0 1.3 collective-permute-done.12.rb
  146.3 1.9 %collective-permute-start.13 = (f32[192,256]{1,0:T(8,128)S(1)}, f32[192,256]{1,0:T(8,128)S(1)}, u32[]{:S(2)}, u32[]{:S(2)}) collective-permute-start(f32[192,256]{1,0:T(8,128)S(1)} %get-tuple-element.140), channel_id=1, source_target_pairs={{1,2},{2,1},{3,4},{4,3},{5,6},{6,5},{7,8},{8,7},{9,10},{10,9},{11,... | collective-permute-start | bytes 589832 | tf_op jit(solution)/shard_map/ppermute | solution.py:44
  148.2 8.1 %all_gather.81.rc = f32[384,256]{1,0:T(8,128)S(1)} all-gather(f32[192,256]{1,0:T(8,128)S(1)} %get-tuple-element.139), channel_id=1, replica_groups={{0,1},{2,3},{4,5},{6,7},{8,9},{10,11},{12,13},{14,15},{17,18},{19,20},{..., dimensions={0}, use_global_device_ids=true | all-gather | bytes 589824 | tf_op jit(solution)/shard_map/all_gather | solution.py:60
  157.2 5.6 %collective-permute-start.14 = (f32[192,256]{1,0:T(8,128)S(1)}, f32[192,256]{1,0:T(8,128)S(1)}, u32[]{:S(2)}, u32[]{:S(2)}) collective-permute-start(f32[192,256]{1,0:T(8,128)S(1)} %get-tuple-element.146), channel_id=1, source_target_pairs={{16,32},{17,33},{18,34},{19,35},{20,36},{21,37},{22,38},{23,39},{2... | collective-permute-start | bytes 589832 | tf_op jit(solution)/shard_map/ppermute | solution.py:44
  162.9 2.0 %shard_map.119 = (f32[768,256]{1,0:T(8,128)}, f32[8,128]{1,0:T(8,128)S(1)}) custom-call(s32[1,768]{1,0:T(1,128)S(1)} %bitcast.24, f32[768,256]{1,0:T(8,128)S(1)} %get-tuple-element.99.old.one, f32[768,256]{1,0:T(8,128)S(1)} %get-tuple-element.120.old.two, f32[768,256]{1,0:T(8,128)S(1)} %get-tuple-element.141.three), custom_call_target="tpu_custom_call" | custom-call | flops 603979776 | bytes 3152896 | tf_op jit(solution)/shard_map/pallas_call | solution.py:311
  164.9 2.1 %all_gather.82.ra = f32[384,256]{1,0:T(8,128)S(1)} all-gather(f32[192,256]{1,0:T(8,128)S(1)} %get-tuple-element.145), channel_id=1, replica_groups={{0,16},{1,17},{2,18},{3,19},{4,20},{5,21},{6,22},{7,23},{8,24},{9,25},{..., dimensions={0}, use_global_device_ids=true | all-gather | bytes 589824 | tf_op jit(solution)/shard_map/all_gather | solution.py:60
  167.0 1.9 %collective-permute-start.15 = (f32[192,256]{1,0:T(8,128)S(1)}, f32[192,256]{1,0:T(8,128)S(1)}, u32[]{:S(2)}, u32[]{:S(2)}) collective-permute-start(f32[192,256]{1,0:T(8,128)S(1)} %get-tuple-element.151), channel_id=1, source_target_pairs={{1,2},{2,1},{3,4},{4,3},{5,6},{6,5},{7,8},{8,7},{9,10},{10,9},{11,... | collective-permute-start | bytes 589832 | tf_op jit(solution)/shard_map/ppermute | solution.py:44
  168.9 9.5 %all_gather.83.rc = f32[384,256]{1,0:T(8,128)S(1)} all-gather(f32[192,256]{1,0:T(8,128)S(1)} %get-tuple-element.150), channel_id=1, replica_groups={{0,1},{2,3},{4,5},{6,7},{8,9},{10,11},{12,13},{14,15},{17,18},{19,20},{..., dimensions={0}, use_global_device_ids=true | all-gather | bytes 589824 | tf_op jit(solution)/shard_map/all_gather | solution.py:60
  178.4 2.3 %shard_map.121 = f32[768,256]{1,0:T(8,128)} custom-call(s32[8,128]{1,0:T(8,128)S(1)} %copy-done.1, s32[1,768]{1,0:T(1,128)S(1)} %bitcast.25, f32[768,256]{1,0:T(8,128)S(1)} %get-tuple-element.143.old, f32[768,256]{1,0:T(8,128)S(1)} %get-tuple-element.144.product, f32[384,256]{1,0:T(8,128)S(1)} %all_gather.82.ra, f32[192,256]{1,0:T(8,128)S(1)} %collective-permute-done.14.rb, ...), custom_call_target="tpu_custom_call" | custom-call | flops 603979776 | bytes 3546112 | tf_op jit(solution)/shard_map/pallas_call | solution.py:311
  (53 shorter events, 9.3 us)
Async XLA Ops:
  0.6 11.0 %copy-start.9 = (bf16[1,1,768,32]{2,3,1,0:T(8,128)(2,1)S(1)}, bf16[1,1,768,32]{2,3,1,0:T(8,128)(2,1)}, u32[]{:S(2)}) copy-start(bf16[1,1,768,32]{2,3,1,0:T(8,128)(2,1)} %param.11) | copy-start | bytes 147460
  0.6 11.1 %copy-start.6 = (s32[1,1,768]{2,1,0:T(1,128)S(1)}, s32[1,1,768]{2,1,0:T(1,128)}, u32[]{:S(2)}) copy-start(s32[1,1,768]{2,1,0:T(1,128)} %param.15) | copy-start | bytes 9220
  0.7 11.1 %copy-start.7 = (bf16[1,1,768,768]{3,2,1,0:T(8,128)(2,1)S(1)}, bf16[1,1,768,768]{3,2,1,0:T(8,128)(2,1)}, u32[]{:S(2)}) copy-start(bf16[1,1,768,768]{3,2,1,0:T(8,128)(2,1)} %param.10) | copy-start | bytes 3538948
  4.3 10.2 %collective-permute-start.1 = (f32[224,256]{1,0:T(8,128)}, f32[224,256]{1,0:T(8,128)S(1)}, u32[]{:S(2)}, u32[]{:S(2)}) collective-permute-start(f32[224,256]{1,0:T(8,128)} %get-tuple-element.82), channel_id=1, source_target_pairs={{0,496},{1,497},{2,498},{3,499},{4,500},{5,501},{6,502},{7,503},{8... | collective-permute-start | bytes 688136 | tf_op jit(solution)/shard_map/ppermute | solution.py:44
  9.7 4.9 %collective-permute-start = (f32[192,256]{1,0:T(8,128)}, f32[192,256]{1,0:T(8,128)S(1)}, u32[]{:S(2)}, u32[]{:S(2)}) collective-permute-start(f32[192,256]{1,0:T(8,128)} %get-tuple-element.81), channel_id=1, source_target_pairs={{0,16},{1,17},{2,18},{3,19},{4,20},{5,21},{6,22},{7,23},{8,24},{9,... | collective-permute-start | bytes 589832 | tf_op jit(solution)/shard_map/ppermute | solution.py:44
  11.8 2.8 %copy-start.3 = (f32[64,256]{1,0:T(8,128)S(1)}, f32[64,256]{1,0:T(8,128)}, u32[]{:S(2)}) copy-start(f32[64,256]{1,0:T(8,128)} %get-tuple-element.83.c) | copy-start | bytes 196612
  11.8 2.8 %copy-start.4 = (f32[64,256]{1,0:T(8,128)S(1)}, f32[64,256]{1,0:T(8,128)}, u32[]{:S(2)}) copy-start(f32[64,256]{1,0:T(8,128)} %get-tuple-element.84.d) | copy-start | bytes 196612
  14.5 6.5 %copy-start.8 = (bf16[1,1,768,768]{3,2,1,0:T(8,128)(2,1)S(1)}, bf16[1,1,768,768]{3,2,1,0:T(8,128)(2,1)}, u32[]{:S(2)}) copy-start(bf16[1,1,768,768]{3,2,1,0:T(8,128)(2,1)} %param.9) | copy-start | bytes 3538948
  14.6 8.8 %collective-permute-start.2 = (f32[192,256]{1,0:T(8,128)S(1)}, f32[192,256]{1,0:T(8,128)S(1)}, u32[]{:S(2)}, u32[]{:S(2)}) collective-permute-start(f32[192,256]{1,0:T(8,128)S(1)} %get-tuple-element.85), channel_id=1, source_target_pairs={{0,1},{1,0},{2,3},{3,2},{4,5},{5,4},{6,7},{7,6},{8,9},{9,8},{10,11... | collective-permute-start | bytes 589832 | tf_op jit(solution)/shard_map/ppermute | solution.py:44
  19.0 6.4 %collective-permute-start.3 = (f32[192,256]{1,0:T(8,128)S(1)}, f32[192,256]{1,0:T(8,128)S(1)}, u32[]{:S(2)}, u32[]{:S(2)}) collective-permute-start(f32[192,256]{1,0:T(8,128)S(1)} %get-tuple-element.86), channel_id=1, source_target_pairs={{1,2},{2,1},{3,4},{4,3},{5,6},{6,5},{7,8},{8,7},{9,10},{10,9},{11,... | collective-permute-start | bytes 589832 | tf_op jit(solution)/shard_map/ppermute | solution.py:44
  21.0 4.4 %copy-start = (f32[768,256]{1,0:T(8,128)S(1)}, f32[768,256]{1,0:T(8,128)}, u32[]{:S(2)}) copy-start(f32[768,256]{1,0:T(8,128)} %get-tuple-element.80.old.product) | copy-start | bytes 2359300
  21.0 4.4 %copy-start.1 = (s32[8,128]{1,0:T(8,128)S(1)}, s32[8,128]{1,0:T(8,128)}, u32[]{:S(2)}) copy-start(s32[8,128]{1,0:T(8,128)} %get-tuple-element.77.table) | copy-start | bytes 12292
  21.0 4.4 %copy-start.5 = (s32[1,1,32]{2,1,0:T(1,128)S(1)}, s32[1,1,32]{2,1,0:T(1,128)}, u32[]{:S(2)}) copy-start(s32[1,1,32]{2,1,0:T(1,128)} %param.13) | copy-start | bytes 388
  25.4 10.8 %copy-start.2 = (f32[1,1,32,32]{3,2,1,0:T(8,128)S(1)}, f32[1,1,32,32]{3,2,1,0:T(8,128)}, u32[]{:S(2)}) copy-start(f32[1,1,32,32]{3,2,1,0:T(8,128)} %param.12) | copy-start | bytes 12292
  39.3 8.2 %collective-permute-start.4 = (f32[192,256]{1,0:T(8,128)S(1)}, f32[192,256]{1,0:T(8,128)S(1)}, u32[]{:S(2)}, u32[]{:S(2)}) collective-permute-start(f32[192,256]{1,0:T(8,128)S(1)} %get-tuple-element.94), channel_id=1, source_target_pairs={{16,32},{17,33},{18,34},{19,35},{20,36},{21,37},{22,38},{23,39},{2... | collective-permute-start | bytes 589832 | tf_op jit(solution)/shard_map/ppermute | solution.py:44
  47.5 10.0 %collective-permute-start.5 = (f32[192,256]{1,0:T(8,128)S(1)}, f32[192,256]{1,0:T(8,128)S(1)}, u32[]{:S(2)}, u32[]{:S(2)}) collective-permute-start(f32[192,256]{1,0:T(8,128)S(1)} %get-tuple-element.98), channel_id=1, source_target_pairs={{1,2},{2,1},{3,4},{4,3},{5,6},{6,5},{7,8},{8,7},{9,10},{10,9},{11,... | collective-permute-start | bytes 589832 | tf_op jit(solution)/shard_map/ppermute | solution.py:44
  58.5 8.2 %collective-permute-start.6 = (f32[192,256]{1,0:T(8,128)S(1)}, f32[192,256]{1,0:T(8,128)S(1)}, u32[]{:S(2)}, u32[]{:S(2)}) collective-permute-start(f32[192,256]{1,0:T(8,128)S(1)} %get-tuple-element.103), channel_id=1, source_target_pairs={{16,32},{17,33},{18,34},{19,35},{20,36},{21,37},{22,38},{23,39},{2... | collective-permute-start | bytes 589832 | tf_op jit(solution)/shard_map/ppermute | solution.py:44
  66.7 9.6 %collective-permute-start.7 = (f32[192,256]{1,0:T(8,128)S(1)}, f32[192,256]{1,0:T(8,128)S(1)}, u32[]{:S(2)}, u32[]{:S(2)}) collective-permute-start(f32[192,256]{1,0:T(8,128)S(1)} %get-tuple-element.107), channel_id=1, source_target_pairs={{1,2},{2,1},{3,4},{4,3},{5,6},{6,5},{7,8},{8,7},{9,10},{10,9},{11,... | collective-permute-start | bytes 589832 | tf_op jit(solution)/shard_map/ppermute | solution.py:44
  87.9 8.2 %collective-permute-start.8 = (f32[192,256]{1,0:T(8,128)S(1)}, f32[192,256]{1,0:T(8,128)S(1)}, u32[]{:S(2)}, u32[]{:S(2)}) collective-permute-start(f32[192,256]{1,0:T(8,128)S(1)} %get-tuple-element.115), channel_id=1, source_target_pairs={{16,32},{17,33},{18,34},{19,35},{20,36},{21,37},{22,38},{23,39},{2... | collective-permute-start | bytes 589832 | tf_op jit(solution)/shard_map/ppermute | solution.py:44
  96.2 10.0 %collective-permute-start.9 = (f32[192,256]{1,0:T(8,128)S(1)}, f32[192,256]{1,0:T(8,128)S(1)}, u32[]{:S(2)}, u32[]{:S(2)}) collective-permute-start(f32[192,256]{1,0:T(8,128)S(1)} %get-tuple-element.119), channel_id=1, source_target_pairs={{1,2},{2,1},{3,4},{4,3},{5,6},{6,5},{7,8},{8,7},{9,10},{10,9},{11,... | collective-permute-start | bytes 589832 | tf_op jit(solution)/shard_map/ppermute | solution.py:44
  107.1 9.1 %collective-permute-start.10 = (f32[192,256]{1,0:T(8,128)S(1)}, f32[192,256]{1,0:T(8,128)S(1)}, u32[]{:S(2)}, u32[]{:S(2)}) collective-permute-start(f32[192,256]{1,0:T(8,128)S(1)} %get-tuple-element.124), channel_id=1, source_target_pairs={{16,32},{17,33},{18,34},{19,35},{20,36},{21,37},{22,38},{23,39},{2... | collective-permute-start | bytes 589832 | tf_op jit(solution)/shard_map/ppermute | solution.py:44
  116.3 10.0 %collective-permute-start.11 = (f32[192,256]{1,0:T(8,128)S(1)}, f32[192,256]{1,0:T(8,128)S(1)}, u32[]{:S(2)}, u32[]{:S(2)}) collective-permute-start(f32[192,256]{1,0:T(8,128)S(1)} %get-tuple-element.128), channel_id=1, source_target_pairs={{1,2},{2,1},{3,4},{4,3},{5,6},{6,5},{7,8},{8,7},{9,10},{10,9},{11,... | collective-permute-start | bytes 589832 | tf_op jit(solution)/shard_map/ppermute | solution.py:44
  138.0 8.2 %collective-permute-start.12 = (f32[192,256]{1,0:T(8,128)S(1)}, f32[192,256]{1,0:T(8,128)S(1)}, u32[]{:S(2)}, u32[]{:S(2)}) collective-permute-start(f32[192,256]{1,0:T(8,128)S(1)} %get-tuple-element.136), channel_id=1, source_target_pairs={{16,32},{17,33},{18,34},{19,35},{20,36},{21,37},{22,38},{23,39},{2... | collective-permute-start | bytes 589832 | tf_op jit(solution)/shard_map/ppermute | solution.py:44
  146.3 10.0 %collective-permute-start.13 = (f32[192,256]{1,0:T(8,128)S(1)}, f32[192,256]{1,0:T(8,128)S(1)}, u32[]{:S(2)}, u32[]{:S(2)}) collective-permute-start(f32[192,256]{1,0:T(8,128)S(1)} %get-tuple-element.140), channel_id=1, source_target_pairs={{1,2},{2,1},{3,4},{4,3},{5,6},{6,5},{7,8},{8,7},{9,10},{10,9},{11,... | collective-permute-start | bytes 589832 | tf_op jit(solution)/shard_map/ppermute | solution.py:44
  157.2 9.7 %collective-permute-start.14 = (f32[192,256]{1,0:T(8,128)S(1)}, f32[192,256]{1,0:T(8,128)S(1)}, u32[]{:S(2)}, u32[]{:S(2)}) collective-permute-start(f32[192,256]{1,0:T(8,128)S(1)} %get-tuple-element.146), channel_id=1, source_target_pairs={{16,32},{17,33},{18,34},{19,35},{20,36},{21,37},{22,38},{23,39},{2... | collective-permute-start | bytes 589832 | tf_op jit(solution)/shard_map/ppermute | solution.py:44
  167.0 11.4 %collective-permute-start.15 = (f32[192,256]{1,0:T(8,128)S(1)}, f32[192,256]{1,0:T(8,128)S(1)}, u32[]{:S(2)}, u32[]{:S(2)}) collective-permute-start(f32[192,256]{1,0:T(8,128)S(1)} %get-tuple-element.151), channel_id=1, source_target_pairs={{1,2},{2,1},{3,4},{4,3},{5,6},{6,5},{7,8},{8,7},{9,10},{10,9},{11,... | collective-permute-start | bytes 589832 | tf_op jit(solution)/shard_map/ppermute | solution.py:44

commit v4 on v3

--- a/solution.py
+++ b/solution.py
@@ -96,10 +96,11 @@
     return [(table[0, k], table[0, 8 + k]) for k in range(8)]
 
 
-def to_sorted(order):
+def to_sorted(order, rows=None):
     n = order.shape[1]
-    column = jnp.transpose(jnp.broadcast_to(order, (128, n)))[:, :1]
-    return (lax.broadcasted_iota(jnp.int32, (n, n), 1) == column).astype(F32).astype(BF16)
+    rows = n if rows is None else rows
+    column = jnp.transpose(jnp.broadcast_to(order, (128, n)))[:rows, :1]
+    return (lax.broadcasted_iota(jnp.int32, (rows, n), 1) == column).astype(F32).astype(BF16)
 
 
 def from_sorted(order):
@@ -135,7 +136,7 @@
             d_ref[...] = rows
 
 
-def absorb(buf, groups, ra, rb, rc, rd):
+def absorb(buf, groups, factor, ra, rb, rc, rd):
     edge_a = half_of(ra, "A", 3 * MROW, MROW, MROW)
     pieces = [half_of(rc, "C", 3 * MROW, k * MROW, MROW) for k in range(3)]
     order = (pieces[0], edge_a, rd[0:64, :], pieces[2], rb[64:128, :], rd[128:192, :], pieces[1], rd[64:128, :])
@@ -143,14 +144,8 @@
     tail = jnp.zeros((TILE, buf.shape[1]), F32)
     for (start, count), piece in zip(groups, order):
         place, skip = window(start)
-        piece = jnp.concatenate([jnp.where(at < count, piece, 0.0), tail], axis=0)
+        piece = jnp.concatenate([jnp.where(at < count, factor * piece, 0.0), tail], axis=0)
         buf[place, :] = buf[place, :] + pltpu.roll(piece, skip, 0)
-
-
-def fill(buf, x):
-    n = x.shape[0]
-    buf[0:n, :] = x
-    buf[n:n + MROW + TILE, :] = jnp.zeros((MROW + TILE, x.shape[1]), F32)
 
 
 def weights(n, table):
@@ -170,17 +165,16 @@
     return jnp.concatenate(parts, axis=0)
 
 
-def k_first(counts_in, order_in, source_in, inverse_in, sorted_ref, table_ref, a_ref, b_ref, c_ref, d_ref,
-            buf, counts, order, source, inverse, arrived):
+def k_first(counts_in, order_in, source_in, table_ref, a_ref, b_ref, c_ref, d_ref,
+            top, counts, order, source, arrived):
     copies = [
         pltpu.make_async_copy(src, dst, arrived.at[k])
-        for k, (src, dst) in enumerate(
-            ((order_in, order), (counts_in, counts), (source_in, source), (inverse_in, inverse)))
+        for k, (src, dst) in enumerate(((order_in, order), (counts_in, counts), (source_in, source)))
     ]
     for copy in copies:
         copy.start()
     copies[0].wait()
-    onehot = to_sorted(order[...])
+    onehot = to_sorted(order[...], top.shape[0])
     copies[1].wait()
     starts, sizes, total = table_of(counts)
     at = lax.broadcasted_iota(jnp.int32, table_ref.shape, 1)
@@ -190,14 +184,12 @@
         table = jnp.where((row == 0) & (at == k), value, table)
     table_ref[...] = table
     copies[2].wait()
-    x = moved(onehot, source[...])
-    sorted_ref[...] = x
-    fill(buf, x)
-    emit(buf, list(zip(starts, sizes)), a_ref, b_ref, c_ref, d_ref)
-    n = inverse.shape[0]
-    copies[3].wait()
-    b_ref[3 * MROW:3 * MROW + n, :] = jnp.zeros((n, b_ref.shape[1]), F32)
-    b_ref[3 * MROW:3 * MROW + n, 0:n] = inverse[...]
+    top[...] = moved(onehot, source[...])
+    emit(top, list(zip(starts, sizes)), a_ref, b_ref, c_ref, d_ref)
+
+
+def k_source(order, source, out):
+    out[...] = moved(to_sorted(order[...]), source[...])
 
 
 def k_relay(ra, rb, c, d, *rest):
@@ -228,16 +220,11 @@
 
 def k_residual(first, peers, size, table, blocks, basis, old, product, ra, rb, rc, rd,
                *rest):
-    res_ref, scaled_ref, give_ref, keep_ref, buf = rest[-5:]
-    groups = groups_of(table)
-    if first:
-        fill(buf, old[...])
-    else:
-        fill(buf, product[...])
-    absorb(buf, groups, ra, rb, rc, rd)
+    res_ref, scaled_ref, give_ref, keep_ref = rest[-4:]
+    res_ref[...] = old[...] if first else old[...] - product[...]
+    absorb(res_ref, groups_of(table), 1.0 if first else -1.0, ra, rb, rc, rd)
     n = old.shape[0]
-    res = buf[0:n, :] if first else old[...] - buf[0:n, :]
-    res_ref[...] = res
+    res = res_ref[...]
     scaled = (weights(n, table) * res).astype(BF16)
     scaled_ref[...] = scaled
     primal = lax.dot_general(basis[...], scaled, (((0,), (0,)), ((), ())), preferred_element_type=F32)
@@ -248,22 +235,27 @@
     keep_ref[size:2 * size, :] = spread_out[2 * size:3 * size, :]
 
 
-def k_middle(size, kept, from_a, mine):
+def k_middle(size, kept, from_a, *rest):
+    mine = rest[-1]
     mine[0:size, :] = kept[0:size, :] + half_of(from_a, "A", size)
     mine[size:2 * size, :] = kept[size:2 * size, :]
-
-
-def k_coarse(size, inv, first_b, mine, theirs, own_ref, b_ref):
+    if len(rest) == 2:
+        mine[2 * size:3 * size, :] = jnp.zeros((size, mine.shape[1]), F32)
+        mine[2 * size:3 * size, 0:size] = rest[0][...]
+
+
+def k_coarse(size, inv, first, mine, theirs, own_ref, b_ref):
     dot = partial(jnp.dot, precision=HIGH, preferred_element_type=F32)
-    their_own = half_of(theirs, "B", 2 * size, 0, size)
-    their_mine = half_of(theirs, "B", 2 * size, size, size)
-    inv_b = first_b[3 * MROW:3 * MROW + size, 0:size]
+    rows = mine.shape[0]
+    their_own = half_of(theirs, "B", rows, 0, size)
+    their_mine = half_of(theirs, "B", rows, size, size)
+    inv_b = half_of(first, "B", 3 * size, 2 * size, size)[:, 0:size]
     own_ref[...] = dot(inv[...], mine[0:size, :] + their_mine)
     b_ref[...] = dot(inv_b, their_own + mine[size:2 * size, :])
 
 
 def k_update(peers, size, table, blocks, basis, matrix, scaled, sol, sol_a, sol_b,
-             up_ref, a_ref, b_ref, c_ref, d_ref, buf):
+             up_ref, a_ref, b_ref, c_ref, d_ref):
     groups = groups_of(table)
     select = chooser(blocks[...], peers, size)
     stack = jnp.concatenate([sol[...], half_of(sol_a, "A", size), sol_b[...]], axis=0)
@@ -273,36 +265,27 @@
     up = up + jnp.dot(basis[...], picked.astype(BF16), preferred_element_type=F32)
     up = weights(n, table) * up
     up_ref[...] = up
-    fill(buf, up)
-    emit(buf, groups, a_ref, b_ref, c_ref, d_ref)
-
-
-def k_apply(keep, gain, table, schur, up, old, ra, rb, rc, rd, dir_ref, v_ref, a_ref, b_ref, c_ref, d_ref, buf):
+    emit(up_ref, groups, a_ref, b_ref, c_ref, d_ref)
+
+
+def k_apply(keep, gain, table, schur, up, old, ra, rb, rc, rd, dir_ref, v_ref, a_ref, b_ref, c_ref, d_ref):
     groups = groups_of(table)
-    fill(buf, up[...])
-    absorb(buf, groups, ra, rb, rc, rd)
-    n = up.shape[0]
-    direction = gain * buf[0:n, :]
-    if keep is not None:
-        direction = keep * old[...] + direction
-    dir_ref[...] = direction
-    v = jnp.dot(schur[...], direction.astype(BF16), preferred_element_type=F32)
-    v_ref[...] = v
-    buf[0:n, :] = v
-    emit(buf, groups, a_ref, b_ref, c_ref, d_ref)
-
-
-def k_solution(order, one, two, three, out, token):
-    token[...] = jnp.zeros(token.shape, F32)
-    out[...] = moved(from_sorted(order[...]), one[...] + two[...] + three[...])
-
-
-def k_final(table, order, old, product, ra, rb, rc, rd, out, buf):
-    groups = groups_of(table)
-    fill(buf, product[...])
-    absorb(buf, groups, ra, rb, rc, rd)
-    n = old.shape[0]
-    out[...] = moved(from_sorted(order[...]), old[...] - buf[0:n, :])
+    own = gain * up[...]
+    dir_ref[...] = own if keep is None else keep * old[...] + own
+    absorb(dir_ref, groups, gain, ra, rb, rc, rd)
+    v_ref[...] = jnp.dot(schur[...], dir_ref[...].astype(BF16), preferred_element_type=F32)
+    emit(v_ref, groups, a_ref, b_ref, c_ref, d_ref)
+
+
+def k_solution(order, one, two, three, out, back):
+    back[...] = from_sorted(order[...])
+    out[...] = moved(back[...], one[...] + two[...] + three[...])
+
+
+def k_final(table, back, old, product, ra, rb, rc, rd, out, buf):
+    buf[...] = old[...] - product[...]
+    absorb(buf, groups_of(table), -1.0, ra, rb, rc, rd)
+    out[...] = moved(back[...], buf[...])
 
 
 def call(kernel, ins, outs, flops, scratch=(), far=0, after=(), room=28):
@@ -321,8 +304,8 @@
 
 def exchange(a, b, c, d, first=False, beside=()):
     leg = jax.ShapeDtypeStruct((3 * MROW, c.shape[1]), F32)
-    rb = swap(b, "B", first)
-    ra = swap(a, "A") if first else pair(a, "A")
+    rb = swap(b, "B")
+    ra = pair(a, "A")
     to_c, to_d = call(k_relay, (ra, rb, c, d), [leg, leg], 0, after=beside)
     rd = swap(to_d, "D")
     rc = swap(to_c, "C") if first else pair(to_c, "C")
@@ -344,27 +327,27 @@
     b16 = lambda *shape: jax.ShapeDtypeStruct(shape, BF16)
     full = f32(n, cols)
     sent = [f32(3 * MROW, cols), f32(3 * MROW, cols), f32(MROW, cols), f32(MROW, cols)]
-    buf = [pltpu.VMEM((n + MROW + TILE, cols), F32)]
     big = 2 * n * n * cols
 
-    src, table, *out = call(
+    shared = 9 * MROW
+    table, *out = call(
         k_first,
-        (counts, order, source, inv),
-        [full, jax.ShapeDtypeStruct((8, 128), jnp.int32), sent[0], f32(3 * MROW + size, cols), sent[2], sent[3]],
+        (counts, order, source),
+        [jax.ShapeDtypeStruct((8, 128), jnp.int32)] + sent,
         2 * big,
-        buf + [
-            pltpu.SMEM((8,), jnp.int32), pltpu.VMEM(order.shape, jnp.int32), pltpu.VMEM((n, cols), F32),
-            pltpu.VMEM((size, size), F32), pltpu.SemaphoreType.DMA((4,)),
+        [
+            pltpu.VMEM((shared, cols), F32), pltpu.SMEM((8,), jnp.int32), pltpu.VMEM(order.shape, jnp.int32),
+            pltpu.VMEM((n, cols), F32), pltpu.SemaphoreType.DMA((3,)),
         ],
-        4, (), 62,
+        3, (), 62,
     )
+    src, = call(k_source, (order, source), [full], 3 * big)
     onehot = [pltpu.VMEM((n, n), BF16)]
     a_s, basis = call(
         k_sort, (order, local_inverse[0, 0], primal_basis[0, 0]), [b16(n, n), b16(n, modes)], 4 * n * n * n, onehot,
     )
     s_s, = call(k_sort, (order, schur[0, 0]), [b16(n, n)], 4 * n * n * n, onehot)
     got = exchange(*out, first=True, beside=(a_s,))
-    first_b = got[1]
 
     res, product, direction = src, src, src
     directions = []
@@ -375,20 +358,22 @@
             partial(k_residual, step == 0, peers, size),
             (table, blocks, basis, res, product, *got),
             [full, b16(n, cols), f32(size, cols), f32(2 * size, cols)],
-            2 * n * modes * cols, buf, after=(s_s,) if step == 0 else (),
+            2 * n * modes * cols, after=(s_s,) if step == 0 else (),
         )
         from_a = pair(give, "A")
-        mine, = call(partial(k_middle, size), (kept, from_a), [f32(2 * size, cols)], 0)
+        extra = (inv,) if step == 0 else ()
+        mine, = call(partial(k_middle, size), (kept, from_a) + extra, [f32((2 + len(extra)) * size, cols)], 0)
         theirs = pair(mine, "B")
+        first = theirs if step == 0 else first
         sol, sol_b = call(
-            partial(k_coarse, size), (inv, first_b, mine, theirs), [f32(size, cols), f32(size, cols)],
+            partial(k_coarse, size), (inv, first, mine, theirs), [f32(size, cols), f32(size, cols)],
             4 * size * size * cols,
         )
         sol_a = pair(sol, "A")
         up, *out = call(
             partial(k_update, peers, size),
             (table, blocks, basis, a_s, scaled, sol, sol_a, sol_b),
-            [full] + sent, big, buf,
+            [full] + sent, big,
         )
         got = exchange(*out)
         if step == 0:
@@ -400,15 +385,15 @@
         direction, product, *out = call(
             partial(k_apply, keep, gain),
             (table, s_s, up, direction, *got),
-            [full, full] + sent, big, buf,
+            [full, full] + sent, big,
         )
         directions.append(direction)
         beside = ()
         if step == ITERS - 1:
-            total, token = call(k_solution, (order, *directions), [full, f32(8, 128)], 2 * big)
-            beside = (token,)
+            total, back = call(k_solution, (order, *directions), [full, b16(n, n)], 3 * big)
+            beside = (back,)
         got = exchange(*out, beside=beside)
-    residual, = call(k_final, (table, order, res, product, *got), [full], 2 * big, buf)
+    residual, = call(k_final, (table, back, res, product, *got), [full], 3 * big, [pltpu.VMEM((n, cols), F32)])
     return total[None, None], residual[None, None]
 
 

time: 181 us -> 181 us (level)
  the two profiles are of different devices: /device:TPU:105 before, /device:TPU:121 now
where the time goes in v4:
time: 181 us
  blocking collectives  94.9 us (52%)
  starting transfers between devices  52.9 us (29%)
  Pallas kernels  23.2 us (13%)
  waiting for transfers between devices  8.5 us (5%)
    all_gather x22, blocking collectives, pair(): return lax.all_gather(x, ('sx', 'sy'), axis_index_groups=pairs, tiled=True)  94.9 us
    ppermute x15, starting transfers between devices, swap(): return lax.ppermute(x, ('sx', 'sy'), pairs)  52.9 us
    pallas_call x28, Pallas kernels, call(): pl.pallas_call(kernel, out_shape=tuple(outs), in_specs=[FAR] * far + [VME...  23.2 us
    ppermute x15, waiting for transfers between devices, swap(): return lax.ppermute(x, ('sx', 'sy'), pairs)  8.5 us
  transfers between devices with their start and end apart: 15, of which 6 were waited for; matrix products, arithmetic and copies ran while one was open for 0% of the time, Pallas kernels for 5%

profile of v4, /device:TPU:121, one launch (start us, length us, event | category | flops | bytes accessed | tf_op | source)
XLA Modules:
  0.0 180.7 jit_solution(13844728286940732144)
XLA Ops:
  0.7 3.0 %shard_map.95 = (s32[8,128]{1,0:T(8,128)}, f32[192,256]{1,0:T(8,128)}, f32[192,256]{1,0:T(8,128)}, f32[64,256]{1,0:T(8,128)}, f32[64,256]{1,0:T(8,128)}) custom-call(s32[8]{0:T(128)} %bitcast.31, s32[1,768]{1,0:T(1,128)} %bitcast.25, f32[768,256]{1,0:T(8,128)} %bitcast.23), custom_call_target="tpu_custom_call" | custom-call | flops 603979776 | bytes 1317920 | tf_op jit(solution)/shard_map/pallas_call | solution.py:294
  3.7 5.3 %collective-permute-start = (f32[192,256]{1,0:T(8,128)}, f32[192,256]{1,0:T(8,128)S(1)}, u32[]{:S(2)}, u32[]{:S(2)}) collective-permute-start(f32[192,256]{1,0:T(8,128)} %get-tuple-element.80), channel_id=1, source_target_pairs={{16,32},{17,33},{18,34},{19,35},{20,36},{21,37},{22,38},{23,39},{2... | collective-permute-start | bytes 589832 | tf_op jit(solution)/shard_map/ppermute | solution.py:44
  9.0 2.3 %all_gather.66.ra = f32[384,256]{1,0:T(8,128)S(1)} all-gather(f32[192,256]{1,0:T(8,128)} %get-tuple-element.79), channel_id=1, replica_groups={{0,16},{1,17},{2,18},{3,19},{4,20},{5,21},{6,22},{7,23},{8,24},{9,25},{..., dimensions={0}, use_global_device_ids=true | all-gather | bytes 589824 | tf_op jit(solution)/shard_map/all_gather | solution.py:60
  11.5 2.7 %shard_map.97 = (bf16[768,768]{1,0:T(8,128)(2,1)S(1)}, bf16[768,32]{1,0:T(8,128)(2,1)S(1)}) custom-call(s32[1,768]{1,0:T(1,128)S(1)} %bitcast.26, bf16[768,768]{1,0:T(8,128)(2,1)S(1)} %bitcast.21, bf16[768,32]{1,0:T(8,128)(2,1)S(1)} %bitcast.14), custom_call_target="tpu_custom_call" | custom-call | flops 1811939328 | bytes 2460672 | tf_op jit(solution)/shard_map/pallas_call | solution.py:294
  14.3 4.7 %collective-permute-start.1 = (f32[192,256]{1,0:T(8,128)S(1)}, f32[192,256]{1,0:T(8,128)S(1)}, u32[]{:S(2)}, u32[]{:S(2)}) collective-permute-start(f32[192,256]{1,0:T(8,128)S(1)} %get-tuple-element.83), channel_id=1, source_target_pairs={{0,1},{1,0},{2,3},{3,2},{4,5},{5,4},{6,7},{7,6},{8,9},{9,8},{10,11... | collective-permute-start | bytes 589832 | tf_op jit(solution)/shard_map/ppermute | solution.py:44
  19.0 2.1 %collective-permute-start.2 = (f32[192,256]{1,0:T(8,128)S(1)}, f32[192,256]{1,0:T(8,128)S(1)}, u32[]{:S(2)}, u32[]{:S(2)}) collective-permute-start(f32[192,256]{1,0:T(8,128)S(1)} %get-tuple-element.84), channel_id=1, source_target_pairs={{1,2},{2,1},{3,4},{4,3},{5,6},{6,5},{7,8},{8,7},{9,10},{10,9},{11,... | collective-permute-start | bytes 589832 | tf_op jit(solution)/shard_map/ppermute | solution.py:44
  21.0 1.4 shard_map.98.old.product
  22.5 2.3 %shard_map.96.rest_0_.schur = bf16[768,768]{1,0:T(8,128)(2,1)S(1)} custom-call(s32[1,768]{1,0:T(1,128)S(1)} %bitcast.28, bf16[768,768]{1,0:T(8,128)(2,1)S(1)} %bitcast.22), custom_call_target="tpu_custom_call" | custom-call | flops 1811939328 | bytes 2362368 | tf_op jit(solution)/shard_map/pallas_call | solution.py:294
  26.6 3.4 %all_gather.67.from_a = f32[64,256]{1,0:T(8,128)S(1)} all-gather(f32[32,256]{1,0:T(8,128)S(1)} %get-tuple-element.87), channel_id=1, replica_groups={{0,16},{1,17},{2,18},{3,19},{4,20},{5,21},{6,22},{7,23},{8,24},{9,25},{..., dimensions={0}, use_global_device_ids=true | all-gather | bytes 98304 | tf_op jit(solution)/shard_map/all_gather | solution.py:60
  30.1 5.9 %all_gather.68.first.theirs = f32[192,256]{1,0:T(8,128)S(1)} all-gather(f32[96,256]{1,0:T(8,128)S(1)} %shard_map.101.mine), channel_id=1, replica_groups={{16,32},{17,33},{18,34},{19,35},{20,36},{21,37},{22,38},{23,39},{24,40}..., dimensions={0}, use_global_device_ids=true | all-gather | bytes 294912 | tf_op jit(solution)/shard_map/all_gather | solution.py:60
  36.2 1.9 %all_gather.69.sol_a = f32[64,256]{1,0:T(8,128)S(1)} all-gather(f32[32,256]{1,0:T(8,128)S(1)} %get-tuple-element.88.sol), channel_id=1, replica_groups={{0,16},{1,17},{2,18},{3,19},{4,20},{5,21},{6,22},{7,23},{8,24},{9,25},{..., dimensions={0}, use_global_device_ids=true | all-gather | bytes 98304 | tf_op jit(solution)/shard_map/all_gather | solution.py:60
  39.1 3.8 %collective-permute-start.3 = (f32[192,256]{1,0:T(8,128)S(1)}, f32[192,256]{1,0:T(8,128)S(1)}, u32[]{:S(2)}, u32[]{:S(2)}) collective-permute-start(f32[192,256]{1,0:T(8,128)S(1)} %get-tuple-element.92), channel_id=1, source_target_pairs={{16,32},{17,33},{18,34},{19,35},{20,36},{21,37},{22,38},{23,39},{2... | collective-permute-start | bytes 589832 | tf_op jit(solution)/shard_map/ppermute | solution.py:44
  42.9 2.1 %all_gather.70.ra = f32[384,256]{1,0:T(8,128)S(1)} all-gather(f32[192,256]{1,0:T(8,128)S(1)} %get-tuple-element.91), channel_id=1, replica_groups={{0,16},{1,17},{2,18},{3,19},{4,20},{5,21},{6,22},{7,23},{8,24},{9,25},{..., dimensions={0}, use_global_device_ids=true | all-gather | bytes 589824 | tf_op jit(solution)/shard_map/all_gather | solution.py:60
  45.0 2.3 %collective-permute-done.3.rb = f32[192,256]{1,0:T(8,128)S(1)} collective-permute-done((f32[192,256]{1,0:T(8,128)S(1)}, f32[192,256]{1,0:T(8,128)S(1)}, u32[]{:S(2)}, u32[]{:S(2)}) %collective-permute-start.3) | collective-permute-done | bytes 196640 | tf_op jit(solution)/shard_map/ppermute | solution.py:44
  47.3 1.9 %collective-permute-start.4 = (f32[192,256]{1,0:T(8,128)S(1)}, f32[192,256]{1,0:T(8,128)S(1)}, u32[]{:S(2)}, u32[]{:S(2)}) collective-permute-start(f32[192,256]{1,0:T(8,128)S(1)} %get-tuple-element.96), channel_id=1, source_target_pairs={{1,2},{2,1},{3,4},{4,3},{5,6},{6,5},{7,8},{8,7},{9,10},{10,9},{11,... | collective-permute-start | bytes 589832 | tf_op jit(solution)/shard_map/ppermute | solution.py:44
  49.2 8.1 %all_gather.71.rc = f32[384,256]{1,0:T(8,128)S(1)} all-gather(f32[192,256]{1,0:T(8,128)S(1)} %get-tuple-element.95), channel_id=1, replica_groups={{0,1},{2,3},{4,5},{6,7},{8,9},{10,11},{12,13},{14,15},{17,18},{19,20},{..., dimensions={0}, use_global_device_ids=true | all-gather | bytes 589824 | tf_op jit(solution)/shard_map/all_gather | solution.py:60
  58.3 4.5 %collective-permute-start.5 = (f32[192,256]{1,0:T(8,128)S(1)}, f32[192,256]{1,0:T(8,128)S(1)}, u32[]{:S(2)}, u32[]{:S(2)}) collective-permute-start(f32[192,256]{1,0:T(8,128)S(1)} %get-tuple-element.101), channel_id=1, source_target_pairs={{16,32},{17,33},{18,34},{19,35},{20,36},{21,37},{22,38},{23,39},{2... | collective-permute-start | bytes 589832 | tf_op jit(solution)/shard_map/ppermute | solution.py:44
  62.8 2.1 %all_gather.72.ra = f32[384,256]{1,0:T(8,128)S(1)} all-gather(f32[192,256]{1,0:T(8,128)S(1)} %get-tuple-element.100), channel_id=1, replica_groups={{0,16},{1,17},{2,18},{3,19},{4,20},{5,21},{6,22},{7,23},{8,24},{9,25},{..., dimensions={0}, use_global_device_ids=true | all-gather | bytes 589824 | tf_op jit(solution)/shard_map/all_gather | solution.py:60
  64.9 1.6 collective-permute-done.5.rb
  66.5 1.9 %collective-permute-start.6 = (f32[192,256]{1,0:T(8,128)S(1)}, f32[192,256]{1,0:T(8,128)S(1)}, u32[]{:S(2)}, u32[]{:S(2)}) collective-permute-start(f32[192,256]{1,0:T(8,128)S(1)} %get-tuple-element.105), channel_id=1, source_target_pairs={{1,2},{2,1},{3,4},{4,3},{5,6},{6,5},{7,8},{8,7},{9,10},{10,9},{11,... | collective-permute-start | bytes 589832 | tf_op jit(solution)/shard_map/ppermute | solution.py:44
  68.4 7.7 %all_gather.73.rc = f32[384,256]{1,0:T(8,128)S(1)} all-gather(f32[192,256]{1,0:T(8,128)S(1)} %get-tuple-element.104), channel_id=1, replica_groups={{0,1},{2,3},{4,5},{6,7},{8,9},{10,11},{12,13},{14,15},{17,18},{19,20},{..., dimensions={0}, use_global_device_ids=true | all-gather | bytes 589824 | tf_op jit(solution)/shard_map/all_gather | solution.py:60
  76.9 1.9 %all_gather.74.from_a = f32[64,256]{1,0:T(8,128)S(1)} all-gather(f32[32,256]{1,0:T(8,128)S(1)} %get-tuple-element.108), channel_id=1, replica_groups={{0,16},{1,17},{2,18},{3,19},{4,20},{5,21},{6,22},{7,23},{8,24},{9,25},{..., dimensions={0}, use_global_device_ids=true | all-gather | bytes 98304 | tf_op jit(solution)/shard_map/all_gather | solution.py:60
  78.8 6.1 %all_gather.75.theirs = f32[128,256]{1,0:T(8,128)S(1)} all-gather(f32[64,256]{1,0:T(8,128)S(1)} %shard_map.108.mine), channel_id=1, replica_groups={{16,32},{17,33},{18,34},{19,35},{20,36},{21,37},{22,38},{23,39},{24,40}..., dimensions={0}, use_global_device_ids=true | all-gather | bytes 196608 | tf_op jit(solution)/shard_map/all_gather | solution.py:60
  85.1 1.9 %all_gather.76.sol_a = f32[64,256]{1,0:T(8,128)S(1)} all-gather(f32[32,256]{1,0:T(8,128)S(1)} %get-tuple-element.109.sol), channel_id=1, replica_groups={{0,16},{1,17},{2,18},{3,19},{4,20},{5,21},{6,22},{7,23},{8,24},{9,25},{..., dimensions={0}, use_global_device_ids=true | all-gather | bytes 98304 | tf_op jit(solution)/shard_map/all_gather | solution.py:60
  88.0 5.1 %collective-permute-start.7 = (f32[192,256]{1,0:T(8,128)S(1)}, f32[192,256]{1,0:T(8,128)S(1)}, u32[]{:S(2)}, u32[]{:S(2)}) collective-permute-start(f32[192,256]{1,0:T(8,128)S(1)} %get-tuple-element.113), channel_id=1, source_target_pairs={{16,32},{17,33},{18,34},{19,35},{20,36},{21,37},{22,38},{23,39},{2... | collective-permute-start | bytes 589832 | tf_op jit(solution)/shard_map/ppermute | solution.py:44
  93.1 2.1 %all_gather.77.ra = f32[384,256]{1,0:T(8,128)S(1)} all-gather(f32[192,256]{1,0:T(8,128)S(1)} %get-tuple-element.112), channel_id=1, replica_groups={{0,16},{1,17},{2,18},{3,19},{4,20},{5,21},{6,22},{7,23},{8,24},{9,25},{..., dimensions={0}, use_global_device_ids=true | all-gather | bytes 589824 | tf_op jit(solution)/shard_map/all_gather | solution.py:60
  96.3 1.9 %collective-permute-start.8 = (f32[192,256]{1,0:T(8,128)S(1)}, f32[192,256]{1,0:T(8,128)S(1)}, u32[]{:S(2)}, u32[]{:S(2)}) collective-permute-start(f32[192,256]{1,0:T(8,128)S(1)} %get-tuple-element.117), channel_id=1, source_target_pairs={{1,2},{2,1},{3,4},{4,3},{5,6},{6,5},{7,8},{8,7},{9,10},{10,9},{11,... | collective-permute-start | bytes 589832 | tf_op jit(solution)/shard_map/ppermute | solution.py:44
  98.2 8.2 %all_gather.78.rc = f32[384,256]{1,0:T(8,128)S(1)} all-gather(f32[192,256]{1,0:T(8,128)S(1)} %get-tuple-element.116), channel_id=1, replica_groups={{0,1},{2,3},{4,5},{6,7},{8,9},{10,11},{12,13},{14,15},{17,18},{19,20},{..., dimensions={0}, use_global_device_ids=true | all-gather | bytes 589824 | tf_op jit(solution)/shard_map/all_gather | solution.py:60
  107.5 5.5 %collective-permute-start.9 = (f32[192,256]{1,0:T(8,128)S(1)}, f32[192,256]{1,0:T(8,128)S(1)}, u32[]{:S(2)}, u32[]{:S(2)}) collective-permute-start(f32[192,256]{1,0:T(8,128)S(1)} %get-tuple-element.122), channel_id=1, source_target_pairs={{16,32},{17,33},{18,34},{19,35},{20,36},{21,37},{22,38},{23,39},{2... | collective-permute-start | bytes 589832 | tf_op jit(solution)/shard_map/ppermute | solution.py:44
  113.0 2.1 %all_gather.79.ra = f32[384,256]{1,0:T(8,128)S(1)} all-gather(f32[192,256]{1,0:T(8,128)S(1)} %get-tuple-element.121), channel_id=1, replica_groups={{0,16},{1,17},{2,18},{3,19},{4,20},{5,21},{6,22},{7,23},{8,24},{9,25},{..., dimensions={0}, use_global_device_ids=true | all-gather | bytes 589824 | tf_op jit(solution)/shard_map/all_gather | solution.py:60
  115.0 1.3 collective-permute-done.9.rb
  116.3 1.9 %collective-permute-start.10 = (f32[192,256]{1,0:T(8,128)S(1)}, f32[192,256]{1,0:T(8,128)S(1)}, u32[]{:S(2)}, u32[]{:S(2)}) collective-permute-start(f32[192,256]{1,0:T(8,128)S(1)} %get-tuple-element.126), channel_id=1, source_target_pairs={{1,2},{2,1},{3,4},{4,3},{5,6},{6,5},{7,8},{8,7},{9,10},{10,9},{11,... | collective-permute-start | bytes 589832 | tf_op jit(solution)/shard_map/ppermute | solution.py:44
  118.3 8.1 %all_gather.80.rc = f32[384,256]{1,0:T(8,128)S(1)} all-gather(f32[192,256]{1,0:T(8,128)S(1)} %get-tuple-element.125), channel_id=1, replica_groups={{0,1},{2,3},{4,5},{6,7},{8,9},{10,11},{12,13},{14,15},{17,18},{19,20},{..., dimensions={0}, use_global_device_ids=true | all-gather | bytes 589824 | tf_op jit(solution)/shard_map/all_gather | solution.py:60
  127.1 1.9 %all_gather.81.from_a = f32[64,256]{1,0:T(8,128)S(1)} all-gather(f32[32,256]{1,0:T(8,128)S(1)} %get-tuple-element.129), channel_id=1, replica_groups={{0,16},{1,17},{2,18},{3,19},{4,20},{5,21},{6,22},{7,23},{8,24},{9,25},{..., dimensions={0}, use_global_device_ids=true | all-gather | bytes 98304 | tf_op jit(solution)/shard_map/all_gather | solution.py:60
  129.0 5.7 %all_gather.82.theirs = f32[128,256]{1,0:T(8,128)S(1)} all-gather(f32[64,256]{1,0:T(8,128)S(1)} %shard_map.115.mine), channel_id=1, replica_groups={{16,32},{17,33},{18,34},{19,35},{20,36},{21,37},{22,38},{23,39},{24,40}..., dimensions={0}, use_global_device_ids=true | all-gather | bytes 196608 | tf_op jit(solution)/shard_map/all_gather | solution.py:60
  134.9 1.9 %all_gather.83.sol_a = f32[64,256]{1,0:T(8,128)S(1)} all-gather(f32[32,256]{1,0:T(8,128)S(1)} %get-tuple-element.130.sol), channel_id=1, replica_groups={{0,16},{1,17},{2,18},{3,19},{4,20},{5,21},{6,22},{7,23},{8,24},{9,25},{..., dimensions={0}, use_global_device_ids=true | all-gather | bytes 98304 | tf_op jit(solution)/shard_map/all_gather | solution.py:60
  137.8 4.9 %collective-permute-start.11 = (f32[192,256]{1,0:T(8,128)S(1)}, f32[192,256]{1,0:T(8,128)S(1)}, u32[]{:S(2)}, u32[]{:S(2)}) collective-permute-start(f32[192,256]{1,0:T(8,128)S(1)} %get-tuple-element.134), channel_id=1, source_target_pairs={{16,32},{17,33},{18,34},{19,35},{20,36},{21,37},{22,38},{23,39},{2... | collective-permute-start | bytes 589832 | tf_op jit(solution)/shard_map/ppermute | solution.py:44
  142.7 2.1 %all_gather.84.ra = f32[384,256]{1,0:T(8,128)S(1)} all-gather(f32[192,256]{1,0:T(8,128)S(1)} %get-tuple-element.133), channel_id=1, replica_groups={{0,16},{1,17},{2,18},{3,19},{4,20},{5,21},{6,22},{7,23},{8,24},{9,25},{..., dimensions={0}, use_global_device_ids=true | all-gather | bytes 589824 | tf_op jit(solution)/shard_map/all_gather | solution.py:60
  144.7 1.3 collective-permute-done.11.rb
  146.0 1.9 %collective-permute-start.12 = (f32[192,256]{1,0:T(8,128)S(1)}, f32[192,256]{1,0:T(8,128)S(1)}, u32[]{:S(2)}, u32[]{:S(2)}) collective-permute-start(f32[192,256]{1,0:T(8,128)S(1)} %get-tuple-element.138), channel_id=1, source_target_pairs={{1,2},{2,1},{3,4},{4,3},{5,6},{6,5},{7,8},{8,7},{9,10},{10,9},{11,... | collective-permute-start | bytes 589832 | tf_op jit(solution)/shard_map/ppermute | solution.py:44
  148.0 8.1 %all_gather.85.rc = f32[384,256]{1,0:T(8,128)S(1)} all-gather(f32[192,256]{1,0:T(8,128)S(1)} %get-tuple-element.137), channel_id=1, replica_groups={{0,1},{2,3},{4,5},{6,7},{8,9},{10,11},{12,13},{14,15},{17,18},{19,20},{..., dimensions={0}, use_global_device_ids=true | all-gather | bytes 589824 | tf_op jit(solution)/shard_map/all_gather | solution.py:60
  156.0 1.1 shard_map.119
  157.1 5.6 %collective-permute-start.13 = (f32[192,256]{1,0:T(8,128)S(1)}, f32[192,256]{1,0:T(8,128)S(1)}, u32[]{:S(2)}, u32[]{:S(2)}) collective-permute-start(f32[192,256]{1,0:T(8,128)S(1)} %get-tuple-element.145), channel_id=1, source_target_pairs={{16,32},{17,33},{18,34},{19,35},{20,36},{21,37},{22,38},{23,39},{2... | collective-permute-start | bytes 589832 | tf_op jit(solution)/shard_map/ppermute | solution.py:44
  162.7 2.2 %shard_map.120 = (f32[768,256]{1,0:T(8,128)}, bf16[768,768]{1,0:T(8,128)(2,1)S(1)}) custom-call(s32[1,768]{1,0:T(1,128)S(1)} %bitcast.29, f32[768,256]{1,0:T(8,128)S(1)} %get-tuple-element.97.old.one, f32[768,256]{1,0:T(8,128)S(1)} %get-tuple-element.118.old.two, f32[768,256]{1,0:T(8,128)S(1)} %get-tuple-element.139.three), custom_call_target="tpu_custom_call" | custom-call | flops 905969664 | bytes 4328448 | tf_op jit(solution)/shard_map/pallas_call | solution.py:294
  164.9 2.1 %all_gather.86.ra = f32[384,256]{1,0:T(8,128)S(1)} all-gather(f32[192,256]{1,0:T(8,128)S(1)} %get-tuple-element.144), channel_id=1, replica_groups={{0,16},{1,17},{2,18},{3,19},{4,20},{5,21},{6,22},{7,23},{8,24},{9,25},{..., dimensions={0}, use_global_device_ids=true | all-gather | bytes 589824 | tf_op jit(solution)/shard_map/all_gather | solution.py:60
  167.0 1.9 %collective-permute-start.14 = (f32[192,256]{1,0:T(8,128)S(1)}, f32[192,256]{1,0:T(8,128)S(1)}, u32[]{:S(2)}, u32[]{:S(2)}) collective-permute-start(f32[192,256]{1,0:T(8,128)S(1)} %get-tuple-element.149), channel_id=1, source_target_pairs={{1,2},{2,1},{3,4},{4,3},{5,6},{6,5},{7,8},{8,7},{9,10},{10,9},{11,... | collective-permute-start | bytes 589832 | tf_op jit(solution)/shard_map/ppermute | solution.py:44
  168.9 9.5 %all_gather.87.rc = f32[384,256]{1,0:T(8,128)S(1)} all-gather(f32[192,256]{1,0:T(8,128)S(1)} %get-tuple-element.148), channel_id=1, replica_groups={{0,1},{2,3},{4,5},{6,7},{8,9},{10,11},{12,13},{14,15},{17,18},{19,20},{..., dimensions={0}, use_global_device_ids=true | all-gather | bytes 589824 | tf_op jit(solution)/shard_map/all_gather | solution.py:60
  178.4 2.3 %shard_map.122 = f32[768,256]{1,0:T(8,128)} custom-call(s32[8,128]{1,0:T(8,128)S(1)} %copy-done, bf16[768,768]{1,0:T(8,128)(2,1)S(1)} %get-tuple-element.141.rest_0_.back, f32[768,256]{1,0:T(8,128)S(1)} %get-tuple-element.142.old, f32[768,256]{1,0:T(8,128)S(1)} %get-tuple-element.143.product, f32[384,256]{1,0:T(8,128)S(1)} %all_gather.86.ra, ...), custom_call_target="tpu_custom_call" | custom-call | flops 905969664 | bytes 4722688 | tf_op jit(solution)/shard_map/pallas_call | solution.py:294
  (53 shorter events, 10.5 us)
Async XLA Ops:
  0.6 10.6 %copy-start.9 = (bf16[1,1,768,32]{2,3,1,0:T(8,128)(2,1)S(1)}, bf16[1,1,768,32]{2,3,1,0:T(8,128)(2,1)}, u32[]{:S(2)}) copy-start(bf16[1,1,768,32]{2,3,1,0:T(8,128)(2,1)} %param.11) | copy-start | bytes 147460
  0.6 10.8 %copy-start.5 = (bf16[1,1,768,768]{3,2,1,0:T(8,128)(2,1)S(1)}, bf16[1,1,768,768]{3,2,1,0:T(8,128)(2,1)}, u32[]{:S(2)}) copy-start(bf16[1,1,768,768]{3,2,1,0:T(8,128)(2,1)} %param.10) | copy-start | bytes 3538948
  0.7 10.8 %copy-start.8 = (s32[1,1,768]{2,1,0:T(1,128)S(1)}, s32[1,1,768]{2,1,0:T(1,128)}, u32[]{:S(2)}) copy-start(s32[1,1,768]{2,1,0:T(1,128)} %param.15) | copy-start | bytes 9220
  3.7 10.5 %collective-permute-start = (f32[192,256]{1,0:T(8,128)}, f32[192,256]{1,0:T(8,128)S(1)}, u32[]{:S(2)}, u32[]{:S(2)}) collective-permute-start(f32[192,256]{1,0:T(8,128)} %get-tuple-element.80), channel_id=1, source_target_pairs={{16,32},{17,33},{18,34},{19,35},{20,36},{21,37},{22,38},{23,39},{2... | collective-permute-start | bytes 589832 | tf_op jit(solution)/shard_map/ppermute | solution.py:44
  11.5 2.7 %copy-start.2 = (f32[64,256]{1,0:T(8,128)S(1)}, f32[64,256]{1,0:T(8,128)}, u32[]{:S(2)}) copy-start(f32[64,256]{1,0:T(8,128)} %get-tuple-element.81.c) | copy-start | bytes 196612
  11.5 2.7 %copy-start.3 = (f32[64,256]{1,0:T(8,128)S(1)}, f32[64,256]{1,0:T(8,128)}, u32[]{:S(2)}) copy-start(f32[64,256]{1,0:T(8,128)} %get-tuple-element.82.d) | copy-start | bytes 196612
  14.2 6.9 %copy-start.7 = (f32[1,1,768,256]{3,2,1,0:T(8,128)S(1)}, f32[1,1,768,256]{3,2,1,0:T(8,128)}, u32[]{:S(2)}) copy-start(f32[1,1,768,256]{3,2,1,0:T(8,128)} %param.8) | copy-start | bytes 2359300
  14.3 10.6 %collective-permute-start.1 = (f32[192,256]{1,0:T(8,128)S(1)}, f32[192,256]{1,0:T(8,128)S(1)}, u32[]{:S(2)}, u32[]{:S(2)}) collective-permute-start(f32[192,256]{1,0:T(8,128)S(1)} %get-tuple-element.83), channel_id=1, source_target_pairs={{0,1},{1,0},{2,3},{3,2},{4,5},{5,4},{6,7},{7,6},{8,9},{9,8},{10,11... | collective-permute-start | bytes 589832 | tf_op jit(solution)/shard_map/ppermute | solution.py:44
  19.0 3.5 %copy-start.6 = (bf16[1,1,768,768]{3,2,1,0:T(8,128)(2,1)S(1)}, bf16[1,1,768,768]{3,2,1,0:T(8,128)(2,1)}, u32[]{:S(2)}) copy-start(bf16[1,1,768,768]{3,2,1,0:T(8,128)(2,1)} %param.9) | copy-start | bytes 3538948
  19.0 6.8 %collective-permute-start.2 = (f32[192,256]{1,0:T(8,128)S(1)}, f32[192,256]{1,0:T(8,128)S(1)}, u32[]{:S(2)}, u32[]{:S(2)}) collective-permute-start(f32[192,256]{1,0:T(8,128)S(1)} %get-tuple-element.84), channel_id=1, source_target_pairs={{1,2},{2,1},{3,4},{4,3},{5,6},{6,5},{7,8},{8,7},{9,10},{10,9},{11,... | collective-permute-start | bytes 589832 | tf_op jit(solution)/shard_map/ppermute | solution.py:44
  22.4 3.4 %copy-start = (s32[8,128]{1,0:T(8,128)S(1)}, s32[8,128]{1,0:T(8,128)}, u32[]{:S(2)}) copy-start(s32[8,128]{1,0:T(8,128)} %get-tuple-element.76.table) | copy-start | bytes 12292
  22.4 3.4 %copy-start.4 = (s32[1,1,32]{2,1,0:T(1,128)S(1)}, s32[1,1,32]{2,1,0:T(1,128)}, u32[]{:S(2)}) copy-start(s32[1,1,32]{2,1,0:T(1,128)} %param.13) | copy-start | bytes 388
  25.8 4.2 %copy-start.1 = (f32[1,1,32,32]{3,2,1,0:T(8,128)S(1)}, f32[1,1,32,32]{3,2,1,0:T(8,128)}, u32[]{:S(2)}) copy-start(f32[1,1,32,32]{3,2,1,0:T(8,128)} %param.12) | copy-start | bytes 12292
  39.1 8.2 %collective-permute-start.3 = (f32[192,256]{1,0:T(8,128)S(1)}, f32[192,256]{1,0:T(8,128)S(1)}, u32[]{:S(2)}, u32[]{:S(2)}) collective-permute-start(f32[192,256]{1,0:T(8,128)S(1)} %get-tuple-element.92), channel_id=1, source_target_pairs={{16,32},{17,33},{18,34},{19,35},{20,36},{21,37},{22,38},{23,39},{2... | collective-permute-start | bytes 589832 | tf_op jit(solution)/shard_map/ppermute | solution.py:44
  47.3 10.0 %collective-permute-start.4 = (f32[192,256]{1,0:T(8,128)S(1)}, f32[192,256]{1,0:T(8,128)S(1)}, u32[]{:S(2)}, u32[]{:S(2)}) collective-permute-start(f32[192,256]{1,0:T(8,128)S(1)} %get-tuple-element.96), channel_id=1, source_target_pairs={{1,2},{2,1},{3,4},{4,3},{5,6},{6,5},{7,8},{8,7},{9,10},{10,9},{11,... | collective-permute-start | bytes 589832 | tf_op jit(solution)/shard_map/ppermute | solution.py:44
  58.3 8.2 %collective-permute-start.5 = (f32[192,256]{1,0:T(8,128)S(1)}, f32[192,256]{1,0:T(8,128)S(1)}, u32[]{:S(2)}, u32[]{:S(2)}) collective-permute-start(f32[192,256]{1,0:T(8,128)S(1)} %get-tuple-element.101), channel_id=1, source_target_pairs={{16,32},{17,33},{18,34},{19,35},{20,36},{21,37},{22,38},{23,39},{2... | collective-permute-start | bytes 589832 | tf_op jit(solution)/shard_map/ppermute | solution.py:44
  66.5 9.6 %collective-permute-start.6 = (f32[192,256]{1,0:T(8,128)S(1)}, f32[192,256]{1,0:T(8,128)S(1)}, u32[]{:S(2)}, u32[]{:S(2)}) collective-permute-start(f32[192,256]{1,0:T(8,128)S(1)} %get-tuple-element.105), channel_id=1, source_target_pairs={{1,2},{2,1},{3,4},{4,3},{5,6},{6,5},{7,8},{8,7},{9,10},{10,9},{11,... | collective-permute-start | bytes 589832 | tf_op jit(solution)/shard_map/ppermute | solution.py:44
  88.0 8.2 %collective-permute-start.7 = (f32[192,256]{1,0:T(8,128)S(1)}, f32[192,256]{1,0:T(8,128)S(1)}, u32[]{:S(2)}, u32[]{:S(2)}) collective-permute-start(f32[192,256]{1,0:T(8,128)S(1)} %get-tuple-element.113), channel_id=1, source_target_pairs={{16,32},{17,33},{18,34},{19,35},{20,36},{21,37},{22,38},{23,39},{2... | collective-permute-start | bytes 589832 | tf_op jit(solution)/shard_map/ppermute | solution.py:44
  96.3 10.2 %collective-permute-start.8 = (f32[192,256]{1,0:T(8,128)S(1)}, f32[192,256]{1,0:T(8,128)S(1)}, u32[]{:S(2)}, u32[]{:S(2)}) collective-permute-start(f32[192,256]{1,0:T(8,128)S(1)} %get-tuple-element.117), channel_id=1, source_target_pairs={{1,2},{2,1},{3,4},{4,3},{5,6},{6,5},{7,8},{8,7},{9,10},{10,9},{11,... | collective-permute-start | bytes 589832 | tf_op jit(solution)/shard_map/ppermute | solution.py:44
  107.5 8.8 %collective-permute-start.9 = (f32[192,256]{1,0:T(8,128)S(1)}, f32[192,256]{1,0:T(8,128)S(1)}, u32[]{:S(2)}, u32[]{:S(2)}) collective-permute-start(f32[192,256]{1,0:T(8,128)S(1)} %get-tuple-element.122), channel_id=1, source_target_pairs={{16,32},{17,33},{18,34},{19,35},{20,36},{21,37},{22,38},{23,39},{2... | collective-permute-start | bytes 589832 | tf_op jit(solution)/shard_map/ppermute | solution.py:44
  116.3 10.0 %collective-permute-start.10 = (f32[192,256]{1,0:T(8,128)S(1)}, f32[192,256]{1,0:T(8,128)S(1)}, u32[]{:S(2)}, u32[]{:S(2)}) collective-permute-start(f32[192,256]{1,0:T(8,128)S(1)} %get-tuple-element.126), channel_id=1, source_target_pairs={{1,2},{2,1},{3,4},{4,3},{5,6},{6,5},{7,8},{8,7},{9,10},{10,9},{11,... | collective-permute-start | bytes 589832 | tf_op jit(solution)/shard_map/ppermute | solution.py:44
  137.8 8.2 %collective-permute-start.11 = (f32[192,256]{1,0:T(8,128)S(1)}, f32[192,256]{1,0:T(8,128)S(1)}, u32[]{:S(2)}, u32[]{:S(2)}) collective-permute-start(f32[192,256]{1,0:T(8,128)S(1)} %get-tuple-element.134), channel_id=1, source_target_pairs={{16,32},{17,33},{18,34},{19,35},{20,36},{21,37},{22,38},{23,39},{2... | collective-permute-start | bytes 589832 | tf_op jit(solution)/shard_map/ppermute | solution.py:44
  146.0 10.0 %collective-permute-start.12 = (f32[192,256]{1,0:T(8,128)S(1)}, f32[192,256]{1,0:T(8,128)S(1)}, u32[]{:S(2)}, u32[]{:S(2)}) collective-permute-start(f32[192,256]{1,0:T(8,128)S(1)} %get-tuple-element.138), channel_id=1, source_target_pairs={{1,2},{2,1},{3,4},{4,3},{5,6},{6,5},{7,8},{8,7},{9,10},{10,9},{11,... | collective-permute-start | bytes 589832 | tf_op jit(solution)/shard_map/ppermute | solution.py:44
  157.1 9.9 %collective-permute-start.13 = (f32[192,256]{1,0:T(8,128)S(1)}, f32[192,256]{1,0:T(8,128)S(1)}, u32[]{:S(2)}, u32[]{:S(2)}) collective-permute-start(f32[192,256]{1,0:T(8,128)S(1)} %get-tuple-element.145), channel_id=1, source_target_pairs={{16,32},{17,33},{18,34},{19,35},{20,36},{21,37},{22,38},{23,39},{2... | collective-permute-start | bytes 589832 | tf_op jit(solution)/shard_map/ppermute | solution.py:44
  167.0 11.4 %collective-permute-start.14 = (f32[192,256]{1,0:T(8,128)S(1)}, f32[192,256]{1,0:T(8,128)S(1)}, u32[]{:S(2)}, u32[]{:S(2)}) collective-permute-start(f32[192,256]{1,0:T(8,128)S(1)} %get-tuple-element.149), channel_id=1, source_target_pairs={{1,2},{2,1},{3,4},{4,3},{5,6},{6,5},{7,8},{8,7},{9,10},{10,9},{11,... | collective-permute-start | bytes 589832 | tf_op jit(solution)/shard_map/ppermute | solution.py:44
